TPU v7x, 32 devices: a whole 2x2x4 slice. The times are simulated.
32 devices in a mesh: seq: 8 (over z, y), head: 4 (over x, core).
Axes of the slice: x: 2, y: 2, z: 4, core: 2. Of those that a mesh axis runs over, the one named last changes fastest.
Arguments:
- queries: bfloat16 [4, 64, 128], P(None, 'head'), may hold values from -12 to 12
- keys: bfloat16 [4, 8, 1024, 128], P(None, 'head', 'seq'), may hold values from -6 to 6
- values: bfloat16 [4, 8, 1024, 128], P(None, 'head', 'seq'), may hold values from -6 to 6
- codes: int32 [4, 8, 32, 1024], P(None, 'head', None, 'seq'), may hold values from 0 to 255
- centroids: float32 [8, 4, 32, 256], P('head'), may hold values from -6 to 6
- picks: int32 [4, 8, 8], P(None, 'head'), may hold values from 0 to 63, as said below
- block_len: int32 [4, 64], P(None, 'seq'), may hold values from 1 to 16
- out_weight: bfloat16 [8192, 8192], P('head', 'seq'), may hold values from -0.0625 to 0.0625
Outputs:
- estimates: float32 [4, 8, 64], P(None, 'head', 'seq')
- attended: bfloat16 [8, 4, 1024], P('seq', 'head')
- layer_out: bfloat16 [4, 8192], P('head', 'seq')
Inputs may be any that keep to these rules, and one draw needn't show every extreme that they name: Each row picks[b, h, :] holds 8 different block numbers in no particular order; among the 8 blocks j * 8 to (j + 1) * 8 - 1 of any j at most 4 are picked, and in every row some j has exactly 4.
All inputs are finite; a program needn't handle non-finite values.
Results may differ from a plain program's by a relative error of at most 0.0049.
Values may be sent and summed in bfloat16 or wider, within the bound.
No kernel may reach another device: no remote copies, remote signals or barrier semaphores. Data moves between devices by JAX's collectives and lax.ppermute only.
A program may use at most 64 MiB of HBM per device.

v0:
```python
import jax
import jax.numpy as jnp
from jax import lax
from jax.sharding import PartitionSpec as P

NEG = -1e30


def slot_matrix(sel_rows, shard, nblk_dev, capacity):
    local = sel_rows - shard * nblk_dev
    inside = (local >= 0) & (local < nblk_dev)
    hits = (local[:, :, None] == lax.iota(jnp.int32, nblk_dev)[None, None, :]) & inside[:, :, None]
    taken = jnp.sum(hits.astype(jnp.int32), axis=1)
    position = jnp.cumsum(taken, axis=1) - 1
    place = (position[:, None, :] == lax.iota(jnp.int32, capacity)[None, :, None]) & (
        taken[:, None, :] > 0
    )
    return place.astype(jnp.bfloat16)


def attend(query, keys_s, values_s, lens_s):
    pairs, rows, width = keys_s.shape
    head_dim = query.shape[-1]
    block = width // head_dim
    key_rows = keys_s.reshape(pairs, rows * block, head_dim)
    value_rows = values_s.reshape(pairs, rows * block, head_dim)
    score = jnp.einsum(
        "pgd,ptd->pgt", query, key_rows, preferred_element_type=jnp.float32
    ) * head_dim ** (-0.5)
    live = (
        lax.iota(jnp.int32, block).astype(jnp.float32)[None, None, :]
        < lens_s.astype(jnp.float32)[:, :, None]
    )
    live = live.reshape(pairs, 1, rows * block)
    top = jnp.max(jnp.where(live, score, NEG), axis=2)
    weight = jnp.where(live, jnp.exp(score - top[:, :, None]), 0.0)
    total = jnp.sum(weight, axis=2)
    acc = jnp.einsum(
        "pgt,ptd->pgd", weight, value_rows.astype(jnp.float32), precision=lax.Precision.HIGHEST
    )
    return (top, total, acc)


def fold_rows(top, total, acc):
    best = jnp.max(top, axis=0)
    scale = jnp.exp(top - best[None])
    return (best, jnp.sum(total * scale, axis=0), jnp.sum(acc * scale[..., None], axis=0))


def shards(queries, keys, values, codes, centroids, picks, block_len, out_weight):
    batch, kv_local, seq_local, head_dim = keys.shape
    group = queries.shape[1] // kv_local
    nblk_dev = block_len.shape[1]
    block = seq_local // nblk_dev
    capacity = nblk_dev // 2
    pairs = batch * kv_local
    sub = centroids.shape[1]
    nsub = centroids.shape[2]
    cent = centroids.shape[3]
    shard = lax.axis_index("seq")
    query_float = queries.astype(jnp.float32).reshape(batch, kv_local, group, nsub, sub)
    table = jnp.einsum(
        "bhgms,hsmc->bhgmc", query_float, centroids, precision=lax.Precision.HIGHEST
    ) * head_dim ** (-0.5)
    table = table.astype(jnp.bfloat16).reshape(pairs, group, nsub * cent)
    lens_pair = jnp.repeat(block_len, kv_local, axis=0)
    step_rows = 4
    steps_count = pairs // step_rows

    def score_group(carry, items):
        tab, code, lens = items
        onehot = (code[:, :, None, :] == lax.iota(jnp.int32, cent)[None, None, :, None]).astype(
            jnp.bfloat16
        )
        onehot = onehot.reshape(step_rows, nsub * cent, seq_local)
        approx = jnp.einsum("pgk,pkt->pgt", tab, onehot, preferred_element_type=jnp.float32)
        approx = approx.reshape(step_rows, group, nblk_dev, block)
        live = (lax.iota(jnp.int32, block)[None, None, :] < lens[:, :, None])[:, None]
        top = jnp.max(jnp.where(live, approx, NEG), axis=(1, 3))
        mass = jnp.sum(jnp.where(live, jnp.exp(approx - top[:, None, :, None]), 0.0), axis=(1, 3))
        return (carry, top + jnp.log(mass))

    grouped = (
        table.reshape(steps_count, step_rows, group, nsub * cent),
        codes.reshape(steps_count, step_rows, nsub, seq_local),
        lens_pair.reshape(steps_count, step_rows, nblk_dev),
    )
    unused, estimated = lax.scan(score_group, 0, grouped)
    estimates = estimated.reshape(batch, kv_local, nblk_dev)
    sel_rows = picks.reshape(pairs, picks.shape[-1])
    place = slot_matrix(sel_rows, shard, nblk_dev, capacity)
    key_blocks = keys.reshape(pairs, nblk_dev, block * head_dim)
    value_blocks = values.reshape(pairs, nblk_dev, block * head_dim)
    lens_float = lens_pair.astype(jnp.float32)
    query_all = queries.reshape(pairs, group, head_dim)
    own_query = lax.dynamic_slice_in_dim(query_all, shard, 1, 0)
    send_keys = jnp.einsum(
        "pcn,pnd->cpd", place, key_blocks, preferred_element_type=jnp.float32
    ).astype(jnp.bfloat16)
    send_values = jnp.einsum(
        "pcn,pnd->cpd", place, value_blocks, preferred_element_type=jnp.float32
    ).astype(jnp.bfloat16)
    send_lens = jnp.einsum("pcn,pn->cp", place.astype(jnp.float32), lens_float).astype(jnp.bfloat16)
    got_keys = lax.all_to_all(send_keys, "seq", split_axis=1, concat_axis=1, tiled=True)
    got_values = lax.all_to_all(send_values, "seq", split_axis=1, concat_axis=1, tiled=True)
    got_lens = lax.all_to_all(send_lens, "seq", split_axis=1, concat_axis=1, tiled=True)
    count = got_keys.shape[0]
    query_rep = jnp.broadcast_to(own_query, (count, group, head_dim))
    pieces = attend(query_rep, got_keys, got_values, got_lens)
    top, total, acc = fold_rows(pieces[0], pieces[1], pieces[2])
    head_out = (acc / total[..., None]).astype(jnp.bfloat16)
    attended = head_out.reshape(1, 1, group * head_dim)
    flat = head_out.reshape(1, group * head_dim)
    weight_parts = out_weight.reshape(kv_local, group * head_dim, out_weight.shape[1])
    piece = lax.all_gather(flat, "seq", axis=0, tiled=True)
    products = jnp.einsum("ik,hkd->ihd", piece, weight_parts, preferred_element_type=jnp.float32)
    parity = lax.iota(jnp.int32, piece.shape[0]) % kv_local
    select = (parity[:, None] == lax.iota(jnp.int32, kv_local)[None, :]).astype(jnp.float32)
    gathered = jnp.sum(products * select[:, :, None], axis=1)
    per_request = jnp.sum(gathered.reshape(batch, kv_local, out_weight.shape[1]), axis=1)
    layer_out = lax.psum_scatter(per_request, "head", scatter_dimension=0, tiled=True).astype(
        jnp.bfloat16
    )
    return (estimates, attended, layer_out)


def solution(mesh):
    placed = (
        P(None, "head", None),
        P(None, "head", "seq", None),
        P(None, "head", "seq", None),
        P(None, "head", None, "seq"),
        P("head", None, None, None),
        P(None, "head", None),
        P(None, "seq"),
        P("head", "seq"),
    )
    return jax.shard_map(
        shards,
        mesh=mesh,
        in_specs=placed,
        out_specs=(P(None, "head", "seq"), P("seq", "head", None), P("head", "seq")),
        check_vma=False,
    )
```

profile of v0, /device:TPU:0, one launch (start us, length us, event | category | flops | bytes accessed | tf_op | source)
XLA Modules:
  0.0 98.4 jit_solution(16973540910457343254)
XLA Ops:
  0.7 0.7 broadcast_subtract_fusion
  1.4 0.1 convert_reduce_fusion
  1.5 0.2 reduce_window_sum.11
  1.7 0.7 convert_element_type.85
  2.4 0.1 fusion.22
  2.5 0.1 copy.65
  2.6 0.7 copy.58
  3.3 7.3 %all-to-all-start = ((bf16[4,8,1]{0,2,1:T(2,128)(2,1)}), bf16[4,8,1]{0,2,1:T(2,128)(2,1)S(1)}, u32[]{:S(2)}, u32[]{:S(2)}) async-start(bf16[4,8,1]{0,2,1:T(2,128)(2,1)} %copy.58), calls=%async_computation | async-start | bytes 8192 | tf_op jit(solution)/shard_map/all_to_all | solution.py:106
  10.6 0.8 copy.54
  11.5 0.1 reshape.217
  11.6 2.0 %fusion.6 = bf16[4,2,8,32,256]{4,2,0,3,1:T(8,128)(2,1)S(1)} fusion(f32[2,4,32,256,1]{3,2,1,0,4:T(8,128)} %bitcast.90, bf16[4,2,8,32,4]{2,1,4,3,0:T(2,128)(2,1)S(1)} %reshape.217), kind=kOutput, calls=%fused_computation.17 | convolution fusion | flops 26214400 | bytes 1327104 | tf_op jit(solution)/shard_map/bhgms,hsmc->bhgmc/dot_general | solution.py:62
  13.6 0.6 copy.57
  14.2 0.5 reshape_reshape.7
  14.8 0.0 copy-start.6
  14.8 11.3 %while.10 = (s32[]{:T(128)}, f32[2,4,8]{2,1,0:T(4,128)S(1)}, s32[2,4,8]{2,1,0:T(4,128)S(1)}, bf16[2,4,8,8192]{3,2,1,0:T(8,128)(2,1)S(1)}, s32[2,4,32,128]{3,2,1,...) while((s32[]{:T(128)}, f32[2,4,8]{2,1,0:T(4,128)S(1)}, s32[2,4,8]{2,1,0:T(4,128)S(1)}, ...), condition=%wide.region_5.6_spmd, body=%wide.region_0.5_spmd.sunk | while | flops 71324128 | bytes 9316725 | solution.py:88
  14.9 0.1 lt.104
  14.9 0.1 lt.105
  15.0 0.1 lt.107
  15.2 2.7 %bitcast_compare_fusion.2 = pred[4,8192,128]{2,1,0:T(32,128)(4,1)S(1)} fusion(s32[8192]{0:T(1024)S(1)} %bitcast.88, s32[4,32,128]{2,1,0:T(8,128)S(1)} %dynamic-slice_bitcast_fusion.6), kind=kLoop, calls=%fused_computation.clone.1 | loop fusion | flops 4194304 | bytes 4292608 | tf_op jit(solution)/shard_map/while/body/eval_jaxpr/eq | solution.py:72
  17.8 2.1 %select_reduce_fusion.6 = (f32[4,128]{1,0:T(4,128)S(1)}, f32[4,8,128]{2,1,0:T(8,128)S(1)}) fusion(pred[4,128]{1,0:T(4,128)(4,1)S(1)} %broadcast_compare_fusion.4, pred[4,8192,128]{2,1,0:T(32,128)(4,1)S(1)} %bitcast_compare_fusion.2, bf16[2,4,8,8192]{3,2,1,0:T(8,128)(2,1)S(1)} %get-tuple-element.109, s32[]{:T(128)S(6)} %copy.84), kind=kOutput, calls=%fused_computation.7.clone.1 | convolution fusion | flops 67116544 | bytes 4737540 | tf_op jit(solution)/shard_map/while/body/eval_jaxpr/pgk,pkt->pgt/dot_general | solution.py:76
  19.9 0.1 reduce_max.43
  20.0 0.1 reduce_max.44
  20.1 0.1 sub.85
  20.2 0.1 sub.86
  20.3 0.1 reduce_sum.86
  20.4 0.1 reduce_sum.87
  20.5 0.1 lt.104
  20.6 0.1 lt.105
  20.7 0.1 lt.107
  20.8 2.7 %bitcast_compare_fusion.2 = pred[4,8192,128]{2,1,0:T(32,128)(4,1)S(1)} fusion(s32[8192]{0:T(1024)S(1)} %bitcast.88, s32[4,32,128]{2,1,0:T(8,128)S(1)} %dynamic-slice_bitcast_fusion.6), kind=kLoop, calls=%fused_computation.clone.1 | loop fusion | flops 4194304 | bytes 4292608 | tf_op jit(solution)/shard_map/while/body/eval_jaxpr/eq | solution.py:72
  23.5 2.1 %select_reduce_fusion.6 = (f32[4,128]{1,0:T(4,128)S(1)}, f32[4,8,128]{2,1,0:T(8,128)S(1)}) fusion(pred[4,128]{1,0:T(4,128)(4,1)S(1)} %broadcast_compare_fusion.4, pred[4,8192,128]{2,1,0:T(32,128)(4,1)S(1)} %bitcast_compare_fusion.2, bf16[2,4,8,8192]{3,2,1,0:T(8,128)(2,1)S(1)} %get-tuple-element.109, s32[]{:T(128)S(6)} %copy.84), kind=kOutput, calls=%fused_computation.7.clone.1 | convolution fusion | flops 67116544 | bytes 4737540 | tf_op jit(solution)/shard_map/while/body/eval_jaxpr/pgk,pkt->pgt/dot_general | solution.py:76
  25.6 0.1 reduce_max.43
  25.7 0.1 reduce_max.44
  25.7 0.1 sub.85
  25.8 0.1 sub.86
  26.0 0.1 reduce_sum.86
  26.0 0.1 reduce_sum.87
  26.1 0.0 copy-start.5
  26.2 0.1 reshape.223
  26.3 0.9 fusion.5
  27.1 0.1 lt.76
  27.2 0.1 reshape.221
  27.4 0.7 dynamic-slice_bitcast_fusion.2
  28.0 0.6 dynamic-slice
  28.7 6.0 %all-to-all-start.2 = ((bf16[4,8,2048]{2,0,1:T(4,128)(2,1)}), bf16[4,8,2048]{2,0,1:T(4,128)(2,1)S(1)}, u32[]{:S(2)}, u32[]{:S(2)}) async-start(bf16[4,8,2048]{2,0,1:T(4,128)(2,1)} %fusion.5), calls=%async_computation.2 | async-start | bytes 262144 | tf_op jit(solution)/shard_map/all_to_all | solution.py:105
  34.7 0.9 fusion.4
  35.5 0.1 copy.59
  35.6 6.4 %all-to-all-done.2 = bf16[4,8,2048]{2,0,1:T(4,128)(2,1)S(1)} async-done(((bf16[4,8,2048]{2,0,1:T(4,128)(2,1)}), bf16[4,8,2048]{2,0,1:T(4,128)(2,1)S(1)}, u32[]{:S(2)}, u32[]{:S(2)}) %all-to-all-start.2) | async-done | bytes 131104 | tf_op jit(solution)/shard_map/all_to_all | solution.py:105
  42.0 3.4 %all-to-all-start.1 = ((bf16[4,8,2048]{2,0,1:T(4,128)(2,1)}), bf16[4,8,2048]{2,0,1:T(4,128)(2,1)S(1)}, u32[]{:S(2)}, u32[]{:S(2)}) async-start(bf16[4,8,2048]{2,0,1:T(4,128)(2,1)} %fusion.4), calls=%async_computation.1 | async-start | bytes 262144 | tf_op jit(solution)/shard_map/all_to_all | solution.py:104
  45.4 0.1 lt.82
  45.5 0.1 lt.83
  45.6 0.1 copy.61
  45.7 0.1 reshape.224
  45.7 7.0 %all-to-all-done.1 = bf16[4,8,2048]{2,0,1:T(4,128)(2,1)S(1)} async-done(((bf16[4,8,2048]{2,0,1:T(4,128)(2,1)}), bf16[4,8,2048]{2,0,1:T(4,128)(2,1)S(1)}, u32[]{:S(2)}, u32[]{:S(2)}) %all-to-all-start.1) | async-done | bytes 131104 | tf_op jit(solution)/shard_map/all_to_all | solution.py:104
  52.7 0.1 copy.60
  52.8 0.1 reshape.222
  52.8 0.2 select_reduce_fusion.3
  53.1 0.2 fusion.15
  53.3 0.3 fusion.8
  53.6 0.1 divide_convert_fusion
  53.7 30.4 %all-gather = bf16[8,1,1024]{2,1,0:T(2,128)(2,1)S(1)} all-gather(bf16[1,1,1024]{2,1,0:T(2,128)(2,1)S(1)} %convert_element_type.94), channel_id=1, replica_groups=mesh['seq'=8,'head'=4] {'seq'}, dimensions={0}, use_global_device_ids=true | all-gather | bytes 18432 | tf_op jit(solution)/shard_map/all_gather | solution.py:115
  84.1 2.8 %fusion.7 = f32[8,1024]{1,0:T(8,128)S(1)} fusion(bf16[2,1024,1024]{2,1,0:T(8,128)(2,1)} %bitcast.87, f32[8,2]{0,1:T(2,128)S(1)} %compare_convert_fusion, bf16[8,1,1024]{2,1,0:T(2,128)(2,1)S(1)} %all-gather), kind=kOutput, calls=%fused_computation.19 | convolution fusion | flops 33579008 | bytes 4243520 | tf_op jit(solution)/shard_map/ik,hkd->ihd/dot_general | solution.py:116
  87.0 10.1 %all-reduce = bf16[4,1024]{1,0:T(4,128)(2,1)S(1)} all-reduce(f32[4,1024]{1,0:T(4,128)S(1)} %reduce_sum.75), channel_id=2, replica_groups=mesh['seq'=8,'head'=4] {'head'}, use_global_device_ids=true, to_apply=%region_15.16.clone | all-reduce | flops 4096 | bytes 24576
  97.2 1.2 %dynamic-slice_convert_fusion = bf16[1,1024]{1,0:T(2,128)(2,1)} fusion(bf16[4,1024]{1,0:T(4,128)(2,1)S(1)} %all-reduce, u32[]{:T(128)} %bitcast.27), kind=kLoop, calls=%fused_computation.39 | loop fusion | bytes 4100 | tf_op jit(solution)/shard_map/convert_element_type | solution.py:121
  (47 shorter events, 0.4 us)
Async XLA Ops:
  0.6 14.1 %copy-start.4 = (s32[4,8]{1,0:T(4,128)S(1)}, s32[4,8]{1,0:T(4,128)}, u32[]{:S(2)}) copy-start(s32[4,8]{1,0:T(4,128)} %param.16) | copy-start | bytes 388
  0.6 14.1 %copy-start = (s32[4,2,32,128]{3,2,1,0:T(8,128)S(1)}, s32[4,2,32,128]{3,2,1,0:T(8,128)}, u32[]{:S(2)}) copy-start(s32[4,2,32,128]{3,2,1,0:T(8,128)} %param.13) | copy-start | bytes 393220
  3.3 25.4 %all-to-all-start = ((bf16[4,8,1]{0,2,1:T(2,128)(2,1)}), bf16[4,8,1]{0,2,1:T(2,128)(2,1)S(1)}, u32[]{:S(2)}, u32[]{:S(2)}) async-start(bf16[4,8,1]{0,2,1:T(2,128)(2,1)} %copy.58), calls=%async_computation | async-start | bytes 8192 | tf_op jit(solution)/shard_map/all_to_all | solution.py:106
  14.8 11.3 %copy-start.1 = (bf16[4,2,128,128]{3,2,1,0:T(8,128)(2,1)S(1)}, bf16[4,2,128,128]{3,2,1,0:T(8,128)(2,1)}, u32[]{:S(2)}) copy-start(bf16[4,2,128,128]{3,2,1,0:T(8,128)(2,1)} %param.12) | copy-start | bytes 786436
  14.8 12.4 %copy-start.2 = (bf16[4,2,128,128]{3,2,1,0:T(8,128)(2,1)S(1)}, bf16[4,2,128,128]{3,2,1,0:T(8,128)(2,1)}, u32[]{:S(2)}) copy-start(bf16[4,2,128,128]{3,2,1,0:T(8,128)(2,1)} %param.11) | copy-start | bytes 786436
  14.8 13.2 %copy-start.6 = (u32[32]{0:T(128)S(1)}, u32[32]{0:T(128)}, u32[]{:S(2)}) copy-start(u32[32]{0:T(128)} %constant.70) | copy-start | bytes 388
  26.1 72.2 %copy-start.5 = (f32[2,4,8]{2,1,0:T(4,128)}, f32[2,4,8]{2,1,0:T(4,128)S(1)}, u32[]{:S(2)}) copy-start(f32[2,4,8]{2,1,0:T(4,128)S(1)} %get-tuple-element.30) | copy-start | bytes 772
  28.7 13.3 %all-to-all-start.2 = ((bf16[4,8,2048]{2,0,1:T(4,128)(2,1)}), bf16[4,8,2048]{2,0,1:T(4,128)(2,1)S(1)}, u32[]{:S(2)}, u32[]{:S(2)}) async-start(bf16[4,8,2048]{2,0,1:T(4,128)(2,1)} %fusion.5), calls=%async_computation.2 | async-start | bytes 262144 | tf_op jit(solution)/shard_map/all_to_all | solution.py:105
  42.0 10.7 %all-to-all-start.1 = ((bf16[4,8,2048]{2,0,1:T(4,128)(2,1)}), bf16[4,8,2048]{2,0,1:T(4,128)(2,1)S(1)}, u32[]{:S(2)}, u32[]{:S(2)}) async-start(bf16[4,8,2048]{2,0,1:T(4,128)(2,1)} %fusion.4), calls=%async_computation.1 | async-start | bytes 262144 | tf_op jit(solution)/shard_map/all_to_all | solution.py:104
  53.7 44.7 %copy-start.3 = (bf16[1,1,1024]{2,1,0:T(2,128)(2,1)}, bf16[1,1,1024]{2,1,0:T(2,128)(2,1)S(1)}, u32[]{:S(2)}) copy-start(bf16[1,1,1024]{2,1,0:T(2,128)(2,1)S(1)} %convert_element_type.94) | copy-start | bytes 6148
where the time goes:
time: 99 us; the launch traced here: 98.4 us
  blocking collectives  40.6 us (41%)
  starting transfers between devices  16.6 us (17%)
  waiting for transfers between devices  13.3 us (13%)
  matrix products  11.4 us (12%)
  other arithmetic  7.87 us (8%)
  local copies, waits for them, and re-layouts  7.55 us (8%)
    all_gather x1, blocking collectives, shards(): piece = lax.all_gather(flat, 'seq', axis=0, tiled=True)  30.4 us
    unnamed x1, blocking collectives  10.1 us
    all_to_all x1, starting transfers between devices, shards(): lax.all_to_all(send_lens, 'seq', split_axis=1, concat_axis=1, tiled=True)  7.28 us
    all_to_all x1, waiting for transfers between devices, shards(): lax.all_to_all(send_keys, 'seq', split_axis=1, concat_axis=1, tiled=True)  6.95 us
    all_to_all x1, waiting for transfers between devices, shards(): lax.all_to_all(send_values, 'seq', split_axis=1, concat_axis=1, tiled=True)  6.38 us
    all_to_all x1, starting transfers between devices, shards(): lax.all_to_all(send_values, 'seq', split_axis=1, concat_axis=1, tiled=True)  5.99 us
    eq x2, other arithmetic, score_group(): code[:, :, None, :] == lax.iota(jnp.int32, cent)[None, None, :, None]  5.33 us
    dot_general x2, matrix products, score_group(): jnp.einsum('pgk,pkt->pgt', tab, onehot, preferred_element_type=jnp.float32)  4.17 us
  transfers between devices with their start and end apart: 3, of which 2 were waited for; matrix products, arithmetic and copies ran while one was open for 19% of the time, Pallas kernels for 0%

commit v1 on v0

v1 whole, which is shorter than its diff:
```python
import functools

import jax
import jax.numpy as jnp
from jax import lax
from jax.experimental import pallas as pl
from jax.experimental.pallas import tpu as pltpu
from jax.sharding import PartitionSpec as P

NEG = -1e30
LANES = 128
NT = (((1,), (1,)), ((), ()))
NN = (((1,), (0,)), ((), ()))


def dot(a, b, dims=NN):
    return lax.dot_general(a, b, dims, preferred_element_type=jnp.float32)


def split(x):
    high = x.astype(jnp.bfloat16)
    low = (x - high.astype(jnp.float32)).astype(jnp.bfloat16)
    return high, low


def chunks(begin, end, body):
    count = end - begin
    step = max(s for s in (1, 2, 3, 4) if count % s == 0)
    if count == step:
        body(begin, step)
    else:
        lax.fori_loop(0, count // step, lambda i, c: (body(begin + i * step, step), c)[1], 0)


def live_rows(len_ref, first, step, tokens, block):
    lens = len_ref[pl.ds(first, step), :]
    lane = lax.broadcasted_iota(jnp.int32, (step, tokens), 1)
    spread = jnp.zeros((step, tokens), jnp.int32)
    for j in range(tokens // block):
        spread = jnp.where(lane // block == j, lens[:, j : j + 1], spread)
    return lane % block < spread


def attend_kernel(
    block,
    q_hbm,
    k_hbm,
    v_hbm,
    picks_hbm,
    len_hbm,
    code_hbm,
    cent_hbm,
    msg_ref,
    q_ref,
    len_ref,
    code_ref,
    cent_ref,
    k_ref,
    v_ref,
    picks_ref,
    acc_ref,
    stat_ref,
    sems,
):
    loads = [
        pltpu.make_async_copy(source, target, sems.at[i])
        for i, (source, target) in enumerate(
            (
                (k_hbm, k_ref),
                (q_hbm, q_ref),
                (picks_hbm, picks_ref),
                (len_hbm, len_ref),
                (v_hbm, v_ref),
                (code_hbm, code_ref),
                (cent_hbm, cent_ref),
            )
        )
    ]
    for load in loads:
        load.start()
    for load in loads[:5]:
        load.wait()
    batch, kv, tokens, feat = k_ref.shape
    group = q_ref.shape[1] // kv
    rows = batch * kv * group
    shard = lax.axis_index("seq")

    def body(first, step):
        live = live_rows(len_ref, first, step, tokens, block)
        lane = lax.broadcasted_iota(jnp.int32, (kv, tokens), 1)
        own = lane // block + shard * (tokens // block)
        for i in range(step):
            b = first + i
            picks = picks_ref[b]
            chosen = picks[:, 0:1] == own
            for k in range(1, picks.shape[1]):
                chosen = chosen | (picks[:, k : k + 1] == own)
            mask = jnp.where(chosen & live[i : i + 1], 1.0, 0.0)
            for h in range(kv):
                on = jnp.broadcast_to(mask[h : h + 1], (group, tokens)) > 0.5
                query = q_ref[b, h * group : (h + 1) * group, :]
                score = dot(query, k_ref[b, h], NT) * feat ** (-0.5)
                score = jnp.where(on, score, NEG)
                top = jnp.max(score, axis=1, keepdims=True)
                weight = jnp.where(on, jnp.exp(score - top), 0.0)
                total = jnp.sum(weight, axis=1, keepdims=True)
                high, low = split(weight)
                value = v_ref[b, h]
                acc = dot(high, value) + dot(low, value)
                place = pl.ds(h * group * batch + b, group, stride=batch)
                acc_ref[place, :] = acc
                lanes = lax.broadcasted_iota(jnp.int32, (group, feat), 1)
                stat_ref[place, :] = jnp.where(lanes < feat // 2, top, total)

    chunks(0, batch, body)
    acc = acc_ref[...].T
    stat = stat_ref[...].T
    top, total = stat[0:1], stat[feat // 2 : feat // 2 + 1]
    pack = max(1, LANES // rows)
    depth = feat // pack
    wide = jnp.concatenate([acc[i * depth : (i + 1) * depth] for i in range(pack)], axis=1)
    msg_ref[0:depth, :] = wide
    stats = jnp.concatenate(
        [jnp.concatenate([row] * pack, axis=1) for row in (top, total)]
        + [jnp.zeros((6, rows * pack), jnp.float32)],
        axis=0,
    )
    msg_ref[depth : depth + 8, :] = stats
    for load in loads[5:]:
        load.wait()


def merge(a, b):
    depth = a.shape[0] - 8
    top_a, top_b = a[depth : depth + 1], b[depth : depth + 1]
    top = jnp.maximum(top_a, top_b)
    scale_a, scale_b = jnp.exp(top_a - top), jnp.exp(top_b - top)
    acc = a[:depth] * scale_a + b[:depth] * scale_b
    total = a[depth + 1 : depth + 2] * scale_a + b[depth + 1 : depth + 2] * scale_b
    return acc, top, total


def merge_kernel(a_ref, b_ref, after, out_ref):
    depth = a_ref.shape[0] - 8
    acc, top, total = merge(a_ref[...], b_ref[...])
    out_ref[0:depth, :] = acc
    out_ref[depth : depth + 8, :] = jnp.concatenate(
        [top, total, jnp.zeros((6, acc.shape[1]), jnp.float32)], axis=0
    )


def project_kernel(batch, kv, feat, a_ref, b_ref, w_ref, attended_ref, keep_ref, send_ref, x_ref):
    acc, _, total = merge(a_ref[...], b_ref[...])
    out = acc / total
    depth = out.shape[0]
    heads = x_ref.shape[1] // feat
    pack = feat // depth
    rows = batch * heads
    tall = jnp.concatenate([out[:, i * rows : (i + 1) * rows] for i in range(pack)], axis=0)
    natural = tall.T
    for q in range(heads):
        x_ref[:, q * feat : (q + 1) * feat] = natural[q * batch : (q + 1) * batch, :]
    own = lax.axis_index("seq")
    span = heads // kv * feat
    start = pl.multiple_of((own % kv) * span, LANES)
    attended_ref[0] = x_ref[pl.ds(own // kv, 1), pl.ds(start, span)].astype(jnp.bfloat16)
    y = dot(x_ref[...].astype(jnp.bfloat16), w_ref[...])
    parts = lax.axis_size("head")
    share = batch // parts
    odd = lax.axis_index("head") % 2 == 1
    even_rows = jnp.concatenate([y[i * share : (i + 1) * share] for i in range(0, parts, 2)], axis=0)
    odd_rows = jnp.concatenate([y[i * share : (i + 1) * share] for i in range(1, parts, 2)], axis=0)
    keep_ref[...] = jnp.where(odd, odd_rows, even_rows)
    send_ref[...] = jnp.where(odd, even_rows, odd_rows)


def estimate_kernel(block, begin, end, q_ref, len_ref, code_ref, cent_ref, est_ref):
    _, kv, nsub, tokens = code_ref.shape
    sub, cent = cent_ref.shape[1], cent_ref.shape[3]
    group = q_ref.shape[1] // kv
    feat = q_ref.shape[2]
    halves = cent // LANES
    d = lax.broadcasted_iota(jnp.int32, (feat, feat), 0)
    k = lax.broadcasted_iota(jnp.int32, (feat, feat), 1)
    perm = jnp.where(d == (k % nsub) * sub + k // nsub, 1.0, 0.0).astype(jnp.bfloat16)
    own = lax.broadcasted_iota(jnp.int32, (group, nsub, feat), 1) == (
        lax.broadcasted_iota(jnp.int32, (group, nsub, feat), 2) % nsub
    )
    books = []
    for h in range(kv):
        high, low = split(cent_ref[h].reshape(sub * nsub, cent))
        books.append(jnp.concatenate([high, low], axis=0))

    def body(first, step):
        live = jnp.where(live_rows(len_ref, first, step, tokens, block), 1.0, 0.0)
        approx, valid = [], []
        for i in range(step):
            b = first + i
            mixed = dot(q_ref[b], perm)
            for h in range(kv):
                query = mixed[h * group : (h + 1) * group]
                spread = jnp.where(own, query[:, None, :], 0.0).reshape(group * nsub, feat)
                spread = spread.astype(jnp.bfloat16)
                table = dot(jnp.concatenate([spread, spread], axis=1), books[h]) * feat ** (-0.5)
                table = table.astype(jnp.bfloat16).astype(jnp.float32)
                code = code_ref[b, h]
                index = code % LANES
                rows = []
                for g in range(group):
                    part = table[g * nsub : (g + 1) * nsub]
                    found = jnp.take_along_axis(
                        part[:, :LANES], index, axis=1, mode="promise_in_bounds"
                    )
                    for c in range(1, halves):
                        other = jnp.take_along_axis(
                            part[:, c * LANES : (c + 1) * LANES],
                            index,
                            axis=1,
                            mode="promise_in_bounds",
                        )
                        found = jnp.where(code >= c * LANES, other, found)
                    rows.append(jnp.sum(found, axis=0, keepdims=True))
                approx.append(jnp.concatenate(rows, axis=0))
                valid.append(jnp.broadcast_to(live[i : i + 1], (group, tokens)) > 0.5)
        pairs = step * kv
        lane = lax.broadcasted_iota(jnp.int32, (pairs, tokens), 1)

        def fold(x, op):
            hop = 1
            while hop < block:
                x = op(x, jnp.take_along_axis(x, lane ^ hop, axis=1, mode="promise_in_bounds"))
                hop *= 2
            return x

        tops = [
            jnp.max(jnp.where(v, a, NEG), axis=0, keepdims=True) for a, v in zip(approx, valid)
        ]
        top = fold(jnp.concatenate(tops, axis=0), jnp.maximum)
        mass = [
            jnp.sum(jnp.where(v, jnp.exp(a - top[p : p + 1]), 0.0), axis=0, keepdims=True)
            for p, (a, v) in enumerate(zip(approx, valid))
        ]
        mass = fold(jnp.concatenate(mass, axis=0), jnp.add)
        est = top + jnp.log(mass)
        blocks = tokens // block
        first_lane = jnp.where(lane < blocks, lane * block, 0)
        est = jnp.take_along_axis(est, first_lane, axis=1, mode="promise_in_bounds")
        for i in range(step):
            est_ref[first + i] = est[i * kv : (i + 1) * kv, :blocks]

    chunks(begin, end, body)


def first_kernel(block, end, q_ref, len_ref, code_ref, cent_ref, w_hbm, est_ref, w_ref, sem):
    copy = pltpu.make_async_copy(w_hbm, w_ref, sem)
    copy.start()
    estimate_kernel(block, 0, end, q_ref, len_ref, code_ref, cent_ref, est_ref)
    copy.wait()


def second_kernel(block, begin, q_ref, len_ref, code_ref, cent_ref, part_ref, after, est_ref, token_ref):
    token_ref[...] = jnp.zeros_like(token_ref)
    est_ref[0:begin] = part_ref[...]
    estimate_kernel(block, begin, code_ref.shape[0], q_ref, len_ref, code_ref, cent_ref, est_ref)


VMEM = pl.BlockSpec(memory_space=pltpu.VMEM)
ANY = pl.BlockSpec(memory_space=pl.ANY)
HBM = pl.BlockSpec(memory_space=pltpu.HBM)


def call(kernel, out, inputs, scratch=(), limit=32, flops=0, data=0):
    return pl.pallas_call(
        kernel,
        out_shape=[shape for shape, _ in out],
        in_specs=[spec for _, spec in inputs],
        out_specs=[spec for _, spec in out],
        scratch_shapes=list(scratch),
        compiler_params=pltpu.CompilerParams(vmem_limit_bytes=limit * 1024 * 1024),
        cost_estimate=pl.CostEstimate(flops=flops, bytes_accessed=data, transcendentals=0),
    )(*[pltpu.with_memory_space_constraint(a, pltpu.HBM) if s is HBM else a for a, s in inputs])


def swap(x, axis, hop):
    size = lax.axis_size(axis)
    return lax.ppermute(x, axis, [(i, i ^ hop) for i in range(size)])


def shards(queries, keys, values, codes, centroids, picks, block_len, out_weight):
    batch, kv, tokens, feat = keys.shape
    heads = queries.shape[1]
    rows = batch * heads
    blocks = block_len.shape[1]
    block = tokens // blocks
    width = out_weight.shape[1]
    seq, parts = lax.axis_size("seq"), lax.axis_size("head")
    pack = max(1, LANES // rows)
    depth = feat // pack

    state = jax.ShapeDtypeStruct((depth + 8, rows * pack), jnp.float32)
    staged = (queries, block_len, codes, centroids)
    message, *staged = call(
        functools.partial(attend_kernel, block),
        [(state, VMEM)] + [(jax.ShapeDtypeStruct(a.shape, a.dtype), VMEM) for a in staged],
        [(a, HBM) for a in (queries, keys, values, picks, block_len, codes, centroids)],
        scratch=[
            pltpu.VMEM(keys.shape, keys.dtype),
            pltpu.VMEM(values.shape, values.dtype),
            pltpu.VMEM(picks.shape, picks.dtype),
            pltpu.VMEM((rows, feat), jnp.float32),
            pltpu.VMEM((rows, feat), jnp.float32),
            pltpu.SemaphoreType.DMA((7,)),
        ],
    )
    half = batch // 2
    source = [(a, VMEM) for a in staged]
    part, weight = call(
        functools.partial(first_kernel, block, half),
        [
            (jax.ShapeDtypeStruct((half, kv, blocks), jnp.float32), VMEM),
            (jax.ShapeDtypeStruct(out_weight.shape, out_weight.dtype), VMEM),
        ],
        source + [(out_weight, HBM)],
        scratch=[pltpu.SemaphoreType.DMA],
        flops=500_000_000,
        data=1 << 22,
    )
    received = swap(message, "seq", 1)
    (message,) = call(
        merge_kernel, [(state, VMEM)], [(message, VMEM), (received, VMEM), (part, ANY)]
    )
    estimates, token = call(
        functools.partial(second_kernel, block, half),
        [
            (jax.ShapeDtypeStruct((batch, kv, blocks), jnp.float32), VMEM),
            (jax.ShapeDtypeStruct((8, LANES), jnp.float32), VMEM),
        ],
        source + [(part, VMEM), (message, ANY)],
        flops=500_000_000,
        data=1 << 22,
    )
    hop = 2
    while hop < seq // 2:
        received = swap(message, "seq", hop)
        (message,) = call(
            merge_kernel, [(state, VMEM)], [(message, VMEM), (received, VMEM), (token, ANY)]
        )
        hop *= 2
    received = swap(message, "seq", hop)
    sums = jax.ShapeDtypeStruct((batch // 2, width), jnp.float32)
    attended, keep, send = call(
        functools.partial(project_kernel, batch, kv, feat),
        [
            (jax.ShapeDtypeStruct((1, 1, heads // kv * feat), jnp.bfloat16), VMEM),
            (sums, VMEM),
            (sums, VMEM),
        ],
        [(message, VMEM), (received, VMEM), (weight, VMEM)],
        scratch=[pltpu.VMEM((batch, heads * feat), jnp.float32)],
    )
    me = lax.axis_index("head")
    total = keep + swap(send, "head", 1)
    hop = 2
    while hop < parts:
        share = total.reshape(2, -1, width) if hop * 2 == parts else None
        upper = (me // hop) % 2 == 1
        total = jnp.where(upper, share[1], share[0]) + swap(
            jnp.where(upper, share[0], share[1]), "head", hop
        )
        hop *= 2
    return (estimates, attended, total.astype(jnp.bfloat16))


def solution(mesh):
    placed = (
        P(None, "head", None),
        P(None, "head", "seq", None),
        P(None, "head", "seq", None),
        P(None, "head", None, "seq"),
        P("head", None, None, None),
        P(None, "head", None),
        P(None, "seq"),
        P("head", "seq"),
    )
    return jax.shard_map(
        shards,
        mesh=mesh,
        in_specs=placed,
        out_specs=(P(None, "head", "seq"), P("seq", "head", None), P("head", "seq")),
        check_vma=False,
    )
```

time: 99 us -> 23.7 us (0.24)
  blocking collectives: 40.6 us -> 0 us
  matrix products: 11.4 us -> 0 us
  waiting for transfers between devices: 13.3 us -> 5.3 us
  local copies, waits for them, and re-layouts: 7.55 us -> 0 us
  Pallas kernels: 0 us -> 7.4 us
  other arithmetic: 7.87 us -> 0.62 us
  starting transfers between devices: 16.6 us -> 9.54 us
    all_gather x1 -> x0, blocking collectives: 30.4 us -> none  [shards(): piece = lax.all_gather(flat, 'seq', axis=0, tiled=True)]
    all_to_all x3 -> x0, starting transfers between devices: 16.6 us -> none  [the longest x1 7.28 us: shards(): lax.all_to_all(send_lens, 'seq', split_axis=1, concat_axis=1, tiled=True)]
    all_to_all x3 -> x0, waiting for transfers between devices: 13.3 us -> none  [the longest x1 6.95 us: shards(): lax.all_to_all(send_keys, 'seq', split_axis=1, concat_axis=1, tiled=True)]
    dot_general x9 -> x0, matrix products: 11.4 us -> none  [the longest x2 4.17 us: score_group(): jnp.einsum('pgk,pkt->pgt', tab, onehot, preferred_element_type=jnp.float32)]
    unnamed x1 -> x0, blocking collectives: 10.1 us -> none
    ppermute x0 -> x5, starting transfers between devices: none -> 9.54 us  [swap(): return lax.ppermute(x, axis, [(i, i ^ hop) for i in range(size)])]
    pallas_call x0 -> x6, Pallas kernels: none -> 7.4 us  [call(): pl.pallas_call(kernel, out_shape=[shape for shape, _ in out], in_specs=[s...]
    eq x2 -> x0, other arithmetic: 5.33 us -> none  [score_group(): code[:, :, None, :] == lax.iota(jnp.int32, cent)[None, None, :, None]]
  transfers between devices with their start and end apart: 3 -> 5, of which waited for: 2 -> 4; matrix products, arithmetic and copies ran while one was open for 19% -> 0% of each run, Pallas kernels for 0% -> 18%
where the time goes in v1:
time: 23.7 us; the launch traced here: 23.5 us
  starting transfers between devices  9.54 us (40%)
  Pallas kernels  7.4 us (31%)
  waiting for transfers between devices  5.3 us (22%)
  between operations  0.68 us (3%)
  other arithmetic  0.62 us (3%)
    ppermute x5, starting transfers between devices, swap(): return lax.ppermute(x, axis, [(i, i ^ hop) for i in range(size)])  9.54 us
    pallas_call x6, Pallas kernels, call(): pl.pallas_call(kernel, out_shape=[shape for shape, _ in out], in_specs=[s...  7.4 us
    ppermute x5, waiting for transfers between devices, swap(): return lax.ppermute(x, axis, [(i, i ^ hop) for i in range(size)])  5.3 us
    convert_element_type x1, other arithmetic, shards(): return (estimates, attended, total.astype(jnp.bfloat16))  0.6 us
  transfers between devices with their start and end apart: 5, of which 4 were waited for; matrix products, arithmetic and copies ran while one was open for 0% of the time, Pallas kernels for 18%

profile of v1, /device:TPU:0, one launch (start us, length us, event | category | flops | bytes accessed | tf_op | source)
XLA Modules:
  0.0 23.5 jit_solution(9354215795420820715)
XLA Ops:
  0.6 2.0 %shard_map.103 = (f32[72,128]{1,0:T(8,128)S(1)}, bf16[4,16,128]{2,1,0:T(8,128)(2,1)S(1)}, s32[4,8]{1,0:T(4,128)S(1)}, s32[4,2,32,128]{3,2,1,0:T(8,128)S(1)}, f32[2,4,32,256]{3,2,1,0:T(8,128)S(1)}) custom-call(bf16[4,16,128]{2,1,0:T(8,128)(2,1)} %q_hbm.1, bf16[4,2,128,128]{3,2,1,0:T(8,128)(2,1)} %k_hbm.1, bf16[4,2,128,128]{3,2,1,0:T(8,128)(2,1)} %v_hbm.1, ...), custom_call_target="tpu_custom_call" | custom-call | tf_op jit(solution)/shard_map/pallas_call | solution.py:273
  2.6 3.0 %collective-permute-start = (f32[72,128]{1,0:T(8,128)S(1)}, f32[72,128]{1,0:T(8,128)S(1)}, u32[]{:S(2)}, u32[]{:S(2)}) collective-permute-start(f32[72,128]{1,0:T(8,128)S(1)} %get-tuple-element.20.a_ref), channel_id=1, source_target_pairs={{0,4},{4,0},{8,12},{12,8},{16,20},{20,16},{24,28},{28,24},{1,5},{5... | collective-permute-start | bytes 110600 | tf_op jit(solution)/shard_map/ppermute | solution.py:286
  5.6 2.2 %shard_map.104 = (f32[2,2,8]{2,1,0:T(2,128)S(1)}, bf16[2048,1024]{1,0:T(8,128)(2,1)S(1)}) custom-call(bf16[4,16,128]{2,1,0:T(8,128)(2,1)S(1)} %get-tuple-element.15.q_ref, s32[4,8]{1,0:T(4,128)S(1)} %get-tuple-element.16.len_ref, s32[4,2,32,128]{3,2,1,0:T(8,128)S(1)} %get-tuple-element.17.code_ref, f32[2,4,32,256]{3,2,1,0:T(8,128)S(1)} %get-tuple-element.18.cent_ref, ...), custom_call_target="tpu_custom_call" | custom-call | flops 500000000 | bytes 4194304 | tf_op jit(solution)/shard_map/pallas_call | solution.py:273
  7.8 0.0 collective-permute-done.b_ref
  7.9 1.9 %collective-permute-start.1 = (f32[72,128]{1,0:T(8,128)S(1)}, f32[72,128]{1,0:T(8,128)S(1)}, u32[]{:S(2)}, u32[]{:S(2)}) collective-permute-start(f32[72,128]{1,0:T(8,128)S(1)} %shard_map.105.after.a_ref), channel_id=1, source_target_pairs={{0,8},{4,12},{8,0},{12,4},{16,24},{20,28},{24,16},{28,20},{1,9},{5... | collective-permute-start | bytes 110600 | tf_op jit(solution)/shard_map/ppermute | solution.py:286
  9.7 2.0 %shard_map.106 = (f32[4,2,8]{2,1,0:T(2,128)}, f32[8,128]{1,0:T(8,128)S(1)}) custom-call(bf16[4,16,128]{2,1,0:T(8,128)(2,1)S(1)} %get-tuple-element.15.q_ref, s32[4,8]{1,0:T(4,128)S(1)} %get-tuple-element.16.len_ref, s32[4,2,32,128]{3,2,1,0:T(8,128)S(1)} %get-tuple-element.17.code_ref, f32[2,4,32,256]{3,2,1,0:T(8,128)S(1)} %get-tuple-element.18.cent_ref, ...), custom_call_target="tpu_custom_call" | custom-call | flops 500000000 | bytes 4194304 | tf_op jit(solution)/shard_map/pallas_call | solution.py:273
  11.7 0.2 collective-permute-done.1.b_ref
  11.9 2.9 %collective-permute-start.2 = (f32[72,128]{1,0:T(8,128)S(1)}, f32[72,128]{1,0:T(8,128)S(1)}, u32[]{:S(2)}, u32[]{:S(2)}) collective-permute-start(f32[72,128]{1,0:T(8,128)S(1)} %shard_map.107.a_ref), channel_id=1, source_target_pairs={{0,16},{4,20},{8,24},{12,28},{16,0},{20,4},{24,8},{28,12},{1,17},{... | collective-permute-start | bytes 110600 | tf_op jit(solution)/shard_map/ppermute | solution.py:286
  14.8 2.0 %collective-permute-done.2.b_ref = f32[72,128]{1,0:T(8,128)S(1)} collective-permute-done((f32[72,128]{1,0:T(8,128)S(1)}, f32[72,128]{1,0:T(8,128)S(1)}, u32[]{:S(2)}, u32[]{:S(2)}) %collective-permute-start.2) | collective-permute-done | bytes 36896 | tf_op jit(solution)/shard_map/ppermute | solution.py:286
  16.8 1.2 %shard_map.108 = (bf16[1,1,1024]{2,1,0:T(2,128)(2,1)}, f32[2,1024]{1,0:T(2,128)S(1)}, f32[2,1024]{1,0:T(2,128)S(1)}) custom-call(f32[72,128]{1,0:T(8,128)S(1)} %shard_map.107.a_ref, f32[72,128]{1,0:T(8,128)S(1)} %collective-permute-done.2.b_ref, bf16[2048,1024]{1,0:T(8,128)(2,1)S(1)} %get-tuple-element.23.w_ref), custom_call_target="tpu_custom_call" | custom-call | tf_op jit(solution)/shard_map/pallas_call | solution.py:273
  18.1 0.0 collective-permute-start.3
  18.1 1.2 %collective-permute-done.3 = f32[2,1024]{1,0:T(2,128)S(1)} collective-permute-done((f32[2,1024]{1,0:T(2,128)S(1)}, f32[2,1024]{1,0:T(2,128)S(1)}, u32[]{:S(2)}, u32[]{:S(2)}) %collective-permute-start.3) | collective-permute-done | bytes 8224 | tf_op jit(solution)/shard_map/ppermute | solution.py:286
  19.3 1.8 %collective-permute-start.4 = (f32[1,1024]{1,0:T(1,128)S(1)}, f32[1,1024]{1,0:T(1,128)S(1)}, u32[]{:S(2)}, u32[]{:S(2)}) collective-permute-start(f32[1,1024]{1,0:T(1,128)S(1)} %broadcast_select_fusion), channel_id=1, source_target_pairs={{0,2},{1,3},{2,0},{3,1},{4,6},{5,7},{6,4},{7,5},{8,10},{9,11},{10,... | collective-permute-start | bytes 12296 | tf_op jit(solution)/shard_map/ppermute | solution.py:286
  21.0 1.9 %collective-permute-done.4 = f32[1,1024]{1,0:T(1,128)S(1)} collective-permute-done((f32[1,1024]{1,0:T(1,128)S(1)}, f32[1,1024]{1,0:T(1,128)S(1)}, u32[]{:S(2)}, u32[]{:S(2)}) %collective-permute-start.4) | collective-permute-done | bytes 4128 | tf_op jit(solution)/shard_map/ppermute | solution.py:286
  22.9 0.6 %fusion.1 = bf16[1,1024]{1,0:T(2,128)(2,1)} fusion(f32[1,1024]{1,0:T(1,128)S(1)} %collective-permute-done.4, pred[]{:T(512)S(6)} %eq.5, f32[2,1024]{1,0:T(2,128)S(1)} %add.12), kind=kLoop, calls=%fused_computation.3 | loop fusion | flops 3072 | bytes 14337 | tf_op jit(solution)/shard_map/convert_element_type | solution.py:371
  (4 shorter events, 0.0 us)
Async XLA Ops:
  2.6 5.2 %collective-permute-start = (f32[72,128]{1,0:T(8,128)S(1)}, f32[72,128]{1,0:T(8,128)S(1)}, u32[]{:S(2)}, u32[]{:S(2)}) collective-permute-start(f32[72,128]{1,0:T(8,128)S(1)} %get-tuple-element.20.a_ref), channel_id=1, source_target_pairs={{0,4},{4,0},{8,12},{12,8},{16,20},{20,16},{24,28},{28,24},{1,5},{5... | collective-permute-start | bytes 110600 | tf_op jit(solution)/shard_map/ppermute | solution.py:286
  7.9 4.0 %collective-permute-start.1 = (f32[72,128]{1,0:T(8,128)S(1)}, f32[72,128]{1,0:T(8,128)S(1)}, u32[]{:S(2)}, u32[]{:S(2)}) collective-permute-start(f32[72,128]{1,0:T(8,128)S(1)} %shard_map.105.after.a_ref), channel_id=1, source_target_pairs={{0,8},{4,12},{8,0},{12,4},{16,24},{20,28},{24,16},{28,20},{1,9},{5... | collective-permute-start | bytes 110600 | tf_op jit(solution)/shard_map/ppermute | solution.py:286
  11.9 4.9 %collective-permute-start.2 = (f32[72,128]{1,0:T(8,128)S(1)}, f32[72,128]{1,0:T(8,128)S(1)}, u32[]{:S(2)}, u32[]{:S(2)}) collective-permute-start(f32[72,128]{1,0:T(8,128)S(1)} %shard_map.107.a_ref), channel_id=1, source_target_pairs={{0,16},{4,20},{8,24},{12,28},{16,0},{20,4},{24,8},{28,12},{1,17},{... | collective-permute-start | bytes 110600 | tf_op jit(solution)/shard_map/ppermute | solution.py:286
  18.1 1.2 %collective-permute-start.3 = (f32[2,1024]{1,0:T(2,128)S(1)}, f32[2,1024]{1,0:T(2,128)S(1)}, u32[]{:S(2)}, u32[]{:S(2)}) collective-permute-start(f32[2,1024]{1,0:T(2,128)S(1)} %get-tuple-element.26), channel_id=1, source_target_pairs={{0,1},{1,0},{2,3},{3,2},{4,5},{5,4},{6,7},{7,6},{8,9},{9,8},{10,11... | collective-permute-start | bytes 24584 | tf_op jit(solution)/shard_map/ppermute | solution.py:286
  19.3 3.7 %collective-permute-start.4 = (f32[1,1024]{1,0:T(1,128)S(1)}, f32[1,1024]{1,0:T(1,128)S(1)}, u32[]{:S(2)}, u32[]{:S(2)}) collective-permute-start(f32[1,1024]{1,0:T(1,128)S(1)} %broadcast_select_fusion), channel_id=1, source_target_pairs={{0,2},{1,3},{2,0},{3,1},{4,6},{5,7},{6,4},{7,5},{8,10},{9,11},{10,... | collective-permute-start | bytes 12296 | tf_op jit(solution)/shard_map/ppermute | solution.py:286

commit v2 on v1

--- a/solution.py
+++ b/solution.py
@@ -11,6 +11,7 @@
 LANES = 128
 NT = (((1,), (1,)), ((), ()))
 NN = (((1,), (0,)), ((), ()))
+TN = (((0,), (0,)), ((), ()))
 
 
 def dot(a, b, dims=NN):
@@ -23,9 +24,18 @@
     return high, low
 
 
+def request_step(count):
+    return max(s for s in (1, 2, 4) if count % s == 0)
+
+
+def lane_plan(batch, heads):
+    step = min(batch, LANES // heads)
+    return step, LANES // (step * heads)
+
+
 def chunks(begin, end, body):
     count = end - begin
-    step = max(s for s in (1, 2, 3, 4) if count % s == 0)
+    step = request_step(count)
     if count == step:
         body(begin, step)
     else:
@@ -58,18 +68,16 @@
     k_ref,
     v_ref,
     picks_ref,
-    acc_ref,
-    stat_ref,
     sems,
 ):
     loads = [
         pltpu.make_async_copy(source, target, sems.at[i])
         for i, (source, target) in enumerate(
             (
-                (k_hbm, k_ref),
-                (q_hbm, q_ref),
                 (picks_hbm, picks_ref),
                 (len_hbm, len_ref),
+                (q_hbm, q_ref),
+                (k_hbm, k_ref),
                 (v_hbm, v_ref),
                 (code_hbm, code_ref),
                 (cent_hbm, cent_ref),
@@ -78,54 +86,71 @@
     ]
     for load in loads:
         load.start()
-    for load in loads[:5]:
+    batch, kv, tokens, feat = k_ref.shape
+    heads = q_ref.shape[1]
+    group = heads // kv
+    blocks = tokens // block
+    shard = lax.axis_index("seq")
+    step, copies = lane_plan(batch, heads)
+    pairs, lanes = step * kv, step * heads * copies
+    depth = feat // copies
+    place = lax.broadcasted_iota(jnp.int32, (block, lanes), 0)
+    lane = lax.broadcasted_iota(jnp.int32, (tokens, lanes), 1)
+    owner = lane % (step * heads) // group
+    expand = jnp.where(
+        lax.broadcasted_iota(jnp.int32, (pairs, lanes), 0) == owner[:pairs], 1.0, 0.0
+    )
+
+    def own(x, size):
+        kept = x[:size]
+        for p in range(1, pairs):
+            kept = jnp.where(owner[:size] == p, x[p * size : (p + 1) * size], kept)
+        return kept
+
+    for load in loads[:3]:
         load.wait()
-    batch, kv, tokens, feat = k_ref.shape
-    group = q_ref.shape[1] // kv
-    rows = batch * kv * group
-    shard = lax.axis_index("seq")
-
-    def body(first, step):
-        live = live_rows(len_ref, first, step, tokens, block)
-        lane = lax.broadcasted_iota(jnp.int32, (kv, tokens), 1)
-        own = lane // block + shard * (tokens // block)
-        for i in range(step):
-            b = first + i
-            picks = picks_ref[b]
-            chosen = picks[:, 0:1] == own
-            for k in range(1, picks.shape[1]):
-                chosen = chosen | (picks[:, k : k + 1] == own)
-            mask = jnp.where(chosen & live[i : i + 1], 1.0, 0.0)
-            for h in range(kv):
-                on = jnp.broadcast_to(mask[h : h + 1], (group, tokens)) > 0.5
-                query = q_ref[b, h * group : (h + 1) * group, :]
-                score = dot(query, k_ref[b, h], NT) * feat ** (-0.5)
-                score = jnp.where(on, score, NEG)
-                top = jnp.max(score, axis=1, keepdims=True)
-                weight = jnp.where(on, jnp.exp(score - top), 0.0)
-                total = jnp.sum(weight, axis=1, keepdims=True)
-                high, low = split(weight)
-                value = v_ref[b, h]
-                acc = dot(high, value) + dot(low, value)
-                place = pl.ds(h * group * batch + b, group, stride=batch)
-                acc_ref[place, :] = acc
-                lanes = lax.broadcasted_iota(jnp.int32, (group, feat), 1)
-                stat_ref[place, :] = jnp.where(lanes < feat // 2, top, total)
-
-    chunks(0, batch, body)
-    acc = acc_ref[...].T
-    stat = stat_ref[...].T
-    top, total = stat[0:1], stat[feat // 2 : feat // 2 + 1]
-    pack = max(1, LANES // rows)
-    depth = feat // pack
-    wide = jnp.concatenate([acc[i * depth : (i + 1) * depth] for i in range(pack)], axis=1)
-    msg_ref[0:depth, :] = wide
-    stats = jnp.concatenate(
-        [jnp.concatenate([row] * pack, axis=1) for row in (top, total)]
-        + [jnp.zeros((6, rows * pack), jnp.float32)],
-        axis=0,
-    )
-    msg_ref[depth : depth + 8, :] = stats
+    limits = []
+    for first in range(0, batch, step):
+        picks = jnp.concatenate([picks_ref[first + i] for i in range(step)], axis=0)
+        lens = jnp.concatenate(
+            [len_ref[first + i : first + i + 1, :] for i in range(step) for _ in range(kv)], axis=0
+        )
+        number = lax.broadcasted_iota(jnp.int32, (pairs, blocks), 1) + shard * blocks
+        chosen = picks[:, 0:1] == number
+        for k in range(1, picks.shape[1]):
+            chosen = chosen | (picks[:, k : k + 1] == number)
+        limit = jnp.where(chosen, lens.astype(jnp.float32), 0.0)
+        limits.append(dot(limit, expand, TN).astype(jnp.int32))
+    loads[3].wait()
+    for c, first in enumerate(range(0, batch, step)):
+        some = pl.ds(first, step)
+        query = q_ref[some].reshape(step * heads, feat)
+        query = jnp.concatenate([query] * copies, axis=0)
+        score = own(dot(k_ref[some].reshape(pairs * tokens, feat), query, NT), tokens)
+        if first == 0:
+            loads[4].wait()
+        on = jnp.concatenate([place < limits[c][j : j + 1] for j in range(blocks)], axis=0)
+        score = jnp.where(on, score * feat ** (-0.5), NEG)
+        top = jnp.max(score, axis=0, keepdims=True)
+        weight = jnp.where(on, jnp.exp(score - top), 0.0)
+        total = jnp.sum(weight, axis=0, keepdims=True)
+        turned = jnp.concatenate(
+            [v_ref[first + p // kv, p % kv].T for p in range(pairs)], axis=0
+        )
+        acc = dot(
+            jnp.concatenate([turned, turned], axis=1), jnp.concatenate(split(weight), axis=0)
+        )
+        acc = own(acc, feat)
+        wide = acc[:depth]
+        for i in range(1, copies):
+            wide = jnp.where(
+                lane[:depth] < i * step * heads, wide, acc[i * depth : (i + 1) * depth]
+            )
+        here = slice(c * lanes, (c + 1) * lanes)
+        msg_ref[0:depth, here] = wide
+        msg_ref[depth : depth + 8, here] = jnp.concatenate(
+            [top, total, jnp.zeros((6, lanes), jnp.float32)], axis=0
+        )
     for load in loads[5:]:
         load.wait()
 
@@ -149,7 +174,7 @@
     )
 
 
-def project_kernel(batch, kv, feat, a_ref, b_ref, w_ref, attended_ref, keep_ref, send_ref, x_ref):
+def project_kernel(batch, kv, feat, a_ref, b_ref, w_ref, attended_ref, keep_ref, send_ref, x_ref, o_ref):
     acc, _, total = merge(a_ref[...], b_ref[...])
     out = acc / total
     depth = out.shape[0]
@@ -157,9 +182,9 @@
     pack = feat // depth
     rows = batch * heads
     tall = jnp.concatenate([out[:, i * rows : (i + 1) * rows] for i in range(pack)], axis=0)
-    natural = tall.T
+    o_ref[...] = tall.T
     for q in range(heads):
-        x_ref[:, q * feat : (q + 1) * feat] = natural[q * batch : (q + 1) * batch, :]
+        x_ref[:, q * feat : (q + 1) * feat] = o_ref[pl.ds(q, batch, stride=heads), :]
     own = lax.axis_index("seq")
     span = heads // kv * feat
     start = pl.multiple_of((own % kv) * span, LANES)
@@ -294,7 +319,7 @@
     block = tokens // blocks
     width = out_weight.shape[1]
     seq, parts = lax.axis_size("seq"), lax.axis_size("head")
-    pack = max(1, LANES // rows)
+    pack = lane_plan(batch, heads)[1]
     depth = feat // pack
 
     state = jax.ShapeDtypeStruct((depth + 8, rows * pack), jnp.float32)
@@ -307,8 +332,6 @@
             pltpu.VMEM(keys.shape, keys.dtype),
             pltpu.VMEM(values.shape, values.dtype),
             pltpu.VMEM(picks.shape, picks.dtype),
-            pltpu.VMEM((rows, feat), jnp.float32),
-            pltpu.VMEM((rows, feat), jnp.float32),
             pltpu.SemaphoreType.DMA((7,)),
         ],
     )
@@ -332,7 +355,7 @@
     estimates, token = call(
         functools.partial(second_kernel, block, half),
         [
-            (jax.ShapeDtypeStruct((batch, kv, blocks), jnp.float32), VMEM),
+            (pltpu.VMEM((batch, kv, blocks), jnp.float32), VMEM),
             (jax.ShapeDtypeStruct((8, LANES), jnp.float32), VMEM),
         ],
         source + [(part, VMEM), (message, ANY)],
@@ -351,12 +374,15 @@
     attended, keep, send = call(
         functools.partial(project_kernel, batch, kv, feat),
         [
-            (jax.ShapeDtypeStruct((1, 1, heads // kv * feat), jnp.bfloat16), VMEM),
+            (pltpu.VMEM((1, 1, heads // kv * feat), jnp.bfloat16), VMEM),
             (sums, VMEM),
             (sums, VMEM),
         ],
         [(message, VMEM), (received, VMEM), (weight, VMEM)],
-        scratch=[pltpu.VMEM((batch, heads * feat), jnp.float32)],
+        scratch=[
+            pltpu.VMEM((batch, heads * feat), jnp.float32),
+            pltpu.VMEM((rows, feat), jnp.float32),
+        ],
     )
     me = lax.axis_index("head")
     total = keep + swap(send, "head", 1)

time: 23.7 us -> 23.1 us (0.975)
  Pallas kernels: 7.4 us -> 6.14 us
  local copies, waits for them, and re-layouts: 0 us -> 1.18 us
  waiting for transfers between devices: 5.3 us -> 4.69 us
    pallas_call x6, Pallas kernels: 7.4 us -> 6.14 us  [call(): pl.pallas_call(kernel, out_shape=[shape for shape, _ in out], in_specs=[s...]
    unnamed x0 -> x2, local copies, waits for them, and re-layouts: none -> 1.18 us
    ppermute x5, waiting for transfers between devices: 5.3 us -> 4.69 us  [swap(): return lax.ppermute(x, axis, [(i, i ^ hop) for i in range(size)])]
  transfers between devices with their start and end apart: 5 -> 5, of which waited for: 4 -> 4; matrix products, arithmetic and copies ran while one was open for 0% -> 5% of each run, Pallas kernels for 18% -> 16%
where the time goes in v2:
time: 23.1 us; the launch traced here: 22.9 us
  starting transfers between devices  9.55 us (41%)
  Pallas kernels  6.14 us (27%)
  waiting for transfers between devices  4.69 us (20%)
  local copies, waits for them, and re-layouts  1.18 us (5%)
  between operations  0.71 us (3%)
  other arithmetic  0.62 us (3%)
    ppermute x5, starting transfers between devices, swap(): return lax.ppermute(x, axis, [(i, i ^ hop) for i in range(size)])  9.55 us
    pallas_call x6, Pallas kernels, call(): pl.pallas_call(kernel, out_shape=[shape for shape, _ in out], in_specs=[s...  6.14 us
    ppermute x5, waiting for transfers between devices, swap(): return lax.ppermute(x, axis, [(i, i ^ hop) for i in range(size)])  4.69 us
    unnamed x2, local copies, waits for them, and re-layouts  1.18 us
    convert_element_type x1, other arithmetic, shards(): return (estimates, attended, total.astype(jnp.bfloat16))  0.6 us
  transfers between devices with their start and end apart: 5, of which 4 were waited for; matrix products, arithmetic and copies ran while one was open for 5% of the time, Pallas kernels for 16%

profile of v2, /device:TPU:0, one launch (start us, length us, event | category | flops | bytes accessed | tf_op | source)
XLA Modules:
  0.0 22.9 jit_solution(6148073066366698885)
XLA Ops:
  0.6 1.7 %shard_map.103 = (f32[72,128]{1,0:T(8,128)S(1)}, bf16[4,16,128]{2,1,0:T(8,128)(2,1)S(1)}, s32[4,8]{1,0:T(4,128)S(1)}, s32[4,2,32,128]{3,2,1,0:T(8,128)S(1)}, f32[2,4,32,256]{3,2,1,0:T(8,128)S(1)}) custom-call(bf16[4,16,128]{2,1,0:T(8,128)(2,1)} %q_hbm.1, bf16[4,2,128,128]{3,2,1,0:T(8,128)(2,1)} %k_hbm.1, bf16[4,2,128,128]{3,2,1,0:T(8,128)(2,1)} %v_hbm.1, ...), custom_call_target="tpu_custom_call" | custom-call | tf_op jit(solution)/shard_map/pallas_call | solution.py:298
  2.4 3.0 %collective-permute-start = (f32[72,128]{1,0:T(8,128)S(1)}, f32[72,128]{1,0:T(8,128)S(1)}, u32[]{:S(2)}, u32[]{:S(2)}) collective-permute-start(f32[72,128]{1,0:T(8,128)S(1)} %get-tuple-element.20.a_ref), channel_id=1, source_target_pairs={{0,4},{4,0},{8,12},{12,8},{16,20},{20,16},{24,28},{28,24},{1,5},{5... | collective-permute-start | bytes 110600 | tf_op jit(solution)/shard_map/ppermute | solution.py:311
  5.4 2.2 %shard_map.104 = (f32[2,2,8]{2,1,0:T(2,128)S(1)}, bf16[2048,1024]{1,0:T(8,128)(2,1)S(1)}) custom-call(bf16[4,16,128]{2,1,0:T(8,128)(2,1)S(1)} %get-tuple-element.15.q_ref, s32[4,8]{1,0:T(4,128)S(1)} %get-tuple-element.16.len_ref, s32[4,2,32,128]{3,2,1,0:T(8,128)S(1)} %get-tuple-element.17.code_ref, f32[2,4,32,256]{3,2,1,0:T(8,128)S(1)} %get-tuple-element.18.cent_ref, ...), custom_call_target="tpu_custom_call" | custom-call | flops 500000000 | bytes 4194304 | tf_op jit(solution)/shard_map/pallas_call | solution.py:298
  7.6 0.0 collective-permute-done.b_ref
  7.7 1.9 %collective-permute-start.1 = (f32[72,128]{1,0:T(8,128)S(1)}, f32[72,128]{1,0:T(8,128)S(1)}, u32[]{:S(2)}, u32[]{:S(2)}) collective-permute-start(f32[72,128]{1,0:T(8,128)S(1)} %shard_map.105.after.a_ref), channel_id=1, source_target_pairs={{0,8},{4,12},{8,0},{12,4},{16,24},{20,28},{24,16},{28,20},{1,9},{5... | collective-permute-start | bytes 110600 | tf_op jit(solution)/shard_map/ppermute | solution.py:311
  9.5 1.4 %shard_map.106 = (f32[4,2,8]{2,1,0:T(2,128)S(1)}, f32[8,128]{1,0:T(8,128)S(1)}) custom-call(bf16[4,16,128]{2,1,0:T(8,128)(2,1)S(1)} %get-tuple-element.15.q_ref, s32[4,8]{1,0:T(4,128)S(1)} %get-tuple-element.16.len_ref, s32[4,2,32,128]{3,2,1,0:T(8,128)S(1)} %get-tuple-element.17.code_ref, f32[2,4,32,256]{3,2,1,0:T(8,128)S(1)} %get-tuple-element.18.cent_ref, ...), custom_call_target="tpu_custom_call" | custom-call | flops 500000000 | bytes 4194304 | tf_op jit(solution)/shard_map/pallas_call | solution.py:298
  10.9 0.8 %collective-permute-done.1.b_ref = f32[72,128]{1,0:T(8,128)S(1)} collective-permute-done((f32[72,128]{1,0:T(8,128)S(1)}, f32[72,128]{1,0:T(8,128)S(1)}, u32[]{:S(2)}, u32[]{:S(2)}) %collective-permute-start.1) | collective-permute-done | bytes 36896 | tf_op jit(solution)/shard_map/ppermute | solution.py:311
  11.7 2.9 %collective-permute-start.2 = (f32[72,128]{1,0:T(8,128)S(1)}, f32[72,128]{1,0:T(8,128)S(1)}, u32[]{:S(2)}, u32[]{:S(2)}) collective-permute-start(f32[72,128]{1,0:T(8,128)S(1)} %shard_map.107.a_ref), channel_id=1, source_target_pairs={{0,16},{4,20},{8,24},{12,28},{16,0},{20,4},{24,8},{28,12},{1,17},{... | collective-permute-start | bytes 110600 | tf_op jit(solution)/shard_map/ppermute | solution.py:311
  14.6 2.0 %collective-permute-done.2.b_ref = f32[72,128]{1,0:T(8,128)S(1)} collective-permute-done((f32[72,128]{1,0:T(8,128)S(1)}, f32[72,128]{1,0:T(8,128)S(1)}, u32[]{:S(2)}, u32[]{:S(2)}) %collective-permute-start.2) | collective-permute-done | bytes 36896 | tf_op jit(solution)/shard_map/ppermute | solution.py:311
  16.6 0.8 %shard_map.108 = (bf16[1,1,1024]{2,1,0:T(2,128)(2,1)S(1)}, f32[2,1024]{1,0:T(2,128)S(1)}, f32[2,1024]{1,0:T(2,128)S(1)}) custom-call(f32[72,128]{1,0:T(8,128)S(1)} %shard_map.107.a_ref, f32[72,128]{1,0:T(8,128)S(1)} %collective-permute-done.2.b_ref, bf16[2048,1024]{1,0:T(8,128)(2,1)S(1)} %get-tuple-element.23.w_ref), custom_call_target="tpu_custom_call" | custom-call | tf_op jit(solution)/shard_map/pallas_call | solution.py:298
  17.4 0.0 collective-permute-start.3
  17.5 1.1 %collective-permute-done.3 = f32[2,1024]{1,0:T(2,128)S(1)} collective-permute-done((f32[2,1024]{1,0:T(2,128)S(1)}, f32[2,1024]{1,0:T(2,128)S(1)}, u32[]{:S(2)}, u32[]{:S(2)}) %collective-permute-start.3) | collective-permute-done | bytes 8224 | tf_op jit(solution)/shard_map/ppermute | solution.py:311
  18.6 1.8 %collective-permute-start.4 = (f32[1,1024]{1,0:T(1,128)S(1)}, f32[1,1024]{1,0:T(1,128)S(1)}, u32[]{:S(2)}, u32[]{:S(2)}) collective-permute-start(f32[1,1024]{1,0:T(1,128)S(1)} %broadcast_select_fusion), channel_id=1, source_target_pairs={{0,2},{1,3},{2,0},{3,1},{4,6},{5,7},{6,4},{7,5},{8,10},{9,11},{10,... | collective-permute-start | bytes 12296 | tf_op jit(solution)/shard_map/ppermute | solution.py:311
  20.4 0.6 %copy.11 = f32[4,2,8]{2,1,0:T(2,128)} copy(f32[4,2,8]{2,1,0:T(2,128)S(1)} %get-tuple-element.27) | data formatting | bytes 512
  21.0 0.6 %copy.12 = bf16[1,1,1024]{2,1,0:T(2,128)(2,1)} copy(bf16[1,1,1024]{2,1,0:T(2,128)(2,1)S(1)} %get-tuple-element.28) | data formatting | bytes 4096
  21.6 0.7 %collective-permute-done.4 = f32[1,1024]{1,0:T(1,128)S(1)} collective-permute-done((f32[1,1024]{1,0:T(1,128)S(1)}, f32[1,1024]{1,0:T(1,128)S(1)}, u32[]{:S(2)}, u32[]{:S(2)}) %collective-permute-start.4) | collective-permute-done | bytes 4128 | tf_op jit(solution)/shard_map/ppermute | solution.py:311
  22.3 0.6 %fusion.1 = bf16[1,1024]{1,0:T(2,128)(2,1)} fusion(f32[1,1024]{1,0:T(1,128)S(1)} %collective-permute-done.4, pred[]{:T(512)S(6)} %eq.5, f32[2,1024]{1,0:T(2,128)S(1)} %add.12), kind=kLoop, calls=%fused_computation.3 | loop fusion | flops 3072 | bytes 14337 | tf_op jit(solution)/shard_map/convert_element_type | solution.py:397
  (4 shorter events, 0.0 us)
Async XLA Ops:
  2.4 5.2 %collective-permute-start = (f32[72,128]{1,0:T(8,128)S(1)}, f32[72,128]{1,0:T(8,128)S(1)}, u32[]{:S(2)}, u32[]{:S(2)}) collective-permute-start(f32[72,128]{1,0:T(8,128)S(1)} %get-tuple-element.20.a_ref), channel_id=1, source_target_pairs={{0,4},{4,0},{8,12},{12,8},{16,20},{20,16},{24,28},{28,24},{1,5},{5... | collective-permute-start | bytes 110600 | tf_op jit(solution)/shard_map/ppermute | solution.py:311
  7.7 4.0 %collective-permute-start.1 = (f32[72,128]{1,0:T(8,128)S(1)}, f32[72,128]{1,0:T(8,128)S(1)}, u32[]{:S(2)}, u32[]{:S(2)}) collective-permute-start(f32[72,128]{1,0:T(8,128)S(1)} %shard_map.105.after.a_ref), channel_id=1, source_target_pairs={{0,8},{4,12},{8,0},{12,4},{16,24},{20,28},{24,16},{28,20},{1,9},{5... | collective-permute-start | bytes 110600 | tf_op jit(solution)/shard_map/ppermute | solution.py:311
  11.7 4.9 %collective-permute-start.2 = (f32[72,128]{1,0:T(8,128)S(1)}, f32[72,128]{1,0:T(8,128)S(1)}, u32[]{:S(2)}, u32[]{:S(2)}) collective-permute-start(f32[72,128]{1,0:T(8,128)S(1)} %shard_map.107.a_ref), channel_id=1, source_target_pairs={{0,16},{4,20},{8,24},{12,28},{16,0},{20,4},{24,8},{28,12},{1,17},{... | collective-permute-start | bytes 110600 | tf_op jit(solution)/shard_map/ppermute | solution.py:311
  17.4 1.2 %collective-permute-start.3 = (f32[2,1024]{1,0:T(2,128)S(1)}, f32[2,1024]{1,0:T(2,128)S(1)}, u32[]{:S(2)}, u32[]{:S(2)}) collective-permute-start(f32[2,1024]{1,0:T(2,128)S(1)} %get-tuple-element.26), channel_id=1, source_target_pairs={{0,1},{1,0},{2,3},{3,2},{4,5},{5,4},{6,7},{7,6},{8,9},{9,8},{10,11... | collective-permute-start | bytes 24584 | tf_op jit(solution)/shard_map/ppermute | solution.py:311
  18.6 3.7 %collective-permute-start.4 = (f32[1,1024]{1,0:T(1,128)S(1)}, f32[1,1024]{1,0:T(1,128)S(1)}, u32[]{:S(2)}, u32[]{:S(2)}) collective-permute-start(f32[1,1024]{1,0:T(1,128)S(1)} %broadcast_select_fusion), channel_id=1, source_target_pairs={{0,2},{1,3},{2,0},{3,1},{4,6},{5,7},{6,4},{7,5},{8,10},{9,11},{10,... | collective-permute-start | bytes 12296 | tf_op jit(solution)/shard_map/ppermute | solution.py:311

commit v3 on v2

--- a/solution.py
+++ b/solution.py
@@ -7,8 +7,10 @@
 from jax.experimental.pallas import tpu as pltpu
 from jax.sharding import PartitionSpec as P
 
-NEG = -1e30
+NEG = -30000.0
 LANES = 128
+STATS = 16
+LN2 = 0.6931471805599453
 NT = (((1,), (1,)), ((), ()))
 NN = (((1,), (0,)), ((), ()))
 TN = (((0,), (0,)), ((), ()))
@@ -60,7 +62,7 @@
     len_hbm,
     code_hbm,
     cent_hbm,
-    msg_ref,
+    state_ref,
     q_ref,
     len_ref,
     code_ref,
@@ -146,57 +148,87 @@
             wide = jnp.where(
                 lane[:depth] < i * step * heads, wide, acc[i * depth : (i + 1) * depth]
             )
-        here = slice(c * lanes, (c + 1) * lanes)
-        msg_ref[0:depth, here] = wide
-        msg_ref[depth : depth + 8, here] = jnp.concatenate(
-            [top, total, jnp.zeros((6, lanes), jnp.float32)], axis=0
+        size = jnp.abs(v_ref[some].reshape(pairs * tokens, feat).astype(jnp.float32))
+        size = jnp.max(jnp.max(size, axis=0, keepdims=True), axis=1, keepdims=True)
+        scale = jnp.floor(jnp.log(jnp.maximum(size, 1e-30)) / LN2)
+        scale = jnp.where(total > 0.0, scale, -100.0)
+        state_ref[:, c * lanes : (c + 1) * lanes] = encode(
+            wide * jnp.exp(scale * -LN2), top, total, scale
         )
     for load in loads[5:]:
         load.wait()
 
 
+def terms(row):
+    out = []
+    for _ in range(3):
+        out.append(row.astype(jnp.bfloat16).astype(jnp.float32))
+        row = row - out[-1]
+    return out
+
+
+def encode(acc, top, total, scale):
+    rows = terms(top) + terms(total) + [scale]
+    rows.append(jnp.zeros((STATS - len(rows), acc.shape[1]), jnp.float32))
+    return jnp.concatenate([acc] + rows, axis=0)
+
+
+def decode(state):
+    depth = state.shape[0] - STATS
+    r = [state[depth + i : depth + i + 1] for i in range(7)]
+    return state[:depth], r[0] + r[1] + r[2], r[3] + r[4] + r[5], r[6]
+
+
 def merge(a, b):
-    depth = a.shape[0] - 8
-    top_a, top_b = a[depth : depth + 1], b[depth : depth + 1]
+    acc_a, top_a, total_a, scale_a = decode(a)
+    acc_b, top_b, total_b, scale_b = decode(b)
     top = jnp.maximum(top_a, top_b)
-    scale_a, scale_b = jnp.exp(top_a - top), jnp.exp(top_b - top)
-    acc = a[:depth] * scale_a + b[:depth] * scale_b
-    total = a[depth + 1 : depth + 2] * scale_a + b[depth + 1 : depth + 2] * scale_b
-    return acc, top, total
+    scale = jnp.maximum(scale_a, scale_b)
+    part_a, part_b = jnp.exp(top_a - top), jnp.exp(top_b - top)
+    acc = acc_a * (part_a * jnp.exp((scale_a - scale) * LN2))
+    acc = acc + acc_b * (part_b * jnp.exp((scale_b - scale) * LN2))
+    return acc, top, total_a * part_a + total_b * part_b, scale
 
 
 def merge_kernel(a_ref, b_ref, after, out_ref):
-    depth = a_ref.shape[0] - 8
-    acc, top, total = merge(a_ref[...], b_ref[...])
-    out_ref[0:depth, :] = acc
-    out_ref[depth : depth + 8, :] = jnp.concatenate(
-        [top, total, jnp.zeros((6, acc.shape[1]), jnp.float32)], axis=0
-    )
-
-
-def project_kernel(batch, kv, feat, a_ref, b_ref, w_ref, attended_ref, keep_ref, send_ref, x_ref, o_ref):
-    acc, _, total = merge(a_ref[...], b_ref[...])
-    out = acc / total
-    depth = out.shape[0]
+    out_ref[...] = encode(*merge(a_ref[...], b_ref[...]))
+
+
+def project_kernel(batch, kv, feat, a_ref, b_ref, w0_ref, w1_ref, w2_ref, att_ref, keep_ref, send_ref, x_ref, o_ref):
     heads = x_ref.shape[1] // feat
-    pack = feat // depth
     rows = batch * heads
-    tall = jnp.concatenate([out[:, i * rows : (i + 1) * rows] for i in range(pack)], axis=0)
+    group = heads // kv
+    acc, _, total, scale = merge(a_ref[...], b_ref[...])
+    out = acc * (jnp.exp(scale * LN2) / total)
+    pack = feat // out.shape[0]
+    tall = jnp.concatenate([out[:, p * rows : (p + 1) * rows] for p in range(pack)], axis=0)
     o_ref[...] = tall.T
     for q in range(heads):
         x_ref[:, q * feat : (q + 1) * feat] = o_ref[pl.ds(q, batch, stride=heads), :]
-    own = lax.axis_index("seq")
-    span = heads // kv * feat
-    start = pl.multiple_of((own % kv) * span, LANES)
-    attended_ref[0] = x_ref[pl.ds(own // kv, 1), pl.ds(start, span)].astype(jnp.bfloat16)
-    y = dot(x_ref[...].astype(jnp.bfloat16), w_ref[...])
+    att_ref[...] = o_ref[pl.ds(pl.multiple_of(lax.axis_index("seq") * group, group), group), :]
+    y, start = 0.0, 0
+    for w_ref in (w0_ref, w1_ref, w2_ref):
+        end = start + w_ref.shape[0]
+        y = y + dot(x_ref[:, start:end].astype(jnp.bfloat16), w_ref[...])
+        start = end
     parts = lax.axis_size("head")
     share = batch // parts
-    odd = lax.axis_index("head") % 2 == 1
-    even_rows = jnp.concatenate([y[i * share : (i + 1) * share] for i in range(0, parts, 2)], axis=0)
-    odd_rows = jnp.concatenate([y[i * share : (i + 1) * share] for i in range(1, parts, 2)], axis=0)
-    keep_ref[...] = jnp.where(odd, odd_rows, even_rows)
-    send_ref[...] = jnp.where(odd, even_rows, odd_rows)
+    me = lax.axis_index("head")
+
+    def rows_of(hop):
+        out = y[:share]
+        for i in range(1, parts):
+            out = jnp.where(me == i ^ hop, y[i * share : (i + 1) * share], out)
+        return out
+
+    keep_ref[...] = jnp.concatenate([rows_of(0), rows_of(3)], axis=0)
+    send_ref[...] = jnp.concatenate([rows_of(1), rows_of(2)], axis=0)
+
+
+def finish_kernel(a_ref, b_ref, att_ref, after, layer_ref, attended_ref):
+    layer_ref[...] = (a_ref[...] + b_ref[...]).astype(jnp.bfloat16)
+    parts = [att_ref[g : g + 1, :] for g in range(att_ref.shape[0])]
+    attended_ref[0] = jnp.concatenate(parts, axis=1).astype(jnp.bfloat16)
 
 
 def estimate_kernel(block, begin, end, q_ref, len_ref, code_ref, cent_ref, est_ref):
@@ -276,17 +308,31 @@
     chunks(begin, end, body)
 
 
-def first_kernel(block, end, q_ref, len_ref, code_ref, cent_ref, w_hbm, est_ref, w_ref, sem):
-    copy = pltpu.make_async_copy(w_hbm, w_ref, sem)
+def fetch(w_hbm, w_ref, start, sem):
+    return pltpu.make_async_copy(w_hbm.at[pl.ds(start, w_ref.shape[0])], w_ref, sem)
+
+
+def first_kernel(block, end, start, q_ref, len_ref, code_ref, cent_ref, w_hbm, est_ref, w_ref, sem):
+    copy = fetch(w_hbm, w_ref, start, sem)
     copy.start()
     estimate_kernel(block, 0, end, q_ref, len_ref, code_ref, cent_ref, est_ref)
     copy.wait()
 
 
-def second_kernel(block, begin, q_ref, len_ref, code_ref, cent_ref, part_ref, after, est_ref, token_ref):
-    token_ref[...] = jnp.zeros_like(token_ref)
+def second_kernel(
+    block, begin, start, q_ref, len_ref, code_ref, cent_ref, w_hbm, part_ref, after, est_ref, w_ref, sem
+):
+    copy = fetch(w_hbm, w_ref, start, sem)
+    copy.start()
     est_ref[0:begin] = part_ref[...]
     estimate_kernel(block, begin, code_ref.shape[0], q_ref, len_ref, code_ref, cent_ref, est_ref)
+    copy.wait()
+
+
+def third_kernel(start, w_hbm, after, w_ref, sem):
+    copy = fetch(w_hbm, w_ref, start, sem)
+    copy.start()
+    copy.wait()
 
 
 VMEM = pl.BlockSpec(memory_space=pltpu.VMEM)
@@ -306,27 +352,35 @@
     )(*[pltpu.with_memory_space_constraint(a, pltpu.HBM) if s is HBM else a for a, s in inputs])
 
 
-def swap(x, axis, hop):
-    size = lax.axis_size(axis)
-    return lax.ppermute(x, axis, [(i, i ^ hop) for i in range(size)])
+def move(x, seq_hop, head_hop):
+    seq, parts = lax.axis_size("seq"), lax.axis_size("head")
+    pairs = [
+        (s * parts + h, (s ^ seq_hop) * parts + (h ^ head_hop))
+        for s in range(seq)
+        for h in range(parts)
+    ]
+    return lax.ppermute(x, ("seq", "head"), pairs)
 
 
 def shards(queries, keys, values, codes, centroids, picks, block_len, out_weight):
     batch, kv, tokens, feat = keys.shape
     heads = queries.shape[1]
     rows = batch * heads
+    group = heads // kv
     blocks = block_len.shape[1]
     block = tokens // blocks
     width = out_weight.shape[1]
     seq, parts = lax.axis_size("seq"), lax.axis_size("head")
+    rounds = seq.bit_length() - 1
     pack = lane_plan(batch, heads)[1]
-    depth = feat // pack
-
-    state = jax.ShapeDtypeStruct((depth + 8, rows * pack), jnp.float32)
+    size = feat // pack + STATS
+    f32, f16 = jnp.float32, jnp.float16
+
     staged = (queries, block_len, codes, centroids)
-    message, *staged = call(
+    shape = jax.ShapeDtypeStruct((size, rows * pack), f32)
+    state, *staged = call(
         functools.partial(attend_kernel, block),
-        [(state, VMEM)] + [(jax.ShapeDtypeStruct(a.shape, a.dtype), VMEM) for a in staged],
+        [(shape, VMEM)] + [(jax.ShapeDtypeStruct(a.shape, a.dtype), VMEM) for a in staged],
         [(a, HBM) for a in (queries, keys, values, picks, block_len, codes, centroids)],
         scratch=[
             pltpu.VMEM(keys.shape, keys.dtype),
@@ -335,66 +389,70 @@
             pltpu.SemaphoreType.DMA((7,)),
         ],
     )
+    source = [(a, VMEM) for a in staged]
     half = batch // 2
-    source = [(a, VMEM) for a in staged]
-    part, weight = call(
-        functools.partial(first_kernel, block, half),
-        [
-            (jax.ShapeDtypeStruct((half, kv, blocks), jnp.float32), VMEM),
-            (jax.ShapeDtypeStruct(out_weight.shape, out_weight.dtype), VMEM),
-        ],
+    cuts = [heads * feat * i // 8 for i in (0, 3, 6, 8)]
+    slabs = [
+        (jax.ShapeDtypeStruct((b - a, width), out_weight.dtype), VMEM)
+        for a, b in zip(cuts, cuts[1:])
+    ]
+    sem = [pltpu.SemaphoreType.DMA]
+    part, *weights = call(
+        functools.partial(first_kernel, block, half, cuts[0]),
+        [(jax.ShapeDtypeStruct((half, kv, blocks), f32), VMEM), slabs[0]],
         source + [(out_weight, HBM)],
-        scratch=[pltpu.SemaphoreType.DMA],
+        scratch=sem,
         flops=500_000_000,
         data=1 << 22,
     )
-    received = swap(message, "seq", 1)
-    (message,) = call(
-        merge_kernel, [(state, VMEM)], [(message, VMEM), (received, VMEM), (part, ANY)]
-    )
-    estimates, token = call(
-        functools.partial(second_kernel, block, half),
-        [
-            (pltpu.VMEM((batch, kv, blocks), jnp.float32), VMEM),
-            (jax.ShapeDtypeStruct((8, LANES), jnp.float32), VMEM),
-        ],
-        source + [(part, VMEM), (message, ANY)],
+    after = part
+    for r in range(rounds):
+        hop = seq >> (r + 1)
+        message = state.astype(f16)
+        if r < rounds // 2 * 2:
+            far, near = move(message, hop, 1), move(message, 0, 1).astype(f32)
+        else:
+            far, near = move(message, hop, 0), state
+        far = far.astype(f32)
+        if r == rounds - 1:
+            break
+        (state,) = call(merge_kernel, [(shape, VMEM)], [(near, VMEM), (far, VMEM), (after, ANY)])
+        if r == 0:
+            estimates, after = call(
+                functools.partial(second_kernel, block, half, cuts[1]),
+                [(pltpu.VMEM((batch, kv, blocks), f32), VMEM), slabs[1]],
+                source + [(out_weight, HBM), (part, VMEM), (state, ANY)],
+                scratch=sem,
+                flops=500_000_000,
+                data=1 << 22,
+            )
+            weights.append(after)
+    weights += call(
+        functools.partial(third_kernel, cuts[2]),
+        [slabs[2]],
+        [(out_weight, HBM), (state, ANY)],
+        scratch=sem,
         flops=500_000_000,
         data=1 << 22,
     )
-    hop = 2
-    while hop < seq // 2:
-        received = swap(message, "seq", hop)
-        (message,) = call(
-            merge_kernel, [(state, VMEM)], [(message, VMEM), (received, VMEM), (token, ANY)]
-        )
-        hop *= 2
-    received = swap(message, "seq", hop)
-    sums = jax.ShapeDtypeStruct((batch // 2, width), jnp.float32)
+    sums = jax.ShapeDtypeStruct((half, width), f32)
     attended, keep, send = call(
         functools.partial(project_kernel, batch, kv, feat),
+        [(jax.ShapeDtypeStruct((group, feat), f32), VMEM), (sums, VMEM), (sums, VMEM)],
+        [(near, VMEM), (far, VMEM)] + [(w, VMEM) for w in weights],
+        scratch=[pltpu.VMEM((batch, heads * feat), f32), pltpu.VMEM((rows, feat), f32)],
+    )
+    total = keep + move(send, 0, 1)
+    own, send = total[: half // 2], total[half // 2 :]
+    layer_out, attended = call(
+        finish_kernel,
         [
-            (pltpu.VMEM((1, 1, heads // kv * feat), jnp.bfloat16), VMEM),
-            (sums, VMEM),
-            (sums, VMEM),
+            (jax.ShapeDtypeStruct((batch // parts, width), jnp.bfloat16), VMEM),
+            (jax.ShapeDtypeStruct((1, 1, group * feat), jnp.bfloat16), VMEM),
         ],
-        [(message, VMEM), (received, VMEM), (weight, VMEM)],
-        scratch=[
-            pltpu.VMEM((batch, heads * feat), jnp.float32),
-            pltpu.VMEM((rows, feat), jnp.float32),
-        ],
-    )
-    me = lax.axis_index("head")
-    total = keep + swap(send, "head", 1)
-    hop = 2
-    while hop < parts:
-        share = total.reshape(2, -1, width) if hop * 2 == parts else None
-        upper = (me // hop) % 2 == 1
-        total = jnp.where(upper, share[1], share[0]) + swap(
-            jnp.where(upper, share[0], share[1]), "head", hop
-        )
-        hop *= 2
-    return (estimates, attended, total.astype(jnp.bfloat16))
+        [(own, VMEM), (move(send, 0, 3), VMEM), (attended, VMEM), (after, ANY)],
+    )
+    return (estimates, attended, layer_out)
 
 
 def solution(mesh):

time: 23.1 us -> 21.4 us (0.926)
  waiting for transfers between devices: 4.69 us -> 3.5 us
  Pallas kernels: 6.14 us -> 7.31 us
  starting transfers between devices: 9.55 us -> 8.92 us
  local copies, waits for them, and re-layouts: 1.18 us -> 0.6 us
  other arithmetic: 0.62 us -> 0.06 us
    ppermute x5 -> x7, waiting for transfers between devices: 4.69 us -> 3.5 us  [move(): return lax.ppermute(x, ('seq', 'head'), pairs)]
    pallas_call x6 -> x8, Pallas kernels: 6.14 us -> 7.31 us  [call(): pl.pallas_call(kernel, out_shape=[shape for shape, _ in out], in_specs=[s...]
    ppermute x5 -> x7, starting transfers between devices: 9.55 us -> 8.92 us  [move(): return lax.ppermute(x, ('seq', 'head'), pairs)]
    unnamed x2 -> x1, local copies, waits for them, and re-layouts: 1.18 us -> 0.59 us
    convert_element_type x1 -> x8, other arithmetic: 0.6 us -> 0.05 us  [the longest x3 0.02 us: shards(): message = state.astype(f16)]
  transfers between devices with their start and end apart: 5 -> 7, of which waited for: 4 -> 4; matrix products, arithmetic and copies ran while one was open for 5% -> 3% of each run, Pallas kernels for 16% -> 19%
where the time goes in v3:
time: 21.4 us; the launch traced here: 21.1 us
  starting transfers between devices  8.92 us (42%)
  Pallas kernels  7.31 us (34%)
  waiting for transfers between devices  3.5 us (16%)
  between operations  0.75 us (4%)
  local copies, waits for them, and re-layouts  0.6 us (3%)
    ppermute x7, starting transfers between devices, move(): return lax.ppermute(x, ('seq', 'head'), pairs)  8.92 us
    pallas_call x8, Pallas kernels, call(): pl.pallas_call(kernel, out_shape=[shape for shape, _ in out], in_specs=[s...  7.31 us
    ppermute x7, waiting for transfers between devices, move(): return lax.ppermute(x, ('seq', 'head'), pairs)  3.5 us
    unnamed x1, local copies, waits for them, and re-layouts  0.59 us
  transfers between devices with their start and end apart: 7, of which 4 were waited for; matrix products, arithmetic and copies ran while one was open for 3% of the time, Pallas kernels for 19%

profile of v3, /device:TPU:0, one launch (start us, length us, event | category | flops | bytes accessed | tf_op | source)
XLA Modules:
  0.0 21.1 jit_solution(8564050121018350235)
XLA Ops:
  0.6 1.8 %shard_map.103 = (f32[80,128]{1,0:T(8,128)S(1)}, bf16[4,16,128]{2,1,0:T(8,128)(2,1)S(1)}, s32[4,8]{1,0:T(4,128)S(1)}, s32[4,2,32,128]{3,2,1,0:T(8,128)S(1)}, f32[2,4,32,256]{3,2,1,0:T(8,128)S(1)}) custom-call(bf16[4,16,128]{2,1,0:T(8,128)(2,1)} %q_hbm.1, bf16[4,2,128,128]{3,2,1,0:T(8,128)(2,1)} %k_hbm.1, bf16[4,2,128,128]{3,2,1,0:T(8,128)(2,1)} %v_hbm.1, ...), custom_call_target="tpu_custom_call" | custom-call | tf_op jit(solution)/shard_map/pallas_call | solution.py:344
  2.4 3.5 %collective-permute-start.1 = (f16[80,128]{1,0:T(8,128)(2,1)S(1)}, f16[80,128]{1,0:T(8,128)(2,1)S(1)}, u32[]{:S(2)}, u32[]{:S(2)}) collective-permute-start(f16[80,128]{1,0:T(8,128)(2,1)S(1)} %convert_element_type.24), channel_id=1, source_target_pairs={{0,17},{1,16},{2,19},{3,18},{4,21},{5,20},{6,23},{7,22},{8,25},{9,... | collective-permute-start | bytes 61448 | tf_op jit(solution)/shard_map/ppermute | solution.py:362
  5.9 0.7 %collective-permute-start = (f16[80,128]{1,0:T(8,128)(2,1)S(1)}, f16[80,128]{1,0:T(8,128)(2,1)S(1)}, u32[]{:S(2)}, u32[]{:S(2)}) collective-permute-start(f16[80,128]{1,0:T(8,128)(2,1)S(1)} %convert_element_type.24), channel_id=1, source_target_pairs={{0,1},{1,0},{2,3},{3,2},{4,5},{5,4},{6,7},{7,6},{8,9},{9,8},{10,11... | collective-permute-start | bytes 61448 | tf_op jit(solution)/shard_map/ppermute | solution.py:362
  6.6 1.4 %shard_map.104 = (f32[2,2,8]{2,1,0:T(2,128)S(1)}, bf16[768,1024]{1,0:T(8,128)(2,1)S(1)}) custom-call(bf16[4,16,128]{2,1,0:T(8,128)(2,1)S(1)} %get-tuple-element.17.q_ref, s32[4,8]{1,0:T(4,128)S(1)} %get-tuple-element.18.len_ref, s32[4,2,32,128]{3,2,1,0:T(8,128)S(1)} %get-tuple-element.19.code_ref, f32[2,4,32,256]{3,2,1,0:T(8,128)S(1)} %get-tuple-element.20.cent_ref, ...), custom_call_target="tpu_custom_call" | custom-call | flops 500000000 | bytes 4194304 | tf_op jit(solution)/shard_map/pallas_call | solution.py:344
  8.0 0.0 collective-permute-done.1
  8.1 0.0 collective-permute-done
  8.1 1.3 %collective-permute-start.3 = (f16[80,128]{1,0:T(8,128)(2,1)S(1)}, f16[80,128]{1,0:T(8,128)(2,1)S(1)}, u32[]{:S(2)}, u32[]{:S(2)}) collective-permute-start(f16[80,128]{1,0:T(8,128)(2,1)S(1)} %convert_element_type.27), channel_id=1, source_target_pairs={{0,9},{1,8},{2,11},{3,10},{4,13},{5,12},{6,15},{7,14},{8,1},{9,0},... | collective-permute-start | bytes 61448 | tf_op jit(solution)/shard_map/ppermute | solution.py:362
  9.5 0.4 %collective-permute-start.2 = (f16[80,128]{1,0:T(8,128)(2,1)S(1)}, f16[80,128]{1,0:T(8,128)(2,1)S(1)}, u32[]{:S(2)}, u32[]{:S(2)}) collective-permute-start(f16[80,128]{1,0:T(8,128)(2,1)S(1)} %convert_element_type.27), channel_id=1, source_target_pairs={{0,1},{1,0},{2,3},{3,2},{4,5},{5,4},{6,7},{7,6},{8,9},{9,8},{10,11... | collective-permute-start | bytes 61448 | tf_op jit(solution)/shard_map/ppermute | solution.py:362
  9.9 1.4 %shard_map.106 = (f32[4,2,8]{2,1,0:T(2,128)S(1)}, bf16[768,1024]{1,0:T(8,128)(2,1)S(1)}) custom-call(bf16[4,16,128]{2,1,0:T(8,128)(2,1)S(1)} %get-tuple-element.17.q_ref, s32[4,8]{1,0:T(4,128)S(1)} %get-tuple-element.18.len_ref, s32[4,2,32,128]{3,2,1,0:T(8,128)S(1)} %get-tuple-element.19.code_ref, f32[2,4,32,256]{3,2,1,0:T(8,128)S(1)} %get-tuple-element.20.cent_ref, ...), custom_call_target="tpu_custom_call" | custom-call | flops 500000000 | bytes 4194304 | tf_op jit(solution)/shard_map/pallas_call | solution.py:344
  11.3 0.1 collective-permute-done.3
  11.4 0.0 collective-permute-done.2
  11.5 1.6 %collective-permute-start.4 = (f16[80,128]{1,0:T(8,128)(2,1)S(1)}, f16[80,128]{1,0:T(8,128)(2,1)S(1)}, u32[]{:S(2)}, u32[]{:S(2)}) collective-permute-start(f16[80,128]{1,0:T(8,128)(2,1)S(1)} %convert_element_type.30), channel_id=1, source_target_pairs={{0,4},{1,5},{2,6},{3,7},{4,0},{5,1},{6,2},{7,3},{8,12},{9,13},{10,... | collective-permute-start | bytes 61448 | tf_op jit(solution)/shard_map/ppermute | solution.py:362
  13.1 1.2 %shard_map.108.w2_ref = bf16[512,1024]{1,0:T(8,128)(2,1)S(1)} custom-call(bf16[2048,1024]{1,0:T(8,128)(2,1)} %w_hbm.5, f32[80,128]{1,0:T(8,128)S(1)} %shard_map.107.after.a_ref), custom_call_target="tpu_custom_call" | custom-call | flops 500000000 | bytes 4194304 | tf_op jit(solution)/shard_map/pallas_call | solution.py:344
  14.3 1.0 %collective-permute-done.4 = f16[80,128]{1,0:T(8,128)(2,1)S(1)} collective-permute-done((f16[80,128]{1,0:T(8,128)(2,1)S(1)}, f16[80,128]{1,0:T(8,128)(2,1)S(1)}, u32[]{:S(2)}, u32[]{:S(2)}) %collective-permute-start.4) | collective-permute-done | bytes 20512 | tf_op jit(solution)/shard_map/ppermute | solution.py:362
  15.4 0.8 %shard_map.109 = (f32[8,128]{1,0:T(8,128)S(1)}, f32[2,1024]{1,0:T(2,128)S(1)}, f32[2,1024]{1,0:T(2,128)S(1)}) custom-call(f32[80,128]{1,0:T(8,128)S(1)} %shard_map.107.after.a_ref, f32[80,128]{1,0:T(8,128)S(1)} %convert_element_type.31.b_ref, bf16[768,1024]{1,0:T(8,128)(2,1)S(1)} %get-tuple-element.25.w0_ref, ...), custom_call_target="tpu_custom_call" | custom-call | tf_op jit(solution)/shard_map/pallas_call | solution.py:344
  16.2 0.1 collective-permute-start.5
  16.3 1.2 %collective-permute-done.5 = f32[2,1024]{1,0:T(2,128)S(1)} collective-permute-done((f32[2,1024]{1,0:T(2,128)S(1)}, f32[2,1024]{1,0:T(2,128)S(1)}, u32[]{:S(2)}, u32[]{:S(2)}) %collective-permute-start.5) | collective-permute-done | bytes 8224 | tf_op jit(solution)/shard_map/ppermute | solution.py:362
  17.4 1.3 %collective-permute-start.6 = (f32[1,1024]{1,0:T(1,128)S(1)}, f32[1,1024]{1,0:T(1,128)S(1)}, u32[]{:S(2)}, u32[]{:S(2)}) collective-permute-start(f32[1,1024]{1,0:T(1,128)S(1)} %get-tuple-element.31), channel_id=1, source_target_pairs={{0,3},{1,2},{2,1},{3,0},{4,7},{5,6},{6,5},{7,4},{8,11},{9,10},{10,... | collective-permute-start | bytes 12296 | tf_op jit(solution)/shard_map/ppermute | solution.py:362
  18.8 0.6 %copy.11 = f32[4,2,8]{2,1,0:T(2,128)} copy(f32[4,2,8]{2,1,0:T(2,128)S(1)} %get-tuple-element.33) | data formatting | bytes 512
  19.3 1.2 %collective-permute-done.6.b_ref = f32[1,1024]{1,0:T(1,128)S(1)} collective-permute-done((f32[1,1024]{1,0:T(1,128)S(1)}, f32[1,1024]{1,0:T(1,128)S(1)}, u32[]{:S(2)}, u32[]{:S(2)}) %collective-permute-start.6) | collective-permute-done | bytes 4128 | tf_op jit(solution)/shard_map/ppermute | solution.py:362
  20.5 0.6 %shard_map.110 = (bf16[1,1024]{1,0:T(2,128)(2,1)}, bf16[1,1,1024]{2,1,0:T(2,128)(2,1)}) custom-call(f32[1,1024]{1,0:T(1,128)S(1)} %get-tuple-element.32.a_ref, f32[1,1024]{1,0:T(1,128)S(1)} %collective-permute-done.6.b_ref, f32[8,128]{1,0:T(8,128)S(1)} %get-tuple-element.28.att_ref, bf16[768,1024]{1,0:T(8,128)(2,1)S(1)} %get-tuple-element.24.after.w1_ref), custom_call_target="tpu_custom_call" | custom-call | tf_op jit(solution)/shard_map/pallas_call | solution.py:344
  (12 shorter events, 0.1 us)
Async XLA Ops:
  2.4 5.6 %collective-permute-start.1 = (f16[80,128]{1,0:T(8,128)(2,1)S(1)}, f16[80,128]{1,0:T(8,128)(2,1)S(1)}, u32[]{:S(2)}, u32[]{:S(2)}) collective-permute-start(f16[80,128]{1,0:T(8,128)(2,1)S(1)} %convert_element_type.24), channel_id=1, source_target_pairs={{0,17},{1,16},{2,19},{3,18},{4,21},{5,20},{6,23},{7,22},{8,25},{9,... | collective-permute-start | bytes 61448 | tf_op jit(solution)/shard_map/ppermute | solution.py:362
  5.9 2.1 %collective-permute-start = (f16[80,128]{1,0:T(8,128)(2,1)S(1)}, f16[80,128]{1,0:T(8,128)(2,1)S(1)}, u32[]{:S(2)}, u32[]{:S(2)}) collective-permute-start(f16[80,128]{1,0:T(8,128)(2,1)S(1)} %convert_element_type.24), channel_id=1, source_target_pairs={{0,1},{1,0},{2,3},{3,2},{4,5},{5,4},{6,7},{7,6},{8,9},{9,8},{10,11... | collective-permute-start | bytes 61448 | tf_op jit(solution)/shard_map/ppermute | solution.py:362
  8.1 3.3 %collective-permute-start.3 = (f16[80,128]{1,0:T(8,128)(2,1)S(1)}, f16[80,128]{1,0:T(8,128)(2,1)S(1)}, u32[]{:S(2)}, u32[]{:S(2)}) collective-permute-start(f16[80,128]{1,0:T(8,128)(2,1)S(1)} %convert_element_type.27), channel_id=1, source_target_pairs={{0,9},{1,8},{2,11},{3,10},{4,13},{5,12},{6,15},{7,14},{8,1},{9,0},... | collective-permute-start | bytes 61448 | tf_op jit(solution)/shard_map/ppermute | solution.py:362
  9.5 2.0 %collective-permute-start.2 = (f16[80,128]{1,0:T(8,128)(2,1)S(1)}, f16[80,128]{1,0:T(8,128)(2,1)S(1)}, u32[]{:S(2)}, u32[]{:S(2)}) collective-permute-start(f16[80,128]{1,0:T(8,128)(2,1)S(1)} %convert_element_type.27), channel_id=1, source_target_pairs={{0,1},{1,0},{2,3},{3,2},{4,5},{5,4},{6,7},{7,6},{8,9},{9,8},{10,11... | collective-permute-start | bytes 61448 | tf_op jit(solution)/shard_map/ppermute | solution.py:362
  11.5 3.8 %collective-permute-start.4 = (f16[80,128]{1,0:T(8,128)(2,1)S(1)}, f16[80,128]{1,0:T(8,128)(2,1)S(1)}, u32[]{:S(2)}, u32[]{:S(2)}) collective-permute-start(f16[80,128]{1,0:T(8,128)(2,1)S(1)} %convert_element_type.30), channel_id=1, source_target_pairs={{0,4},{1,5},{2,6},{3,7},{4,0},{5,1},{6,2},{7,3},{8,12},{9,13},{10,... | collective-permute-start | bytes 61448 | tf_op jit(solution)/shard_map/ppermute | solution.py:362
  16.2 1.2 %collective-permute-start.5 = (f32[2,1024]{1,0:T(2,128)S(1)}, f32[2,1024]{1,0:T(2,128)S(1)}, u32[]{:S(2)}, u32[]{:S(2)}) collective-permute-start(f32[2,1024]{1,0:T(2,128)S(1)} %get-tuple-element.27), channel_id=1, source_target_pairs={{0,1},{1,0},{2,3},{3,2},{4,5},{5,4},{6,7},{7,6},{8,9},{9,8},{10,11... | collective-permute-start | bytes 24584 | tf_op jit(solution)/shard_map/ppermute | solution.py:362
  17.4 3.1 %collective-permute-start.6 = (f32[1,1024]{1,0:T(1,128)S(1)}, f32[1,1024]{1,0:T(1,128)S(1)}, u32[]{:S(2)}, u32[]{:S(2)}) collective-permute-start(f32[1,1024]{1,0:T(1,128)S(1)} %get-tuple-element.31), channel_id=1, source_target_pairs={{0,3},{1,2},{2,1},{3,0},{4,7},{5,6},{6,5},{7,4},{8,11},{9,10},{10,... | collective-permute-start | bytes 12296 | tf_op jit(solution)/shard_map/ppermute | solution.py:362

commit v4 on v3

--- a/solution.py
+++ b/solution.py
@@ -103,11 +103,12 @@
         lax.broadcasted_iota(jnp.int32, (pairs, lanes), 0) == owner[:pairs], 1.0, 0.0
     )
 
-    def own(x, size):
-        kept = x[:size]
-        for p in range(1, pairs):
-            kept = jnp.where(owner[:size] == p, x[p * size : (p + 1) * size], kept)
-        return kept
+    of_row = lax.broadcasted_iota(jnp.int32, (lanes, feat), 0) % (step * heads) // group
+
+    def spread(x):
+        return jnp.concatenate(
+            [jnp.where(owner == p, x, jnp.zeros_like(x)) for p in range(pairs)], axis=0
+        )
 
     for load in loads[:3]:
         load.wait()
@@ -128,7 +129,11 @@
         some = pl.ds(first, step)
         query = q_ref[some].reshape(step * heads, feat)
         query = jnp.concatenate([query] * copies, axis=0)
-        score = own(dot(k_ref[some].reshape(pairs * tokens, feat), query, NT), tokens)
+        query = jnp.concatenate(
+            [jnp.where(of_row == p, query, jnp.zeros_like(query)) for p in range(pairs)], axis=1
+        )
+        keys = jnp.concatenate([k_ref[first + p // kv, p % kv] for p in range(pairs)], axis=1)
+        score = dot(keys, query, NT)
         if first == 0:
             loads[4].wait()
         on = jnp.concatenate([place < limits[c][j : j + 1] for j in range(blocks)], axis=0)
@@ -137,12 +142,14 @@
         weight = jnp.where(on, jnp.exp(score - top), 0.0)
         total = jnp.sum(weight, axis=0, keepdims=True)
         turned = jnp.concatenate(
-            [v_ref[first + p // kv, p % kv].T for p in range(pairs)], axis=0
-        )
-        acc = dot(
-            jnp.concatenate([turned, turned], axis=1), jnp.concatenate(split(weight), axis=0)
-        )
-        acc = own(acc, feat)
+            [v_ref[first + p // kv, p % kv].T for p in range(pairs)], axis=1
+        )
+        high, low = split(weight)
+        if copies == 2:
+            acc = dot(turned, spread(jnp.where(lane < lanes // 2, high, low)))
+            acc = acc + pltpu.roll(acc, lanes // 2, 1)
+        else:
+            acc = dot(turned, spread(high)) + dot(turned, spread(low))
         wide = acc[:depth]
         for i in range(1, copies):
             wide = jnp.where(
@@ -179,26 +186,30 @@
     return state[:depth], r[0] + r[1] + r[2], r[3] + r[4] + r[5], r[6]
 
 
-def merge(a, b):
-    acc_a, top_a, total_a, scale_a = decode(a)
-    acc_b, top_b, total_b, scale_b = decode(b)
-    top = jnp.maximum(top_a, top_b)
-    scale = jnp.maximum(scale_a, scale_b)
-    part_a, part_b = jnp.exp(top_a - top), jnp.exp(top_b - top)
-    acc = acc_a * (part_a * jnp.exp((scale_a - scale) * LN2))
-    acc = acc + acc_b * (part_b * jnp.exp((scale_b - scale) * LN2))
-    return acc, top, total_a * part_a + total_b * part_b, scale
-
-
-def merge_kernel(a_ref, b_ref, after, out_ref):
-    out_ref[...] = encode(*merge(a_ref[...], b_ref[...]))
-
-
-def project_kernel(batch, kv, feat, a_ref, b_ref, w0_ref, w1_ref, w2_ref, att_ref, keep_ref, send_ref, x_ref, o_ref):
+def merge(states):
+    parts = [decode(state) for state in states]
+    top = functools.reduce(jnp.maximum, [p[1] for p in parts])
+    scale = functools.reduce(jnp.maximum, [p[3] for p in parts])
+    acc = total = 0.0
+    for part_acc, part_top, part_total, part_scale in parts:
+        weight = jnp.exp(part_top - top)
+        acc = acc + part_acc * (weight * jnp.exp((part_scale - scale) * LN2))
+        total = total + part_total * weight
+    return acc, top, total, scale
+
+
+def merge_kernel(*refs):
+    *state_refs, after, out_ref = refs
+    out_ref[...] = encode(*merge([ref[...] for ref in state_refs]))
+
+
+def project_kernel(batch, kv, feat, count, *refs):
+    state_refs, refs = refs[:count], refs[count:]
+    w0_ref, w1_ref, att_ref, keep_ref, send_ref, x_ref, o_ref = refs
     heads = x_ref.shape[1] // feat
     rows = batch * heads
     group = heads // kv
-    acc, _, total, scale = merge(a_ref[...], b_ref[...])
+    acc, _, total, scale = merge([ref[...] for ref in state_refs])
     out = acc * (jnp.exp(scale * LN2) / total)
     pack = feat // out.shape[0]
     tall = jnp.concatenate([out[:, p * rows : (p + 1) * rows] for p in range(pack)], axis=0)
@@ -207,7 +218,7 @@
         x_ref[:, q * feat : (q + 1) * feat] = o_ref[pl.ds(q, batch, stride=heads), :]
     att_ref[...] = o_ref[pl.ds(pl.multiple_of(lax.axis_index("seq") * group, group), group), :]
     y, start = 0.0, 0
-    for w_ref in (w0_ref, w1_ref, w2_ref):
+    for w_ref in (w0_ref, w1_ref):
         end = start + w_ref.shape[0]
         y = y + dot(x_ref[:, start:end].astype(jnp.bfloat16), w_ref[...])
         start = end
@@ -329,12 +340,6 @@
     copy.wait()
 
 
-def third_kernel(start, w_hbm, after, w_ref, sem):
-    copy = fetch(w_hbm, w_ref, start, sem)
-    copy.start()
-    copy.wait()
-
-
 VMEM = pl.BlockSpec(memory_space=pltpu.VMEM)
 ANY = pl.BlockSpec(memory_space=pl.ANY)
 HBM = pl.BlockSpec(memory_space=pltpu.HBM)
@@ -391,7 +396,7 @@
     )
     source = [(a, VMEM) for a in staged]
     half = batch // 2
-    cuts = [heads * feat * i // 8 for i in (0, 3, 6, 8)]
+    cuts = [heads * feat * i // 2 for i in (0, 1, 2)]
     slabs = [
         (jax.ShapeDtypeStruct((b - a, width), out_weight.dtype), VMEM)
         for a, b in zip(cuts, cuts[1:])
@@ -406,17 +411,17 @@
         data=1 << 22,
     )
     after = part
-    for r in range(rounds):
-        hop = seq >> (r + 1)
+    phases = [[1 << i] for i in range(2, rounds)] + [[1, 2, 3]]
+    for r, hops in enumerate(phases):
         message = state.astype(f16)
-        if r < rounds // 2 * 2:
-            far, near = move(message, hop, 1), move(message, 0, 1).astype(f32)
-        else:
-            far, near = move(message, hop, 0), state
-        far = far.astype(f32)
-        if r == rounds - 1:
+        crossed = int(r < len(phases) // 2 * 2)
+        states = [move(message, hop, crossed).astype(f32) for hop in hops[::-1]]
+        states.append(move(message, 0, 1).astype(f32) if crossed else state)
+        if r == len(phases) - 1:
             break
-        (state,) = call(merge_kernel, [(shape, VMEM)], [(near, VMEM), (far, VMEM), (after, ANY)])
+        (state,) = call(
+            merge_kernel, [(shape, VMEM)], [(a, VMEM) for a in states] + [(after, ANY)]
+        )
         if r == 0:
             estimates, after = call(
                 functools.partial(second_kernel, block, half, cuts[1]),
@@ -427,19 +432,11 @@
                 data=1 << 22,
             )
             weights.append(after)
-    weights += call(
-        functools.partial(third_kernel, cuts[2]),
-        [slabs[2]],
-        [(out_weight, HBM), (state, ANY)],
-        scratch=sem,
-        flops=500_000_000,
-        data=1 << 22,
-    )
     sums = jax.ShapeDtypeStruct((half, width), f32)
     attended, keep, send = call(
-        functools.partial(project_kernel, batch, kv, feat),
+        functools.partial(project_kernel, batch, kv, feat, len(states)),
         [(jax.ShapeDtypeStruct((group, feat), f32), VMEM), (sums, VMEM), (sums, VMEM)],
-        [(near, VMEM), (far, VMEM)] + [(w, VMEM) for w in weights],
+        [(a, VMEM) for a in states + weights],
         scratch=[pltpu.VMEM((batch, heads * feat), f32), pltpu.VMEM((rows, feat), f32)],
     )
     total = keep + move(send, 0, 1)

time: 21.4 us -> 20.4 us (0.953)
  Pallas kernels: 7.31 us -> 6.42 us
  waiting for transfers between devices: 3.5 us -> 3.18 us
  starting transfers between devices: 8.92 us -> 9.15 us
    pallas_call x8 -> x6, Pallas kernels: 7.31 us -> 6.42 us  [call(): pl.pallas_call(kernel, out_shape=[shape for shape, _ in out], in_specs=[s...]
    ppermute x7 -> x8, waiting for transfers between devices: 3.5 us -> 3.18 us  [move(): return lax.ppermute(x, ('seq', 'head'), pairs)]
    ppermute x7 -> x8, starting transfers between devices: 8.92 us -> 9.15 us  [move(): return lax.ppermute(x, ('seq', 'head'), pairs)]
  transfers between devices with their start and end apart: 7 -> 8, of which waited for: 4 -> 4; matrix products, arithmetic and copies ran while one was open for 3% -> 3% of each run, Pallas kernels for 19% -> 16%
where the time goes in v4:
time: 20.4 us; the launch traced here: 20.2 us
  starting transfers between devices  9.15 us (45%)
  Pallas kernels  6.42 us (31%)
  waiting for transfers between devices  3.18 us (16%)
  between operations  0.75 us (4%)
  local copies, waits for them, and re-layouts  0.6 us (3%)
    ppermute x8, starting transfers between devices, move(): return lax.ppermute(x, ('seq', 'head'), pairs)  9.15 us
    pallas_call x6, Pallas kernels, call(): pl.pallas_call(kernel, out_shape=[shape for shape, _ in out], in_specs=[s...  6.42 us
    ppermute x8, waiting for transfers between devices, move(): return lax.ppermute(x, ('seq', 'head'), pairs)  3.18 us
    unnamed x1, local copies, waits for them, and re-layouts  0.59 us
  transfers between devices with their start and end apart: 8, of which 4 were waited for; matrix products, arithmetic and copies ran while one was open for 3% of the time, Pallas kernels for 16%

profile of v4, /device:TPU:0, one launch (start us, length us, event | category | flops | bytes accessed | tf_op | source)
XLA Modules:
  0.0 20.2 jit_solution(13022607855671027389)
XLA Ops:
  0.6 1.7 %shard_map.103 = (f32[80,128]{1,0:T(8,128)S(1)}, bf16[4,16,128]{2,1,0:T(8,128)(2,1)S(1)}, s32[4,8]{1,0:T(4,128)S(1)}, s32[4,2,32,128]{3,2,1,0:T(8,128)S(1)}, f32[2,4,32,256]{3,2,1,0:T(8,128)S(1)}) custom-call(bf16[4,16,128]{2,1,0:T(8,128)(2,1)} %q_hbm.1, bf16[4,2,128,128]{3,2,1,0:T(8,128)(2,1)} %k_hbm.1, bf16[4,2,128,128]{3,2,1,0:T(8,128)(2,1)} %v_hbm.1, ...), custom_call_target="tpu_custom_call" | custom-call | tf_op jit(solution)/shard_map/pallas_call | solution.py:349
  2.4 3.5 %collective-permute-start = (f16[80,128]{1,0:T(8,128)(2,1)S(1)}, f16[80,128]{1,0:T(8,128)(2,1)S(1)}, u32[]{:S(2)}, u32[]{:S(2)}) collective-permute-start(f16[80,128]{1,0:T(8,128)(2,1)S(1)} %convert_element_type.24), channel_id=1, source_target_pairs={{0,17},{1,16},{2,19},{3,18},{4,21},{5,20},{6,23},{7,22},{8,25},{9,... | collective-permute-start | bytes 61448 | tf_op jit(solution)/shard_map/ppermute | solution.py:367
  5.9 0.7 %collective-permute-start.1 = (f16[80,128]{1,0:T(8,128)(2,1)S(1)}, f16[80,128]{1,0:T(8,128)(2,1)S(1)}, u32[]{:S(2)}, u32[]{:S(2)}) collective-permute-start(f16[80,128]{1,0:T(8,128)(2,1)S(1)} %convert_element_type.24), channel_id=1, source_target_pairs={{0,1},{1,0},{2,3},{3,2},{4,5},{5,4},{6,7},{7,6},{8,9},{9,8},{10,11... | collective-permute-start | bytes 61448 | tf_op jit(solution)/shard_map/ppermute | solution.py:367
  6.6 1.6 %shard_map.104 = (f32[2,2,8]{2,1,0:T(2,128)S(1)}, bf16[1024,1024]{1,0:T(8,128)(2,1)S(1)}) custom-call(bf16[4,16,128]{2,1,0:T(8,128)(2,1)S(1)} %get-tuple-element.17.q_ref, s32[4,8]{1,0:T(4,128)S(1)} %get-tuple-element.18.len_ref, s32[4,2,32,128]{3,2,1,0:T(8,128)S(1)} %get-tuple-element.19.code_ref, f32[2,4,32,256]{3,2,1,0:T(8,128)S(1)} %get-tuple-element.20.cent_ref, ...), custom_call_target="tpu_custom_call" | custom-call | flops 500000000 | bytes 4194304 | tf_op jit(solution)/shard_map/pallas_call | solution.py:349
  8.2 0.0 collective-permute-done
  8.3 0.0 collective-permute-done.1
  8.3 2.2 %collective-permute-start.2 = (f16[80,128]{1,0:T(8,128)(2,1)S(1)}, f16[80,128]{1,0:T(8,128)(2,1)S(1)}, u32[]{:S(2)}, u32[]{:S(2)}) collective-permute-start(f16[80,128]{1,0:T(8,128)(2,1)S(1)} %convert_element_type.27), channel_id=1, source_target_pairs={{0,13},{1,12},{2,15},{3,14},{4,9},{5,8},{6,11},{7,10},{8,5},{9,4},... | collective-permute-start | bytes 61448 | tf_op jit(solution)/shard_map/ppermute | solution.py:367
  10.5 0.6 %collective-permute-start.3 = (f16[80,128]{1,0:T(8,128)(2,1)S(1)}, f16[80,128]{1,0:T(8,128)(2,1)S(1)}, u32[]{:S(2)}, u32[]{:S(2)}) collective-permute-start(f16[80,128]{1,0:T(8,128)(2,1)S(1)} %convert_element_type.27), channel_id=1, source_target_pairs={{0,9},{1,8},{2,11},{3,10},{4,13},{5,12},{6,15},{7,14},{8,1},{9,0},... | collective-permute-start | bytes 61448 | tf_op jit(solution)/shard_map/ppermute | solution.py:367
  11.1 0.2 collective-permute-start.4
  11.3 0.4 %collective-permute-start.5 = (f16[80,128]{1,0:T(8,128)(2,1)S(1)}, f16[80,128]{1,0:T(8,128)(2,1)S(1)}, u32[]{:S(2)}, u32[]{:S(2)}) collective-permute-start(f16[80,128]{1,0:T(8,128)(2,1)S(1)} %convert_element_type.27), channel_id=1, source_target_pairs={{0,1},{1,0},{2,3},{3,2},{4,5},{5,4},{6,7},{7,6},{8,9},{9,8},{10,11... | collective-permute-start | bytes 61448 | tf_op jit(solution)/shard_map/ppermute | solution.py:367
  11.7 1.6 %shard_map.106 = (f32[4,2,8]{2,1,0:T(2,128)S(1)}, bf16[1024,1024]{1,0:T(8,128)(2,1)S(1)}) custom-call(bf16[4,16,128]{2,1,0:T(8,128)(2,1)S(1)} %get-tuple-element.17.q_ref, s32[4,8]{1,0:T(4,128)S(1)} %get-tuple-element.18.len_ref, s32[4,2,32,128]{3,2,1,0:T(8,128)S(1)} %get-tuple-element.19.code_ref, f32[2,4,32,256]{3,2,1,0:T(8,128)S(1)} %get-tuple-element.20.cent_ref, ...), custom_call_target="tpu_custom_call" | custom-call | flops 500000000 | bytes 4194304 | tf_op jit(solution)/shard_map/pallas_call | solution.py:349
  13.3 0.0 collective-permute-done.2
  13.4 0.4 %collective-permute-done.3 = f16[80,128]{1,0:T(8,128)(2,1)S(1)} collective-permute-done((f16[80,128]{1,0:T(8,128)(2,1)S(1)}, f16[80,128]{1,0:T(8,128)(2,1)S(1)}, u32[]{:S(2)}, u32[]{:S(2)}) %collective-permute-start.3) | collective-permute-done | bytes 20512 | tf_op jit(solution)/shard_map/ppermute | solution.py:367
  13.7 0.6 %collective-permute-done.4 = f16[80,128]{1,0:T(8,128)(2,1)S(1)} collective-permute-done((f16[80,128]{1,0:T(8,128)(2,1)S(1)}, f16[80,128]{1,0:T(8,128)(2,1)S(1)}, u32[]{:S(2)}, u32[]{:S(2)}) %collective-permute-start.4) | collective-permute-done | bytes 20512 | tf_op jit(solution)/shard_map/ppermute | solution.py:367
  14.3 0.0 collective-permute-done.5
  14.4 0.8 %shard_map.107 = (f32[8,128]{1,0:T(8,128)S(1)}, f32[2,1024]{1,0:T(2,128)S(1)}, f32[2,1024]{1,0:T(2,128)S(1)}) custom-call(f32[80,128]{1,0:T(8,128)S(1)} %convert_element_type.28.refs_0_, f32[80,128]{1,0:T(8,128)S(1)} %convert_element_type.29.refs_1_, f32[80,128]{1,0:T(8,128)S(1)} %convert_element_type.30.refs_2_, ...), custom_call_target="tpu_custom_call" | custom-call | tf_op jit(solution)/shard_map/pallas_call | solution.py:349
  15.2 0.2 %collective-permute-start.6 = (f32[2,1024]{1,0:T(2,128)S(1)}, f32[2,1024]{1,0:T(2,128)S(1)}, u32[]{:S(2)}, u32[]{:S(2)}) collective-permute-start(f32[2,1024]{1,0:T(2,128)S(1)} %get-tuple-element.27), channel_id=1, source_target_pairs={{0,1},{1,0},{2,3},{3,2},{4,5},{5,4},{6,7},{7,6},{8,9},{9,8},{10,11... | collective-permute-start | bytes 24584 | tf_op jit(solution)/shard_map/ppermute | solution.py:367
  15.4 1.0 %collective-permute-done.6 = f32[2,1024]{1,0:T(2,128)S(1)} collective-permute-done((f32[2,1024]{1,0:T(2,128)S(1)}, f32[2,1024]{1,0:T(2,128)S(1)}, u32[]{:S(2)}, u32[]{:S(2)}) %collective-permute-start.6) | collective-permute-done | bytes 8224 | tf_op jit(solution)/shard_map/ppermute | solution.py:367
  16.4 1.3 %collective-permute-start.7 = (f32[1,1024]{1,0:T(1,128)S(1)}, f32[1,1024]{1,0:T(1,128)S(1)}, u32[]{:S(2)}, u32[]{:S(2)}) collective-permute-start(f32[1,1024]{1,0:T(1,128)S(1)} %get-tuple-element.31), channel_id=1, source_target_pairs={{0,3},{1,2},{2,1},{3,0},{4,7},{5,6},{6,5},{7,4},{8,11},{9,10},{10,... | collective-permute-start | bytes 12296 | tf_op jit(solution)/shard_map/ppermute | solution.py:367
  17.8 0.6 %copy.11 = f32[4,2,8]{2,1,0:T(2,128)} copy(f32[4,2,8]{2,1,0:T(2,128)S(1)} %get-tuple-element.33) | data formatting | bytes 512
  18.4 1.2 %collective-permute-done.7.b_ref = f32[1,1024]{1,0:T(1,128)S(1)} collective-permute-done((f32[1,1024]{1,0:T(1,128)S(1)}, f32[1,1024]{1,0:T(1,128)S(1)}, u32[]{:S(2)}, u32[]{:S(2)}) %collective-permute-start.7) | collective-permute-done | bytes 4128 | tf_op jit(solution)/shard_map/ppermute | solution.py:367
  19.5 0.6 %shard_map.108 = (bf16[1,1024]{1,0:T(2,128)(2,1)}, bf16[1,1,1024]{2,1,0:T(2,128)(2,1)}) custom-call(f32[1,1024]{1,0:T(1,128)S(1)} %get-tuple-element.32.a_ref, f32[1,1024]{1,0:T(1,128)S(1)} %collective-permute-done.7.b_ref, f32[8,128]{1,0:T(8,128)S(1)} %get-tuple-element.28.att_ref, bf16[1024,1024]{1,0:T(8,128)(2,1)S(1)} %get-tuple-element.25.refs_5_.after), custom_call_target="tpu_custom_call" | custom-call | tf_op jit(solution)/shard_map/pallas_call | solution.py:349
  (11 shorter events, 0.1 us)
Async XLA Ops:
  2.4 5.8 %collective-permute-start = (f16[80,128]{1,0:T(8,128)(2,1)S(1)}, f16[80,128]{1,0:T(8,128)(2,1)S(1)}, u32[]{:S(2)}, u32[]{:S(2)}) collective-permute-start(f16[80,128]{1,0:T(8,128)(2,1)S(1)} %convert_element_type.24), channel_id=1, source_target_pairs={{0,17},{1,16},{2,19},{3,18},{4,21},{5,20},{6,23},{7,22},{8,25},{9,... | collective-permute-start | bytes 61448 | tf_op jit(solution)/shard_map/ppermute | solution.py:367
  5.9 2.3 %collective-permute-start.1 = (f16[80,128]{1,0:T(8,128)(2,1)S(1)}, f16[80,128]{1,0:T(8,128)(2,1)S(1)}, u32[]{:S(2)}, u32[]{:S(2)}) collective-permute-start(f16[80,128]{1,0:T(8,128)(2,1)S(1)} %convert_element_type.24), channel_id=1, source_target_pairs={{0,1},{1,0},{2,3},{3,2},{4,5},{5,4},{6,7},{7,6},{8,9},{9,8},{10,11... | collective-permute-start | bytes 61448 | tf_op jit(solution)/shard_map/ppermute | solution.py:367
  8.3 5.0 %collective-permute-start.2 = (f16[80,128]{1,0:T(8,128)(2,1)S(1)}, f16[80,128]{1,0:T(8,128)(2,1)S(1)}, u32[]{:S(2)}, u32[]{:S(2)}) collective-permute-start(f16[80,128]{1,0:T(8,128)(2,1)S(1)} %convert_element_type.27), channel_id=1, source_target_pairs={{0,13},{1,12},{2,15},{3,14},{4,9},{5,8},{6,11},{7,10},{8,5},{9,4},... | collective-permute-start | bytes 61448 | tf_op jit(solution)/shard_map/ppermute | solution.py:367
  10.5 3.2 %collective-permute-start.3 = (f16[80,128]{1,0:T(8,128)(2,1)S(1)}, f16[80,128]{1,0:T(8,128)(2,1)S(1)}, u32[]{:S(2)}, u32[]{:S(2)}) collective-permute-start(f16[80,128]{1,0:T(8,128)(2,1)S(1)} %convert_element_type.27), channel_id=1, source_target_pairs={{0,9},{1,8},{2,11},{3,10},{4,13},{5,12},{6,15},{7,14},{8,1},{9,0},... | collective-permute-start | bytes 61448 | tf_op jit(solution)/shard_map/ppermute | solution.py:367
  11.1 3.2 %collective-permute-start.4 = (f16[80,128]{1,0:T(8,128)(2,1)S(1)}, f16[80,128]{1,0:T(8,128)(2,1)S(1)}, u32[]{:S(2)}, u32[]{:S(2)}) collective-permute-start(f16[80,128]{1,0:T(8,128)(2,1)S(1)} %convert_element_type.27), channel_id=1, source_target_pairs={{0,5},{1,4},{2,7},{3,6},{4,1},{5,0},{6,3},{7,2},{8,13},{9,12},{10,... | collective-permute-start | bytes 61448 | tf_op jit(solution)/shard_map/ppermute | solution.py:367
  11.3 3.1 %collective-permute-start.5 = (f16[80,128]{1,0:T(8,128)(2,1)S(1)}, f16[80,128]{1,0:T(8,128)(2,1)S(1)}, u32[]{:S(2)}, u32[]{:S(2)}) collective-permute-start(f16[80,128]{1,0:T(8,128)(2,1)S(1)} %convert_element_type.27), channel_id=1, source_target_pairs={{0,1},{1,0},{2,3},{3,2},{4,5},{5,4},{6,7},{7,6},{8,9},{9,8},{10,11... | collective-permute-start | bytes 61448 | tf_op jit(solution)/shard_map/ppermute | solution.py:367
  15.2 1.2 %collective-permute-start.6 = (f32[2,1024]{1,0:T(2,128)S(1)}, f32[2,1024]{1,0:T(2,128)S(1)}, u32[]{:S(2)}, u32[]{:S(2)}) collective-permute-start(f32[2,1024]{1,0:T(2,128)S(1)} %get-tuple-element.27), channel_id=1, source_target_pairs={{0,1},{1,0},{2,3},{3,2},{4,5},{5,4},{6,7},{7,6},{8,9},{9,8},{10,11... | collective-permute-start | bytes 24584 | tf_op jit(solution)/shard_map/ppermute | solution.py:367
  16.4 3.1 %collective-permute-start.7 = (f32[1,1024]{1,0:T(1,128)S(1)}, f32[1,1024]{1,0:T(1,128)S(1)}, u32[]{:S(2)}, u32[]{:S(2)}) collective-permute-start(f32[1,1024]{1,0:T(1,128)S(1)} %get-tuple-element.31), channel_id=1, source_target_pairs={{0,3},{1,2},{2,1},{3,0},{4,7},{5,6},{6,5},{7,4},{8,11},{9,10},{10,... | collective-permute-start | bytes 12296 | tf_op jit(solution)/shard_map/ppermute | solution.py:367

commit v5 on v4

--- a/solution.py
+++ b/solution.py
@@ -62,11 +62,13 @@
     len_hbm,
     code_hbm,
     cent_hbm,
+    w_hbm,
     state_ref,
     q_ref,
     len_ref,
     code_ref,
     cent_ref,
+    w_ref,
     k_ref,
     v_ref,
     picks_ref,
@@ -83,6 +85,7 @@
                 (v_hbm, v_ref),
                 (code_hbm, code_ref),
                 (cent_hbm, cent_ref),
+                (w_hbm.at[pl.ds(0, w_ref.shape[0])], w_ref),
             )
         )
     ]
@@ -205,7 +208,7 @@
 
 def project_kernel(batch, kv, feat, count, *refs):
     state_refs, refs = refs[:count], refs[count:]
-    w0_ref, w1_ref, att_ref, keep_ref, send_ref, x_ref, o_ref = refs
+    w0_ref, w1_ref, w2_ref, att_ref, keep_ref, send_ref, x_ref, o_ref = refs
     heads = x_ref.shape[1] // feat
     rows = batch * heads
     group = heads // kv
@@ -218,7 +221,7 @@
         x_ref[:, q * feat : (q + 1) * feat] = o_ref[pl.ds(q, batch, stride=heads), :]
     att_ref[...] = o_ref[pl.ds(pl.multiple_of(lax.axis_index("seq") * group, group), group), :]
     y, start = 0.0, 0
-    for w_ref in (w0_ref, w1_ref):
+    for w_ref in (w0_ref, w1_ref, w2_ref):
         end = start + w_ref.shape[0]
         y = y + dot(x_ref[:, start:end].astype(jnp.bfloat16), w_ref[...])
         start = end
@@ -236,7 +239,9 @@
     send_ref[...] = jnp.concatenate([rows_of(1), rows_of(2)], axis=0)
 
 
-def finish_kernel(a_ref, b_ref, att_ref, after, layer_ref, attended_ref):
+def finish_kernel(a_ref, b_ref, att_ref, low_ref, high_ref, layer_ref, attended_ref, est_ref):
+    est_ref[0 : low_ref.shape[0]] = low_ref[...]
+    est_ref[low_ref.shape[0] :] = high_ref[...]
     layer_ref[...] = (a_ref[...] + b_ref[...]).astype(jnp.bfloat16)
     parts = [att_ref[g : g + 1, :] for g in range(att_ref.shape[0])]
     attended_ref[0] = jnp.concatenate(parts, axis=1).astype(jnp.bfloat16)
@@ -314,7 +319,7 @@
         first_lane = jnp.where(lane < blocks, lane * block, 0)
         est = jnp.take_along_axis(est, first_lane, axis=1, mode="promise_in_bounds")
         for i in range(step):
-            est_ref[first + i] = est[i * kv : (i + 1) * kv, :blocks]
+            est_ref[first - begin + i] = est[i * kv : (i + 1) * kv, :blocks]
 
     chunks(begin, end, body)
 
@@ -330,14 +335,14 @@
     copy.wait()
 
 
-def second_kernel(
-    block, begin, start, q_ref, len_ref, code_ref, cent_ref, w_hbm, part_ref, after, est_ref, w_ref, sem
-):
+def second_kernel(start, w_hbm, after, w_ref, sem):
     copy = fetch(w_hbm, w_ref, start, sem)
     copy.start()
-    est_ref[0:begin] = part_ref[...]
+    copy.wait()
+
+
+def third_kernel(block, begin, q_ref, len_ref, code_ref, cent_ref, after, est_ref):
     estimate_kernel(block, begin, code_ref.shape[0], q_ref, len_ref, code_ref, cent_ref, est_ref)
-    copy.wait()
 
 
 VMEM = pl.BlockSpec(memory_space=pltpu.VMEM)
@@ -381,52 +386,56 @@
     size = feat // pack + STATS
     f32, f16 = jnp.float32, jnp.float16
 
+    cuts = [heads * feat * i // 16 for i in (0, 4, 10, 16)]
+    slabs = [
+        (jax.ShapeDtypeStruct((b - a, width), out_weight.dtype), VMEM)
+        for a, b in zip(cuts, cuts[1:])
+    ]
     staged = (queries, block_len, codes, centroids)
     shape = jax.ShapeDtypeStruct((size, rows * pack), f32)
-    state, *staged = call(
+    state, *staged, weight = call(
         functools.partial(attend_kernel, block),
-        [(shape, VMEM)] + [(jax.ShapeDtypeStruct(a.shape, a.dtype), VMEM) for a in staged],
-        [(a, HBM) for a in (queries, keys, values, picks, block_len, codes, centroids)],
+        [(shape, VMEM)] + [(jax.ShapeDtypeStruct(a.shape, a.dtype), VMEM) for a in staged]
+        + [slabs[0]],
+        [
+            (a, HBM)
+            for a in (queries, keys, values, picks, block_len, codes, centroids, out_weight)
+        ],
         scratch=[
             pltpu.VMEM(keys.shape, keys.dtype),
             pltpu.VMEM(values.shape, values.dtype),
             pltpu.VMEM(picks.shape, picks.dtype),
-            pltpu.SemaphoreType.DMA((7,)),
+            pltpu.SemaphoreType.DMA((8,)),
         ],
     )
     source = [(a, VMEM) for a in staged]
     half = batch // 2
-    cuts = [heads * feat * i // 2 for i in (0, 1, 2)]
-    slabs = [
-        (jax.ShapeDtypeStruct((b - a, width), out_weight.dtype), VMEM)
-        for a, b in zip(cuts, cuts[1:])
-    ]
     sem = [pltpu.SemaphoreType.DMA]
-    part, *weights = call(
-        functools.partial(first_kernel, block, half, cuts[0]),
-        [(jax.ShapeDtypeStruct((half, kv, blocks), f32), VMEM), slabs[0]],
+    part, second = call(
+        functools.partial(first_kernel, block, half, cuts[1]),
+        [(jax.ShapeDtypeStruct((half, kv, blocks), f32), VMEM), slabs[1]],
         source + [(out_weight, HBM)],
         scratch=sem,
         flops=500_000_000,
         data=1 << 22,
     )
-    after = part
+    weights, after = [weight, second], part
     phases = [[1 << i] for i in range(2, rounds)] + [[1, 2, 3]]
     for r, hops in enumerate(phases):
         message = state.astype(f16)
         crossed = int(r < len(phases) // 2 * 2)
-        states = [move(message, hop, crossed).astype(f32) for hop in hops[::-1]]
-        states.append(move(message, 0, 1).astype(f32) if crossed else state)
+        states = [move(message, hop, crossed).astype(f32) for hop in hops]
+        states.insert(0, move(message, 0, 1).astype(f32) if crossed else state)
         if r == len(phases) - 1:
             break
         (state,) = call(
             merge_kernel, [(shape, VMEM)], [(a, VMEM) for a in states] + [(after, ANY)]
         )
         if r == 0:
-            estimates, after = call(
-                functools.partial(second_kernel, block, half, cuts[1]),
-                [(pltpu.VMEM((batch, kv, blocks), f32), VMEM), slabs[1]],
-                source + [(out_weight, HBM), (part, VMEM), (state, ANY)],
+            (after,) = call(
+                functools.partial(second_kernel, cuts[2]),
+                [slabs[2]],
+                [(out_weight, HBM), (state, ANY)],
                 scratch=sem,
                 flops=500_000_000,
                 data=1 << 22,
@@ -441,13 +450,21 @@
     )
     total = keep + move(send, 0, 1)
     own, send = total[: half // 2], total[half // 2 :]
-    layer_out, attended = call(
+    (last,) = call(
+        functools.partial(third_kernel, block, half),
+        [(jax.ShapeDtypeStruct((batch - half, kv, blocks), f32), VMEM)],
+        source + [(total, ANY)],
+        flops=500_000_000,
+        data=1 << 22,
+    )
+    layer_out, attended, estimates = call(
         finish_kernel,
         [
             (jax.ShapeDtypeStruct((batch // parts, width), jnp.bfloat16), VMEM),
             (jax.ShapeDtypeStruct((1, 1, group * feat), jnp.bfloat16), VMEM),
+            (jax.ShapeDtypeStruct((batch, kv, blocks), f32), VMEM),
         ],
-        [(own, VMEM), (move(send, 0, 3), VMEM), (attended, VMEM), (after, ANY)],
+        [(a, VMEM) for a in (own, move(send, 0, 3), attended, part, last)],
     )
     return (estimates, attended, layer_out)
 

time: 20.4 us -> 20.1 us (0.985)
  Pallas kernels: 6.42 us -> 7.43 us
  waiting for transfers between devices: 3.18 us -> 2.56 us
  local copies, waits for them, and re-layouts: 0.6 us -> 0.01 us
    pallas_call x6 -> x7, Pallas kernels: 6.42 us -> 7.43 us  [call(): pl.pallas_call(kernel, out_shape=[shape for shape, _ in out], in_specs=[s...]
    ppermute x8, waiting for transfers between devices: 3.18 us -> 2.56 us  [move(): return lax.ppermute(x, ('seq', 'head'), pairs)]
    unnamed x1 -> x0, local copies, waits for them, and re-layouts: 0.59 us -> none
  transfers between devices with their start and end apart: 8 -> 8, of which waited for: 4 -> 4; matrix products, arithmetic and copies ran while one was open for 3% -> 0% of each run, Pallas kernels for 16% -> 21%
where the time goes in v5:
time: 20.1 us; the launch traced here: 19.9 us
  starting transfers between devices  9.15 us (46%)
  Pallas kernels  7.43 us (37%)
  waiting for transfers between devices  2.56 us (13%)
  between operations  0.75 us (4%)
    ppermute x8, starting transfers between devices, move(): return lax.ppermute(x, ('seq', 'head'), pairs)  9.15 us
    pallas_call x7, Pallas kernels, call(): pl.pallas_call(kernel, out_shape=[shape for shape, _ in out], in_specs=[s...  7.43 us
    ppermute x8, waiting for transfers between devices, move(): return lax.ppermute(x, ('seq', 'head'), pairs)  2.56 us
  transfers between devices with their start and end apart: 8, of which 4 were waited for; matrix products, arithmetic and copies ran while one was open for 0% of the time, Pallas kernels for 21%

profile of v5, /device:TPU:0, one launch (start us, length us, event | category | flops | bytes accessed | tf_op | source)
XLA Modules:
  0.0 19.9 jit_solution(6764415475973834921)
XLA Ops:
  0.6 1.8 %shard_map.103 = (f32[80,128]{1,0:T(8,128)S(1)}, bf16[4,16,128]{2,1,0:T(8,128)(2,1)S(1)}, s32[4,8]{1,0:T(4,128)S(1)}, s32[4,2,32,128]{3,2,1,0:T(8,128)S(1)}, f32...) custom-call(bf16[4,16,128]{2,1,0:T(8,128)(2,1)} %q_hbm.1, bf16[4,2,128,128]{3,2,1,0:T(8,128)(2,1)} %k_hbm.1, ...), custom_call_target="tpu_custom_call" | custom-call | tf_op jit(solution)/shard_map/pallas_call | solution.py:354
  2.4 3.5 %collective-permute-start.1 = (f16[80,128]{1,0:T(8,128)(2,1)S(1)}, f16[80,128]{1,0:T(8,128)(2,1)S(1)}, u32[]{:S(2)}, u32[]{:S(2)}) collective-permute-start(f16[80,128]{1,0:T(8,128)(2,1)S(1)} %convert_element_type.24), channel_id=1, source_target_pairs={{0,17},{1,16},{2,19},{3,18},{4,21},{5,20},{6,23},{7,22},{8,25},{9,... | collective-permute-start | bytes 61448 | tf_op jit(solution)/shard_map/ppermute | solution.py:372
  6.0 0.7 %collective-permute-start = (f16[80,128]{1,0:T(8,128)(2,1)S(1)}, f16[80,128]{1,0:T(8,128)(2,1)S(1)}, u32[]{:S(2)}, u32[]{:S(2)}) collective-permute-start(f16[80,128]{1,0:T(8,128)(2,1)S(1)} %convert_element_type.24), channel_id=1, source_target_pairs={{0,1},{1,0},{2,3},{3,2},{4,5},{5,4},{6,7},{7,6},{8,9},{9,8},{10,11... | collective-permute-start | bytes 61448 | tf_op jit(solution)/shard_map/ppermute | solution.py:372
  6.6 1.4 %shard_map.104 = (f32[2,2,8]{2,1,0:T(2,128)S(1)}, bf16[768,1024]{1,0:T(8,128)(2,1)S(1)}) custom-call(bf16[4,16,128]{2,1,0:T(8,128)(2,1)S(1)} %get-tuple-element.18.q_ref, s32[4,8]{1,0:T(4,128)S(1)} %get-tuple-element.19.len_ref, s32[4,2,32,128]{3,2,1,0:T(8,128)S(1)} %get-tuple-element.20.code_ref, f32[2,4,32,256]{3,2,1,0:T(8,128)S(1)} %get-tuple-element.21.cent_ref, ...), custom_call_target="tpu_custom_call" | custom-call | flops 500000000 | bytes 4194304 | tf_op jit(solution)/shard_map/pallas_call | solution.py:354
  8.1 0.0 collective-permute-done.1
  8.1 0.0 collective-permute-done
  8.2 2.3 %collective-permute-start.5 = (f16[80,128]{1,0:T(8,128)(2,1)S(1)}, f16[80,128]{1,0:T(8,128)(2,1)S(1)}, u32[]{:S(2)}, u32[]{:S(2)}) collective-permute-start(f16[80,128]{1,0:T(8,128)(2,1)S(1)} %convert_element_type.27), channel_id=1, source_target_pairs={{0,13},{1,12},{2,15},{3,14},{4,9},{5,8},{6,11},{7,10},{8,5},{9,4},... | collective-permute-start | bytes 61448 | tf_op jit(solution)/shard_map/ppermute | solution.py:372
  10.4 0.5 %collective-permute-start.4 = (f16[80,128]{1,0:T(8,128)(2,1)S(1)}, f16[80,128]{1,0:T(8,128)(2,1)S(1)}, u32[]{:S(2)}, u32[]{:S(2)}) collective-permute-start(f16[80,128]{1,0:T(8,128)(2,1)S(1)} %convert_element_type.27), channel_id=1, source_target_pairs={{0,9},{1,8},{2,11},{3,10},{4,13},{5,12},{6,15},{7,14},{8,1},{9,0},... | collective-permute-start | bytes 61448 | tf_op jit(solution)/shard_map/ppermute | solution.py:372
  10.9 0.2 collective-permute-start.3
  11.1 0.4 %collective-permute-start.2 = (f16[80,128]{1,0:T(8,128)(2,1)S(1)}, f16[80,128]{1,0:T(8,128)(2,1)S(1)}, u32[]{:S(2)}, u32[]{:S(2)}) collective-permute-start(f16[80,128]{1,0:T(8,128)(2,1)S(1)} %convert_element_type.27), channel_id=1, source_target_pairs={{0,1},{1,0},{2,3},{3,2},{4,5},{5,4},{6,7},{7,6},{8,9},{9,8},{10,11... | collective-permute-start | bytes 61448 | tf_op jit(solution)/shard_map/ppermute | solution.py:372
  11.6 1.4 %shard_map.106.refs_6_ = bf16[768,1024]{1,0:T(8,128)(2,1)S(1)} custom-call(bf16[2048,1024]{1,0:T(8,128)(2,1)} %w_hbm.5, f32[80,128]{1,0:T(8,128)S(1)} %shard_map.105.after), custom_call_target="tpu_custom_call" | custom-call | flops 500000000 | bytes 4194304 | tf_op jit(solution)/shard_map/pallas_call | solution.py:354
  13.0 0.0 collective-permute-done.5
  13.0 0.6 %collective-permute-done.4 = f16[80,128]{1,0:T(8,128)(2,1)S(1)} collective-permute-done((f16[80,128]{1,0:T(8,128)(2,1)S(1)}, f16[80,128]{1,0:T(8,128)(2,1)S(1)}, u32[]{:S(2)}, u32[]{:S(2)}) %collective-permute-start.4) | collective-permute-done | bytes 20512 | tf_op jit(solution)/shard_map/ppermute | solution.py:372
  13.6 0.5 %collective-permute-done.3 = f16[80,128]{1,0:T(8,128)(2,1)S(1)} collective-permute-done((f16[80,128]{1,0:T(8,128)(2,1)S(1)}, f16[80,128]{1,0:T(8,128)(2,1)S(1)}, u32[]{:S(2)}, u32[]{:S(2)}) %collective-permute-start.3) | collective-permute-done | bytes 20512 | tf_op jit(solution)/shard_map/ppermute | solution.py:372
  14.1 0.0 collective-permute-done.2
  14.2 0.8 %shard_map.107 = (f32[8,128]{1,0:T(8,128)S(1)}, f32[2,1024]{1,0:T(2,128)S(1)}, f32[2,1024]{1,0:T(2,128)S(1)}) custom-call(f32[80,128]{1,0:T(8,128)S(1)} %convert_element_type.28.refs_0_, f32[80,128]{1,0:T(8,128)S(1)} %convert_element_type.29.refs_1_, f32[80,128]{1,0:T(8,128)S(1)} %convert_element_type.30.refs_2_, ...), custom_call_target="tpu_custom_call" | custom-call | tf_op jit(solution)/shard_map/pallas_call | solution.py:354
  15.0 0.2 %collective-permute-start.6 = (f32[2,1024]{1,0:T(2,128)S(1)}, f32[2,1024]{1,0:T(2,128)S(1)}, u32[]{:S(2)}, u32[]{:S(2)}) collective-permute-start(f32[2,1024]{1,0:T(2,128)S(1)} %get-tuple-element.26), channel_id=1, source_target_pairs={{0,1},{1,0},{2,3},{3,2},{4,5},{5,4},{6,7},{7,6},{8,9},{9,8},{10,11... | collective-permute-start | bytes 24584 | tf_op jit(solution)/shard_map/ppermute | solution.py:372
  15.2 1.0 %collective-permute-done.6 = f32[2,1024]{1,0:T(2,128)S(1)} collective-permute-done((f32[2,1024]{1,0:T(2,128)S(1)}, f32[2,1024]{1,0:T(2,128)S(1)}, u32[]{:S(2)}, u32[]{:S(2)}) %collective-permute-start.6) | collective-permute-done | bytes 8224 | tf_op jit(solution)/shard_map/ppermute | solution.py:372
  16.2 1.3 %collective-permute-start.7 = (f32[1,1024]{1,0:T(1,128)S(1)}, f32[1,1024]{1,0:T(1,128)S(1)}, u32[]{:S(2)}, u32[]{:S(2)}) collective-permute-start(f32[1,1024]{1,0:T(1,128)S(1)} %get-tuple-element.31), channel_id=1, source_target_pairs={{0,3},{1,2},{2,1},{3,0},{4,7},{5,6},{6,5},{7,4},{8,11},{9,10},{10,... | collective-permute-start | bytes 12296 | tf_op jit(solution)/shard_map/ppermute | solution.py:372
  17.6 1.4 %shard_map.108.high_ref = f32[2,2,8]{2,1,0:T(2,128)S(1)} custom-call(bf16[4,16,128]{2,1,0:T(8,128)(2,1)S(1)} %get-tuple-element.18.q_ref, s32[4,8]{1,0:T(4,128)S(1)} %get-tuple-element.19.len_ref, s32[4,2,32,128]{3,2,1,0:T(8,128)S(1)} %get-tuple-element.20.code_ref, f32[2,4,32,256]{3,2,1,0:T(8,128)S(1)} %get-tuple-element.21.cent_ref, f32[2,1024]{1,0:T(2,128)S(1)} %add.3.after), custom_call_target="tpu_custom_call" | custom-call | flops 500000000 | bytes 4194304 | tf_op jit(solution)/shard_map/pallas_call | solution.py:354
  18.9 0.4 %collective-permute-done.7.b_ref = f32[1,1024]{1,0:T(1,128)S(1)} collective-permute-done((f32[1,1024]{1,0:T(1,128)S(1)}, f32[1,1024]{1,0:T(1,128)S(1)}, u32[]{:S(2)}, u32[]{:S(2)}) %collective-permute-start.7) | collective-permute-done | bytes 4128 | tf_op jit(solution)/shard_map/ppermute | solution.py:372
  19.3 0.6 %shard_map.109 = (bf16[1,1024]{1,0:T(2,128)(2,1)}, bf16[1,1,1024]{2,1,0:T(2,128)(2,1)}, f32[4,2,8]{2,1,0:T(2,128)}) custom-call(f32[1,1024]{1,0:T(1,128)S(1)} %get-tuple-element.32.a_ref, f32[1,1024]{1,0:T(1,128)S(1)} %collective-permute-done.7.b_ref, f32[8,128]{1,0:T(8,128)S(1)} %get-tuple-element.27.att_ref, ...), custom_call_target="tpu_custom_call" | custom-call | tf_op jit(solution)/shard_map/pallas_call | solution.py:354
  (11 shorter events, 0.1 us)
Async XLA Ops:
  2.4 5.6 %collective-permute-start.1 = (f16[80,128]{1,0:T(8,128)(2,1)S(1)}, f16[80,128]{1,0:T(8,128)(2,1)S(1)}, u32[]{:S(2)}, u32[]{:S(2)}) collective-permute-start(f16[80,128]{1,0:T(8,128)(2,1)S(1)} %convert_element_type.24), channel_id=1, source_target_pairs={{0,17},{1,16},{2,19},{3,18},{4,21},{5,20},{6,23},{7,22},{8,25},{9,... | collective-permute-start | bytes 61448 | tf_op jit(solution)/shard_map/ppermute | solution.py:372
  6.0 2.1 %collective-permute-start = (f16[80,128]{1,0:T(8,128)(2,1)S(1)}, f16[80,128]{1,0:T(8,128)(2,1)S(1)}, u32[]{:S(2)}, u32[]{:S(2)}) collective-permute-start(f16[80,128]{1,0:T(8,128)(2,1)S(1)} %convert_element_type.24), channel_id=1, source_target_pairs={{0,1},{1,0},{2,3},{3,2},{4,5},{5,4},{6,7},{7,6},{8,9},{9,8},{10,11... | collective-permute-start | bytes 61448 | tf_op jit(solution)/shard_map/ppermute | solution.py:372
  8.2 4.8 %collective-permute-start.5 = (f16[80,128]{1,0:T(8,128)(2,1)S(1)}, f16[80,128]{1,0:T(8,128)(2,1)S(1)}, u32[]{:S(2)}, u32[]{:S(2)}) collective-permute-start(f16[80,128]{1,0:T(8,128)(2,1)S(1)} %convert_element_type.27), channel_id=1, source_target_pairs={{0,13},{1,12},{2,15},{3,14},{4,9},{5,8},{6,11},{7,10},{8,5},{9,4},... | collective-permute-start | bytes 61448 | tf_op jit(solution)/shard_map/ppermute | solution.py:372
  10.4 3.2 %collective-permute-start.4 = (f16[80,128]{1,0:T(8,128)(2,1)S(1)}, f16[80,128]{1,0:T(8,128)(2,1)S(1)}, u32[]{:S(2)}, u32[]{:S(2)}) collective-permute-start(f16[80,128]{1,0:T(8,128)(2,1)S(1)} %convert_element_type.27), channel_id=1, source_target_pairs={{0,9},{1,8},{2,11},{3,10},{4,13},{5,12},{6,15},{7,14},{8,1},{9,0},... | collective-permute-start | bytes 61448 | tf_op jit(solution)/shard_map/ppermute | solution.py:372
  10.9 3.2 %collective-permute-start.3 = (f16[80,128]{1,0:T(8,128)(2,1)S(1)}, f16[80,128]{1,0:T(8,128)(2,1)S(1)}, u32[]{:S(2)}, u32[]{:S(2)}) collective-permute-start(f16[80,128]{1,0:T(8,128)(2,1)S(1)} %convert_element_type.27), channel_id=1, source_target_pairs={{0,5},{1,4},{2,7},{3,6},{4,1},{5,0},{6,3},{7,2},{8,13},{9,12},{10,... | collective-permute-start | bytes 61448 | tf_op jit(solution)/shard_map/ppermute | solution.py:372
  11.1 3.0 %collective-permute-start.2 = (f16[80,128]{1,0:T(8,128)(2,1)S(1)}, f16[80,128]{1,0:T(8,128)(2,1)S(1)}, u32[]{:S(2)}, u32[]{:S(2)}) collective-permute-start(f16[80,128]{1,0:T(8,128)(2,1)S(1)} %convert_element_type.27), channel_id=1, source_target_pairs={{0,1},{1,0},{2,3},{3,2},{4,5},{5,4},{6,7},{7,6},{8,9},{9,8},{10,11... | collective-permute-start | bytes 61448 | tf_op jit(solution)/shard_map/ppermute | solution.py:372
  15.0 1.2 %collective-permute-start.6 = (f32[2,1024]{1,0:T(2,128)S(1)}, f32[2,1024]{1,0:T(2,128)S(1)}, u32[]{:S(2)}, u32[]{:S(2)}) collective-permute-start(f32[2,1024]{1,0:T(2,128)S(1)} %get-tuple-element.26), channel_id=1, source_target_pairs={{0,1},{1,0},{2,3},{3,2},{4,5},{5,4},{6,7},{7,6},{8,9},{9,8},{10,11... | collective-permute-start | bytes 24584 | tf_op jit(solution)/shard_map/ppermute | solution.py:372
  16.2 3.1 %collective-permute-start.7 = (f32[1,1024]{1,0:T(1,128)S(1)}, f32[1,1024]{1,0:T(1,128)S(1)}, u32[]{:S(2)}, u32[]{:S(2)}) collective-permute-start(f32[1,1024]{1,0:T(1,128)S(1)} %get-tuple-element.31), channel_id=1, source_target_pairs={{0,3},{1,2},{2,1},{3,0},{4,7},{5,6},{6,5},{7,4},{8,11},{9,10},{10,... | collective-permute-start | bytes 12296 | tf_op jit(solution)/shard_map/ppermute | solution.py:372

commit v6 on v5

--- a/solution.py
+++ b/solution.py
@@ -158,12 +158,8 @@
             wide = jnp.where(
                 lane[:depth] < i * step * heads, wide, acc[i * depth : (i + 1) * depth]
             )
-        size = jnp.abs(v_ref[some].reshape(pairs * tokens, feat).astype(jnp.float32))
-        size = jnp.max(jnp.max(size, axis=0, keepdims=True), axis=1, keepdims=True)
-        scale = jnp.floor(jnp.log(jnp.maximum(size, 1e-30)) / LN2)
-        scale = jnp.where(total > 0.0, scale, -100.0)
         state_ref[:, c * lanes : (c + 1) * lanes] = encode(
-            wide * jnp.exp(scale * -LN2), top, total, scale
+            wide, top, total, jnp.zeros_like(top)
         )
     for load in loads[5:]:
         load.wait()
@@ -178,9 +174,11 @@
 
 
 def encode(acc, top, total, scale):
-    rows = terms(top) + terms(total) + [scale]
+    size = jnp.max(jnp.abs(acc), axis=0, keepdims=True)
+    shift = jnp.floor(jnp.log(jnp.maximum(size, 1e-30)) / LN2)
+    rows = terms(top) + terms(total) + [scale + shift]
     rows.append(jnp.zeros((STATS - len(rows), acc.shape[1]), jnp.float32))
-    return jnp.concatenate([acc] + rows, axis=0)
+    return jnp.concatenate([acc * jnp.exp(shift * -LN2)] + rows, axis=0)
 
 
 def decode(state):

time: 20.1 us -> 20.2 us (level)
  no operation moved by 1% of the time
where the time goes in v6:
time: 20.2 us; the launch traced here: 20 us
  starting transfers between devices  9.15 us (45%)
  Pallas kernels  7.47 us (37%)
  waiting for transfers between devices  2.55 us (13%)
  between operations  0.75 us (4%)
    ppermute x8, starting transfers between devices, move(): return lax.ppermute(x, ('seq', 'head'), pairs)  9.15 us
    pallas_call x7, Pallas kernels, call(): pl.pallas_call(kernel, out_shape=[shape for shape, _ in out], in_specs=[s...  7.47 us
    ppermute x8, waiting for transfers between devices, move(): return lax.ppermute(x, ('seq', 'head'), pairs)  2.55 us
  transfers between devices with their start and end apart: 8, of which 4 were waited for; matrix products, arithmetic and copies ran while one was open for 0% of the time, Pallas kernels for 21%

profile of v6, /device:TPU:0, one launch (start us, length us, event | category | flops | bytes accessed | tf_op | source)
XLA Modules:
  0.0 20.0 jit_solution(14876885211542026357)
XLA Ops:
  0.6 1.8 %shard_map.103 = (f32[80,128]{1,0:T(8,128)S(1)}, bf16[4,16,128]{2,1,0:T(8,128)(2,1)S(1)}, s32[4,8]{1,0:T(4,128)S(1)}, s32[4,2,32,128]{3,2,1,0:T(8,128)S(1)}, f32...) custom-call(bf16[4,16,128]{2,1,0:T(8,128)(2,1)} %q_hbm.1, bf16[4,2,128,128]{3,2,1,0:T(8,128)(2,1)} %k_hbm.1, ...), custom_call_target="tpu_custom_call" | custom-call | tf_op jit(solution)/shard_map/pallas_call | solution.py:352
  2.4 3.5 %collective-permute-start.1 = (f16[80,128]{1,0:T(8,128)(2,1)S(1)}, f16[80,128]{1,0:T(8,128)(2,1)S(1)}, u32[]{:S(2)}, u32[]{:S(2)}) collective-permute-start(f16[80,128]{1,0:T(8,128)(2,1)S(1)} %convert_element_type.24), channel_id=1, source_target_pairs={{0,17},{1,16},{2,19},{3,18},{4,21},{5,20},{6,23},{7,22},{8,25},{9,... | collective-permute-start | bytes 61448 | tf_op jit(solution)/shard_map/ppermute | solution.py:370
  6.0 0.7 %collective-permute-start = (f16[80,128]{1,0:T(8,128)(2,1)S(1)}, f16[80,128]{1,0:T(8,128)(2,1)S(1)}, u32[]{:S(2)}, u32[]{:S(2)}) collective-permute-start(f16[80,128]{1,0:T(8,128)(2,1)S(1)} %convert_element_type.24), channel_id=1, source_target_pairs={{0,1},{1,0},{2,3},{3,2},{4,5},{5,4},{6,7},{7,6},{8,9},{9,8},{10,11... | collective-permute-start | bytes 61448 | tf_op jit(solution)/shard_map/ppermute | solution.py:370
  6.7 1.4 %shard_map.104 = (f32[2,2,8]{2,1,0:T(2,128)S(1)}, bf16[768,1024]{1,0:T(8,128)(2,1)S(1)}) custom-call(bf16[4,16,128]{2,1,0:T(8,128)(2,1)S(1)} %get-tuple-element.18.q_ref, s32[4,8]{1,0:T(4,128)S(1)} %get-tuple-element.19.len_ref, s32[4,2,32,128]{3,2,1,0:T(8,128)S(1)} %get-tuple-element.20.code_ref, f32[2,4,32,256]{3,2,1,0:T(8,128)S(1)} %get-tuple-element.21.cent_ref, ...), custom_call_target="tpu_custom_call" | custom-call | flops 500000000 | bytes 4194304 | tf_op jit(solution)/shard_map/pallas_call | solution.py:352
  8.1 0.0 collective-permute-done.1
  8.1 0.0 collective-permute-done
  8.2 2.3 %collective-permute-start.5 = (f16[80,128]{1,0:T(8,128)(2,1)S(1)}, f16[80,128]{1,0:T(8,128)(2,1)S(1)}, u32[]{:S(2)}, u32[]{:S(2)}) collective-permute-start(f16[80,128]{1,0:T(8,128)(2,1)S(1)} %convert_element_type.27), channel_id=1, source_target_pairs={{0,13},{1,12},{2,15},{3,14},{4,9},{5,8},{6,11},{7,10},{8,5},{9,4},... | collective-permute-start | bytes 61448 | tf_op jit(solution)/shard_map/ppermute | solution.py:370
  10.5 0.5 %collective-permute-start.4 = (f16[80,128]{1,0:T(8,128)(2,1)S(1)}, f16[80,128]{1,0:T(8,128)(2,1)S(1)}, u32[]{:S(2)}, u32[]{:S(2)}) collective-permute-start(f16[80,128]{1,0:T(8,128)(2,1)S(1)} %convert_element_type.27), channel_id=1, source_target_pairs={{0,9},{1,8},{2,11},{3,10},{4,13},{5,12},{6,15},{7,14},{8,1},{9,0},... | collective-permute-start | bytes 61448 | tf_op jit(solution)/shard_map/ppermute | solution.py:370
  11.0 0.2 collective-permute-start.3
  11.2 0.4 %collective-permute-start.2 = (f16[80,128]{1,0:T(8,128)(2,1)S(1)}, f16[80,128]{1,0:T(8,128)(2,1)S(1)}, u32[]{:S(2)}, u32[]{:S(2)}) collective-permute-start(f16[80,128]{1,0:T(8,128)(2,1)S(1)} %convert_element_type.27), channel_id=1, source_target_pairs={{0,1},{1,0},{2,3},{3,2},{4,5},{5,4},{6,7},{7,6},{8,9},{9,8},{10,11... | collective-permute-start | bytes 61448 | tf_op jit(solution)/shard_map/ppermute | solution.py:370
  11.6 1.4 %shard_map.106.refs_6_ = bf16[768,1024]{1,0:T(8,128)(2,1)S(1)} custom-call(bf16[2048,1024]{1,0:T(8,128)(2,1)} %w_hbm.5, f32[80,128]{1,0:T(8,128)S(1)} %shard_map.105.after), custom_call_target="tpu_custom_call" | custom-call | flops 500000000 | bytes 4194304 | tf_op jit(solution)/shard_map/pallas_call | solution.py:352
  13.0 0.0 collective-permute-done.5
  13.0 0.6 %collective-permute-done.4 = f16[80,128]{1,0:T(8,128)(2,1)S(1)} collective-permute-done((f16[80,128]{1,0:T(8,128)(2,1)S(1)}, f16[80,128]{1,0:T(8,128)(2,1)S(1)}, u32[]{:S(2)}, u32[]{:S(2)}) %collective-permute-start.4) | collective-permute-done | bytes 20512 | tf_op jit(solution)/shard_map/ppermute | solution.py:370
  13.7 0.5 %collective-permute-done.3 = f16[80,128]{1,0:T(8,128)(2,1)S(1)} collective-permute-done((f16[80,128]{1,0:T(8,128)(2,1)S(1)}, f16[80,128]{1,0:T(8,128)(2,1)S(1)}, u32[]{:S(2)}, u32[]{:S(2)}) %collective-permute-start.3) | collective-permute-done | bytes 20512 | tf_op jit(solution)/shard_map/ppermute | solution.py:370
  14.2 0.0 collective-permute-done.2
  14.2 0.8 %shard_map.107 = (f32[8,128]{1,0:T(8,128)S(1)}, f32[2,1024]{1,0:T(2,128)S(1)}, f32[2,1024]{1,0:T(2,128)S(1)}) custom-call(f32[80,128]{1,0:T(8,128)S(1)} %convert_element_type.28.refs_0_, f32[80,128]{1,0:T(8,128)S(1)} %convert_element_type.29.refs_1_, f32[80,128]{1,0:T(8,128)S(1)} %convert_element_type.30.refs_2_, ...), custom_call_target="tpu_custom_call" | custom-call | tf_op jit(solution)/shard_map/pallas_call | solution.py:352
  15.0 0.2 %collective-permute-start.6 = (f32[2,1024]{1,0:T(2,128)S(1)}, f32[2,1024]{1,0:T(2,128)S(1)}, u32[]{:S(2)}, u32[]{:S(2)}) collective-permute-start(f32[2,1024]{1,0:T(2,128)S(1)} %get-tuple-element.26), channel_id=1, source_target_pairs={{0,1},{1,0},{2,3},{3,2},{4,5},{5,4},{6,7},{7,6},{8,9},{9,8},{10,11... | collective-permute-start | bytes 24584 | tf_op jit(solution)/shard_map/ppermute | solution.py:370
  15.2 1.0 %collective-permute-done.6 = f32[2,1024]{1,0:T(2,128)S(1)} collective-permute-done((f32[2,1024]{1,0:T(2,128)S(1)}, f32[2,1024]{1,0:T(2,128)S(1)}, u32[]{:S(2)}, u32[]{:S(2)}) %collective-permute-start.6) | collective-permute-done | bytes 8224 | tf_op jit(solution)/shard_map/ppermute | solution.py:370
  16.3 1.3 %collective-permute-start.7 = (f32[1,1024]{1,0:T(1,128)S(1)}, f32[1,1024]{1,0:T(1,128)S(1)}, u32[]{:S(2)}, u32[]{:S(2)}) collective-permute-start(f32[1,1024]{1,0:T(1,128)S(1)} %get-tuple-element.31), channel_id=1, source_target_pairs={{0,3},{1,2},{2,1},{3,0},{4,7},{5,6},{6,5},{7,4},{8,11},{9,10},{10,... | collective-permute-start | bytes 12296 | tf_op jit(solution)/shard_map/ppermute | solution.py:370
  17.6 1.4 %shard_map.108.high_ref = f32[2,2,8]{2,1,0:T(2,128)S(1)} custom-call(bf16[4,16,128]{2,1,0:T(8,128)(2,1)S(1)} %get-tuple-element.18.q_ref, s32[4,8]{1,0:T(4,128)S(1)} %get-tuple-element.19.len_ref, s32[4,2,32,128]{3,2,1,0:T(8,128)S(1)} %get-tuple-element.20.code_ref, f32[2,4,32,256]{3,2,1,0:T(8,128)S(1)} %get-tuple-element.21.cent_ref, f32[2,1024]{1,0:T(2,128)S(1)} %add.3.after), custom_call_target="tpu_custom_call" | custom-call | flops 500000000 | bytes 4194304 | tf_op jit(solution)/shard_map/pallas_call | solution.py:352
  19.0 0.4 %collective-permute-done.7.b_ref = f32[1,1024]{1,0:T(1,128)S(1)} collective-permute-done((f32[1,1024]{1,0:T(1,128)S(1)}, f32[1,1024]{1,0:T(1,128)S(1)}, u32[]{:S(2)}, u32[]{:S(2)}) %collective-permute-start.7) | collective-permute-done | bytes 4128 | tf_op jit(solution)/shard_map/ppermute | solution.py:370
  19.4 0.6 %shard_map.109 = (bf16[1,1024]{1,0:T(2,128)(2,1)}, bf16[1,1,1024]{2,1,0:T(2,128)(2,1)}, f32[4,2,8]{2,1,0:T(2,128)}) custom-call(f32[1,1024]{1,0:T(1,128)S(1)} %get-tuple-element.32.a_ref, f32[1,1024]{1,0:T(1,128)S(1)} %collective-permute-done.7.b_ref, f32[8,128]{1,0:T(8,128)S(1)} %get-tuple-element.27.att_ref, ...), custom_call_target="tpu_custom_call" | custom-call | tf_op jit(solution)/shard_map/pallas_call | solution.py:352
  (11 shorter events, 0.1 us)
Async XLA Ops:
  2.4 5.6 %collective-permute-start.1 = (f16[80,128]{1,0:T(8,128)(2,1)S(1)}, f16[80,128]{1,0:T(8,128)(2,1)S(1)}, u32[]{:S(2)}, u32[]{:S(2)}) collective-permute-start(f16[80,128]{1,0:T(8,128)(2,1)S(1)} %convert_element_type.24), channel_id=1, source_target_pairs={{0,17},{1,16},{2,19},{3,18},{4,21},{5,20},{6,23},{7,22},{8,25},{9,... | collective-permute-start | bytes 61448 | tf_op jit(solution)/shard_map/ppermute | solution.py:370
  6.0 2.1 %collective-permute-start = (f16[80,128]{1,0:T(8,128)(2,1)S(1)}, f16[80,128]{1,0:T(8,128)(2,1)S(1)}, u32[]{:S(2)}, u32[]{:S(2)}) collective-permute-start(f16[80,128]{1,0:T(8,128)(2,1)S(1)} %convert_element_type.24), channel_id=1, source_target_pairs={{0,1},{1,0},{2,3},{3,2},{4,5},{5,4},{6,7},{7,6},{8,9},{9,8},{10,11... | collective-permute-start | bytes 61448 | tf_op jit(solution)/shard_map/ppermute | solution.py:370
  8.2 4.8 %collective-permute-start.5 = (f16[80,128]{1,0:T(8,128)(2,1)S(1)}, f16[80,128]{1,0:T(8,128)(2,1)S(1)}, u32[]{:S(2)}, u32[]{:S(2)}) collective-permute-start(f16[80,128]{1,0:T(8,128)(2,1)S(1)} %convert_element_type.27), channel_id=1, source_target_pairs={{0,13},{1,12},{2,15},{3,14},{4,9},{5,8},{6,11},{7,10},{8,5},{9,4},... | collective-permute-start | bytes 61448 | tf_op jit(solution)/shard_map/ppermute | solution.py:370
  10.5 3.2 %collective-permute-start.4 = (f16[80,128]{1,0:T(8,128)(2,1)S(1)}, f16[80,128]{1,0:T(8,128)(2,1)S(1)}, u32[]{:S(2)}, u32[]{:S(2)}) collective-permute-start(f16[80,128]{1,0:T(8,128)(2,1)S(1)} %convert_element_type.27), channel_id=1, source_target_pairs={{0,9},{1,8},{2,11},{3,10},{4,13},{5,12},{6,15},{7,14},{8,1},{9,0},... | collective-permute-start | bytes 61448 | tf_op jit(solution)/shard_map/ppermute | solution.py:370
  11.0 3.2 %collective-permute-start.3 = (f16[80,128]{1,0:T(8,128)(2,1)S(1)}, f16[80,128]{1,0:T(8,128)(2,1)S(1)}, u32[]{:S(2)}, u32[]{:S(2)}) collective-permute-start(f16[80,128]{1,0:T(8,128)(2,1)S(1)} %convert_element_type.27), channel_id=1, source_target_pairs={{0,5},{1,4},{2,7},{3,6},{4,1},{5,0},{6,3},{7,2},{8,13},{9,12},{10,... | collective-permute-start | bytes 61448 | tf_op jit(solution)/shard_map/ppermute | solution.py:370
  11.2 3.0 %collective-permute-start.2 = (f16[80,128]{1,0:T(8,128)(2,1)S(1)}, f16[80,128]{1,0:T(8,128)(2,1)S(1)}, u32[]{:S(2)}, u32[]{:S(2)}) collective-permute-start(f16[80,128]{1,0:T(8,128)(2,1)S(1)} %convert_element_type.27), channel_id=1, source_target_pairs={{0,1},{1,0},{2,3},{3,2},{4,5},{5,4},{6,7},{7,6},{8,9},{9,8},{10,11... | collective-permute-start | bytes 61448 | tf_op jit(solution)/shard_map/ppermute | solution.py:370
  15.0 1.2 %collective-permute-start.6 = (f32[2,1024]{1,0:T(2,128)S(1)}, f32[2,1024]{1,0:T(2,128)S(1)}, u32[]{:S(2)}, u32[]{:S(2)}) collective-permute-start(f32[2,1024]{1,0:T(2,128)S(1)} %get-tuple-element.26), channel_id=1, source_target_pairs={{0,1},{1,0},{2,3},{3,2},{4,5},{5,4},{6,7},{7,6},{8,9},{9,8},{10,11... | collective-permute-start | bytes 24584 | tf_op jit(solution)/shard_map/ppermute | solution.py:370
  16.3 3.1 %collective-permute-start.7 = (f32[1,1024]{1,0:T(1,128)S(1)}, f32[1,1024]{1,0:T(1,128)S(1)}, u32[]{:S(2)}, u32[]{:S(2)}) collective-permute-start(f32[1,1024]{1,0:T(1,128)S(1)} %get-tuple-element.31), channel_id=1, source_target_pairs={{0,3},{1,2},{2,1},{3,0},{4,7},{5,6},{6,5},{7,4},{8,11},{9,10},{10,... | collective-permute-start | bytes 12296 | tf_op jit(solution)/shard_map/ppermute | solution.py:370

commit v7 on v6

--- a/solution.py
+++ b/solution.py
@@ -9,7 +9,7 @@
 
 NEG = -30000.0
 LANES = 128
-STATS = 16
+STATS = 8
 LN2 = 0.6931471805599453
 NT = (((1,), (1,)), ((), ()))
 NN = (((1,), (0,)), ((), ()))
@@ -422,9 +422,14 @@
     for r, hops in enumerate(phases):
         message = state.astype(f16)
         crossed = int(r < len(phases) // 2 * 2)
-        states = [move(message, hop, crossed).astype(f32) for hop in hops]
-        states.insert(0, move(message, 0, 1).astype(f32) if crossed else state)
+        states = [move(message, hop, crossed).astype(f32) for hop in hops[::-1]]
+        states.append(move(message, 0, 1).astype(f32) if crossed else state)
         if r == len(phases) - 1:
+            if len(states) > 2:
+                (early,) = call(
+                    merge_kernel, [(shape, VMEM)], [(a, VMEM) for a in states[:2]] + [(after, ANY)]
+                )
+                states = [early] + states[2:]
             break
         (state,) = call(
             merge_kernel, [(shape, VMEM)], [(a, VMEM) for a in states] + [(after, ANY)]

time: 20.2 us -> 20.2 us (level)
    pallas_call x7 -> x8, Pallas kernels: 7.47 us -> 7.51 us  [call(): pl.pallas_call(kernel, out_shape=[shape for shape, _ in out], in_specs=[s...]
where the time goes in v7:
time: 20.2 us; the launch traced here: 20 us
  starting transfers between devices  9.23 us (46%)
  Pallas kernels  7.51 us (37%)
  waiting for transfers between devices  2.42 us (12%)
  between operations  0.76 us (4%)
    ppermute x8, starting transfers between devices, move(): return lax.ppermute(x, ('seq', 'head'), pairs)  9.23 us
    pallas_call x8, Pallas kernels, call(): pl.pallas_call(kernel, out_shape=[shape for shape, _ in out], in_specs=[s...  7.51 us
    ppermute x8, waiting for transfers between devices, move(): return lax.ppermute(x, ('seq', 'head'), pairs)  2.42 us
  transfers between devices with their start and end apart: 8, of which 4 were waited for; matrix products, arithmetic and copies ran while one was open for 0% of the time, Pallas kernels for 21%

profile of v7, /device:TPU:0, one launch (start us, length us, event | category | flops | bytes accessed | tf_op | source)
XLA Modules:
  0.0 20.0 jit_solution(604404582674722277)
XLA Ops:
  0.6 1.8 %shard_map.103 = (f32[72,128]{1,0:T(8,128)S(1)}, bf16[4,16,128]{2,1,0:T(8,128)(2,1)S(1)}, s32[4,8]{1,0:T(4,128)S(1)}, s32[4,2,32,128]{3,2,1,0:T(8,128)S(1)}, f32...) custom-call(bf16[4,16,128]{2,1,0:T(8,128)(2,1)} %q_hbm.1, bf16[4,2,128,128]{3,2,1,0:T(8,128)(2,1)} %k_hbm.1, ...), custom_call_target="tpu_custom_call" | custom-call | tf_op jit(solution)/shard_map/pallas_call | solution.py:352
  2.4 3.5 %collective-permute-start = (f16[72,128]{1,0:T(8,128)(2,1)S(1)}, f16[72,128]{1,0:T(8,128)(2,1)S(1)}, u32[]{:S(2)}, u32[]{:S(2)}) collective-permute-start(f16[72,128]{1,0:T(8,128)(2,1)S(1)} %convert_element_type.24), channel_id=1, source_target_pairs={{0,17},{1,16},{2,19},{3,18},{4,21},{5,20},{6,23},{7,22},{8,25},{9,... | collective-permute-start | bytes 55304 | tf_op jit(solution)/shard_map/ppermute | solution.py:370
  6.0 0.7 %collective-permute-start.1 = (f16[72,128]{1,0:T(8,128)(2,1)S(1)}, f16[72,128]{1,0:T(8,128)(2,1)S(1)}, u32[]{:S(2)}, u32[]{:S(2)}) collective-permute-start(f16[72,128]{1,0:T(8,128)(2,1)S(1)} %convert_element_type.24), channel_id=1, source_target_pairs={{0,1},{1,0},{2,3},{3,2},{4,5},{5,4},{6,7},{7,6},{8,9},{9,8},{10,11... | collective-permute-start | bytes 55304 | tf_op jit(solution)/shard_map/ppermute | solution.py:370
  6.7 1.4 %shard_map.104 = (f32[2,2,8]{2,1,0:T(2,128)S(1)}, bf16[768,1024]{1,0:T(8,128)(2,1)S(1)}) custom-call(bf16[4,16,128]{2,1,0:T(8,128)(2,1)S(1)} %get-tuple-element.18.q_ref, s32[4,8]{1,0:T(4,128)S(1)} %get-tuple-element.19.len_ref, s32[4,2,32,128]{3,2,1,0:T(8,128)S(1)} %get-tuple-element.20.code_ref, f32[2,4,32,256]{3,2,1,0:T(8,128)S(1)} %get-tuple-element.21.cent_ref, ...), custom_call_target="tpu_custom_call" | custom-call | flops 500000000 | bytes 4194304 | tf_op jit(solution)/shard_map/pallas_call | solution.py:352
  8.1 0.0 collective-permute-done
  8.1 0.0 collective-permute-done.1
  8.2 2.2 %collective-permute-start.2 = (f16[72,128]{1,0:T(8,128)(2,1)S(1)}, f16[72,128]{1,0:T(8,128)(2,1)S(1)}, u32[]{:S(2)}, u32[]{:S(2)}) collective-permute-start(f16[72,128]{1,0:T(8,128)(2,1)S(1)} %convert_element_type.27), channel_id=1, source_target_pairs={{0,13},{1,12},{2,15},{3,14},{4,9},{5,8},{6,11},{7,10},{8,5},{9,4},... | collective-permute-start | bytes 55304 | tf_op jit(solution)/shard_map/ppermute | solution.py:370
  10.4 0.5 %collective-permute-start.3 = (f16[72,128]{1,0:T(8,128)(2,1)S(1)}, f16[72,128]{1,0:T(8,128)(2,1)S(1)}, u32[]{:S(2)}, u32[]{:S(2)}) collective-permute-start(f16[72,128]{1,0:T(8,128)(2,1)S(1)} %convert_element_type.27), channel_id=1, source_target_pairs={{0,9},{1,8},{2,11},{3,10},{4,13},{5,12},{6,15},{7,14},{8,1},{9,0},... | collective-permute-start | bytes 55304 | tf_op jit(solution)/shard_map/ppermute | solution.py:370
  11.0 0.2 collective-permute-start.4
  11.2 0.4 %collective-permute-start.5 = (f16[72,128]{1,0:T(8,128)(2,1)S(1)}, f16[72,128]{1,0:T(8,128)(2,1)S(1)}, u32[]{:S(2)}, u32[]{:S(2)}) collective-permute-start(f16[72,128]{1,0:T(8,128)(2,1)S(1)} %convert_element_type.27), channel_id=1, source_target_pairs={{0,1},{1,0},{2,3},{3,2},{4,5},{5,4},{6,7},{7,6},{8,9},{9,8},{10,11... | collective-permute-start | bytes 55304 | tf_op jit(solution)/shard_map/ppermute | solution.py:370
  11.6 1.4 %shard_map.106.refs_2_.refs_5_ = bf16[768,1024]{1,0:T(8,128)(2,1)S(1)} custom-call(bf16[2048,1024]{1,0:T(8,128)(2,1)} %w_hbm.5, f32[72,128]{1,0:T(8,128)S(1)} %shard_map.105.after), custom_call_target="tpu_custom_call" | custom-call | flops 500000000 | bytes 4194304 | tf_op jit(solution)/shard_map/pallas_call | solution.py:352
  13.0 0.0 collective-permute-done.2
  13.0 0.6 %collective-permute-done.3 = f16[72,128]{1,0:T(8,128)(2,1)S(1)} collective-permute-done((f16[72,128]{1,0:T(8,128)(2,1)S(1)}, f16[72,128]{1,0:T(8,128)(2,1)S(1)}, u32[]{:S(2)}, u32[]{:S(2)}) %collective-permute-start.3) | collective-permute-done | bytes 18464 | tf_op jit(solution)/shard_map/ppermute | solution.py:370
  13.7 0.5 %collective-permute-done.4 = f16[72,128]{1,0:T(8,128)(2,1)S(1)} collective-permute-done((f16[72,128]{1,0:T(8,128)(2,1)S(1)}, f16[72,128]{1,0:T(8,128)(2,1)S(1)}, u32[]{:S(2)}, u32[]{:S(2)}) %collective-permute-start.4) | collective-permute-done | bytes 18464 | tf_op jit(solution)/shard_map/ppermute | solution.py:370
  14.2 0.0 collective-permute-done.5
  14.2 0.8 %shard_map.108 = (f32[8,128]{1,0:T(8,128)S(1)}, f32[2,1024]{1,0:T(2,128)S(1)}, f32[2,1024]{1,0:T(2,128)S(1)}) custom-call(f32[72,128]{1,0:T(8,128)S(1)} %shard_map.107.refs_0_, f32[72,128]{1,0:T(8,128)S(1)} %convert_element_type.30.refs_1_, f32[72,128]{1,0:T(8,128)S(1)} %convert_element_type.31.refs_2_, bf16[512,1024]{1,0:T(8,128)(2,1)S(1)} %get-tuple-element.23.refs_3_, ...), custom_call_target="tpu_custom_call" | custom-call | tf_op jit(solution)/shard_map/pallas_call | solution.py:352
  15.0 0.3 %collective-permute-start.6 = (f32[2,1024]{1,0:T(2,128)S(1)}, f32[2,1024]{1,0:T(2,128)S(1)}, u32[]{:S(2)}, u32[]{:S(2)}) collective-permute-start(f32[2,1024]{1,0:T(2,128)S(1)} %get-tuple-element.26), channel_id=1, source_target_pairs={{0,1},{1,0},{2,3},{3,2},{4,5},{5,4},{6,7},{7,6},{8,9},{9,8},{10,11... | collective-permute-start | bytes 24584 | tf_op jit(solution)/shard_map/ppermute | solution.py:370
  15.3 1.0 %collective-permute-done.6 = f32[2,1024]{1,0:T(2,128)S(1)} collective-permute-done((f32[2,1024]{1,0:T(2,128)S(1)}, f32[2,1024]{1,0:T(2,128)S(1)}, u32[]{:S(2)}, u32[]{:S(2)}) %collective-permute-start.6) | collective-permute-done | bytes 8224 | tf_op jit(solution)/shard_map/ppermute | solution.py:370
  16.3 1.4 %collective-permute-start.7 = (f32[1,1024]{1,0:T(1,128)S(1)}, f32[1,1024]{1,0:T(1,128)S(1)}, u32[]{:S(2)}, u32[]{:S(2)}) collective-permute-start(f32[1,1024]{1,0:T(1,128)S(1)} %get-tuple-element.31), channel_id=1, source_target_pairs={{0,3},{1,2},{2,1},{3,0},{4,7},{5,6},{6,5},{7,4},{8,11},{9,10},{10,... | collective-permute-start | bytes 12296 | tf_op jit(solution)/shard_map/ppermute | solution.py:370
  17.6 1.4 %shard_map.109.high_ref = f32[2,2,8]{2,1,0:T(2,128)S(1)} custom-call(bf16[4,16,128]{2,1,0:T(8,128)(2,1)S(1)} %get-tuple-element.18.q_ref, s32[4,8]{1,0:T(4,128)S(1)} %get-tuple-element.19.len_ref, s32[4,2,32,128]{3,2,1,0:T(8,128)S(1)} %get-tuple-element.20.code_ref, f32[2,4,32,256]{3,2,1,0:T(8,128)S(1)} %get-tuple-element.21.cent_ref, f32[2,1024]{1,0:T(2,128)S(1)} %add.3.after), custom_call_target="tpu_custom_call" | custom-call | flops 500000000 | bytes 4194304 | tf_op jit(solution)/shard_map/pallas_call | solution.py:352
  19.0 0.4 %collective-permute-done.7.b_ref = f32[1,1024]{1,0:T(1,128)S(1)} collective-permute-done((f32[1,1024]{1,0:T(1,128)S(1)}, f32[1,1024]{1,0:T(1,128)S(1)}, u32[]{:S(2)}, u32[]{:S(2)}) %collective-permute-start.7) | collective-permute-done | bytes 4128 | tf_op jit(solution)/shard_map/ppermute | solution.py:370
  19.4 0.6 %shard_map.110 = (bf16[1,1024]{1,0:T(2,128)(2,1)}, bf16[1,1,1024]{2,1,0:T(2,128)(2,1)}, f32[4,2,8]{2,1,0:T(2,128)}) custom-call(f32[1,1024]{1,0:T(1,128)S(1)} %get-tuple-element.32.a_ref, f32[1,1024]{1,0:T(1,128)S(1)} %collective-permute-done.7.b_ref, f32[8,128]{1,0:T(8,128)S(1)} %get-tuple-element.27.att_ref, ...), custom_call_target="tpu_custom_call" | custom-call | tf_op jit(solution)/shard_map/pallas_call | solution.py:352
  (12 shorter events, 0.1 us)
Async XLA Ops:
  2.4 5.6 %collective-permute-start = (f16[72,128]{1,0:T(8,128)(2,1)S(1)}, f16[72,128]{1,0:T(8,128)(2,1)S(1)}, u32[]{:S(2)}, u32[]{:S(2)}) collective-permute-start(f16[72,128]{1,0:T(8,128)(2,1)S(1)} %convert_element_type.24), channel_id=1, source_target_pairs={{0,17},{1,16},{2,19},{3,18},{4,21},{5,20},{6,23},{7,22},{8,25},{9,... | collective-permute-start | bytes 55304 | tf_op jit(solution)/shard_map/ppermute | solution.py:370
  6.0 2.1 %collective-permute-start.1 = (f16[72,128]{1,0:T(8,128)(2,1)S(1)}, f16[72,128]{1,0:T(8,128)(2,1)S(1)}, u32[]{:S(2)}, u32[]{:S(2)}) collective-permute-start(f16[72,128]{1,0:T(8,128)(2,1)S(1)} %convert_element_type.24), channel_id=1, source_target_pairs={{0,1},{1,0},{2,3},{3,2},{4,5},{5,4},{6,7},{7,6},{8,9},{9,8},{10,11... | collective-permute-start | bytes 55304 | tf_op jit(solution)/shard_map/ppermute | solution.py:370
  8.2 4.8 %collective-permute-start.2 = (f16[72,128]{1,0:T(8,128)(2,1)S(1)}, f16[72,128]{1,0:T(8,128)(2,1)S(1)}, u32[]{:S(2)}, u32[]{:S(2)}) collective-permute-start(f16[72,128]{1,0:T(8,128)(2,1)S(1)} %convert_element_type.27), channel_id=1, source_target_pairs={{0,13},{1,12},{2,15},{3,14},{4,9},{5,8},{6,11},{7,10},{8,5},{9,4},... | collective-permute-start | bytes 55304 | tf_op jit(solution)/shard_map/ppermute | solution.py:370
  10.4 3.2 %collective-permute-start.3 = (f16[72,128]{1,0:T(8,128)(2,1)S(1)}, f16[72,128]{1,0:T(8,128)(2,1)S(1)}, u32[]{:S(2)}, u32[]{:S(2)}) collective-permute-start(f16[72,128]{1,0:T(8,128)(2,1)S(1)} %convert_element_type.27), channel_id=1, source_target_pairs={{0,9},{1,8},{2,11},{3,10},{4,13},{5,12},{6,15},{7,14},{8,1},{9,0},... | collective-permute-start | bytes 55304 | tf_op jit(solution)/shard_map/ppermute | solution.py:370
  11.0 3.2 %collective-permute-start.4 = (f16[72,128]{1,0:T(8,128)(2,1)S(1)}, f16[72,128]{1,0:T(8,128)(2,1)S(1)}, u32[]{:S(2)}, u32[]{:S(2)}) collective-permute-start(f16[72,128]{1,0:T(8,128)(2,1)S(1)} %convert_element_type.27), channel_id=1, source_target_pairs={{0,5},{1,4},{2,7},{3,6},{4,1},{5,0},{6,3},{7,2},{8,13},{9,12},{10,... | collective-permute-start | bytes 55304 | tf_op jit(solution)/shard_map/ppermute | solution.py:370
  11.2 3.0 %collective-permute-start.5 = (f16[72,128]{1,0:T(8,128)(2,1)S(1)}, f16[72,128]{1,0:T(8,128)(2,1)S(1)}, u32[]{:S(2)}, u32[]{:S(2)}) collective-permute-start(f16[72,128]{1,0:T(8,128)(2,1)S(1)} %convert_element_type.27), channel_id=1, source_target_pairs={{0,1},{1,0},{2,3},{3,2},{4,5},{5,4},{6,7},{7,6},{8,9},{9,8},{10,11... | collective-permute-start | bytes 55304 | tf_op jit(solution)/shard_map/ppermute | solution.py:370
  15.0 1.2 %collective-permute-start.6 = (f32[2,1024]{1,0:T(2,128)S(1)}, f32[2,1024]{1,0:T(2,128)S(1)}, u32[]{:S(2)}, u32[]{:S(2)}) collective-permute-start(f32[2,1024]{1,0:T(2,128)S(1)} %get-tuple-element.26), channel_id=1, source_target_pairs={{0,1},{1,0},{2,3},{3,2},{4,5},{5,4},{6,7},{7,6},{8,9},{9,8},{10,11... | collective-permute-start | bytes 24584 | tf_op jit(solution)/shard_map/ppermute | solution.py:370
  16.3 3.1 %collective-permute-start.7 = (f32[1,1024]{1,0:T(1,128)S(1)}, f32[1,1024]{1,0:T(1,128)S(1)}, u32[]{:S(2)}, u32[]{:S(2)}) collective-permute-start(f32[1,1024]{1,0:T(1,128)S(1)} %get-tuple-element.31), channel_id=1, source_target_pairs={{0,3},{1,2},{2,1},{3,0},{4,7},{5,6},{6,5},{7,4},{8,11},{9,10},{10,... | collective-permute-start | bytes 12296 | tf_op jit(solution)/shard_map/ppermute | solution.py:370

commit v8 on v7

--- a/solution.py
+++ b/solution.py
@@ -384,7 +384,7 @@
     size = feat // pack + STATS
     f32, f16 = jnp.float32, jnp.float16
 
-    cuts = [heads * feat * i // 16 for i in (0, 4, 10, 16)]
+    cuts = [heads * feat * i // 16 for i in (0, 5, 10, 16)]
     slabs = [
         (jax.ShapeDtypeStruct((b - a, width), out_weight.dtype), VMEM)
         for a, b in zip(cuts, cuts[1:])

time: 20.2 us -> 20.1 us (level)
  no operation moved by 1% of the time
where the time goes in v8:
time: 20.1 us; the launch traced here: 19.9 us
  starting transfers between devices  9.23 us (46%)
  Pallas kernels  7.49 us (37%)
  waiting for transfers between devices  2.42 us (12%)
  between operations  0.76 us (4%)
    ppermute x8, starting transfers between devices, move(): return lax.ppermute(x, ('seq', 'head'), pairs)  9.23 us
    pallas_call x8, Pallas kernels, call(): pl.pallas_call(kernel, out_shape=[shape for shape, _ in out], in_specs=[s...  7.49 us
    ppermute x8, waiting for transfers between devices, move(): return lax.ppermute(x, ('seq', 'head'), pairs)  2.42 us
  transfers between devices with their start and end apart: 8, of which 4 were waited for; matrix products, arithmetic and copies ran while one was open for 0% of the time, Pallas kernels for 21%

profile of v8, /device:TPU:0, one launch (start us, length us, event | category | flops | bytes accessed | tf_op | source)
XLA Modules:
  0.0 19.9 jit_solution(11966619624043134161)
XLA Ops:
  0.6 1.8 %shard_map.103 = (f32[72,128]{1,0:T(8,128)S(1)}, bf16[4,16,128]{2,1,0:T(8,128)(2,1)S(1)}, s32[4,8]{1,0:T(4,128)S(1)}, s32[4,2,32,128]{3,2,1,0:T(8,128)S(1)}, f32...) custom-call(bf16[4,16,128]{2,1,0:T(8,128)(2,1)} %q_hbm.1, bf16[4,2,128,128]{3,2,1,0:T(8,128)(2,1)} %k_hbm.1, ...), custom_call_target="tpu_custom_call" | custom-call | tf_op jit(solution)/shard_map/pallas_call | solution.py:352
  2.4 3.5 %collective-permute-start = (f16[72,128]{1,0:T(8,128)(2,1)S(1)}, f16[72,128]{1,0:T(8,128)(2,1)S(1)}, u32[]{:S(2)}, u32[]{:S(2)}) collective-permute-start(f16[72,128]{1,0:T(8,128)(2,1)S(1)} %convert_element_type.24), channel_id=1, source_target_pairs={{0,17},{1,16},{2,19},{3,18},{4,21},{5,20},{6,23},{7,22},{8,25},{9,... | collective-permute-start | bytes 55304 | tf_op jit(solution)/shard_map/ppermute | solution.py:370
  6.0 0.7 %collective-permute-start.1 = (f16[72,128]{1,0:T(8,128)(2,1)S(1)}, f16[72,128]{1,0:T(8,128)(2,1)S(1)}, u32[]{:S(2)}, u32[]{:S(2)}) collective-permute-start(f16[72,128]{1,0:T(8,128)(2,1)S(1)} %convert_element_type.24), channel_id=1, source_target_pairs={{0,1},{1,0},{2,3},{3,2},{4,5},{5,4},{6,7},{7,6},{8,9},{9,8},{10,11... | collective-permute-start | bytes 55304 | tf_op jit(solution)/shard_map/ppermute | solution.py:370
  6.7 1.4 %shard_map.104 = (f32[2,2,8]{2,1,0:T(2,128)S(1)}, bf16[640,1024]{1,0:T(8,128)(2,1)S(1)}) custom-call(bf16[4,16,128]{2,1,0:T(8,128)(2,1)S(1)} %get-tuple-element.18.q_ref, s32[4,8]{1,0:T(4,128)S(1)} %get-tuple-element.19.len_ref, s32[4,2,32,128]{3,2,1,0:T(8,128)S(1)} %get-tuple-element.20.code_ref, f32[2,4,32,256]{3,2,1,0:T(8,128)S(1)} %get-tuple-element.21.cent_ref, ...), custom_call_target="tpu_custom_call" | custom-call | flops 500000000 | bytes 4194304 | tf_op jit(solution)/shard_map/pallas_call | solution.py:352
  8.1 0.0 collective-permute-done
  8.1 0.0 collective-permute-done.1
  8.2 2.3 %collective-permute-start.2 = (f16[72,128]{1,0:T(8,128)(2,1)S(1)}, f16[72,128]{1,0:T(8,128)(2,1)S(1)}, u32[]{:S(2)}, u32[]{:S(2)}) collective-permute-start(f16[72,128]{1,0:T(8,128)(2,1)S(1)} %convert_element_type.27), channel_id=1, source_target_pairs={{0,13},{1,12},{2,15},{3,14},{4,9},{5,8},{6,11},{7,10},{8,5},{9,4},... | collective-permute-start | bytes 55304 | tf_op jit(solution)/shard_map/ppermute | solution.py:370
  10.4 0.5 %collective-permute-start.3 = (f16[72,128]{1,0:T(8,128)(2,1)S(1)}, f16[72,128]{1,0:T(8,128)(2,1)S(1)}, u32[]{:S(2)}, u32[]{:S(2)}) collective-permute-start(f16[72,128]{1,0:T(8,128)(2,1)S(1)} %convert_element_type.27), channel_id=1, source_target_pairs={{0,9},{1,8},{2,11},{3,10},{4,13},{5,12},{6,15},{7,14},{8,1},{9,0},... | collective-permute-start | bytes 55304 | tf_op jit(solution)/shard_map/ppermute | solution.py:370
  10.9 0.2 collective-permute-start.4
  11.1 0.4 %collective-permute-start.5 = (f16[72,128]{1,0:T(8,128)(2,1)S(1)}, f16[72,128]{1,0:T(8,128)(2,1)S(1)}, u32[]{:S(2)}, u32[]{:S(2)}) collective-permute-start(f16[72,128]{1,0:T(8,128)(2,1)S(1)} %convert_element_type.27), channel_id=1, source_target_pairs={{0,1},{1,0},{2,3},{3,2},{4,5},{5,4},{6,7},{7,6},{8,9},{9,8},{10,11... | collective-permute-start | bytes 55304 | tf_op jit(solution)/shard_map/ppermute | solution.py:370
  11.6 1.4 %shard_map.106.refs_2_.refs_5_ = bf16[768,1024]{1,0:T(8,128)(2,1)S(1)} custom-call(bf16[2048,1024]{1,0:T(8,128)(2,1)} %w_hbm.5, f32[72,128]{1,0:T(8,128)S(1)} %shard_map.105.after), custom_call_target="tpu_custom_call" | custom-call | flops 500000000 | bytes 4194304 | tf_op jit(solution)/shard_map/pallas_call | solution.py:352
  13.0 0.0 collective-permute-done.2
  13.0 0.6 %collective-permute-done.3 = f16[72,128]{1,0:T(8,128)(2,1)S(1)} collective-permute-done((f16[72,128]{1,0:T(8,128)(2,1)S(1)}, f16[72,128]{1,0:T(8,128)(2,1)S(1)}, u32[]{:S(2)}, u32[]{:S(2)}) %collective-permute-start.3) | collective-permute-done | bytes 18464 | tf_op jit(solution)/shard_map/ppermute | solution.py:370
  13.7 0.5 %collective-permute-done.4 = f16[72,128]{1,0:T(8,128)(2,1)S(1)} collective-permute-done((f16[72,128]{1,0:T(8,128)(2,1)S(1)}, f16[72,128]{1,0:T(8,128)(2,1)S(1)}, u32[]{:S(2)}, u32[]{:S(2)}) %collective-permute-start.4) | collective-permute-done | bytes 18464 | tf_op jit(solution)/shard_map/ppermute | solution.py:370
  14.1 0.0 collective-permute-done.5
  14.2 0.8 %shard_map.108 = (f32[8,128]{1,0:T(8,128)S(1)}, f32[2,1024]{1,0:T(2,128)S(1)}, f32[2,1024]{1,0:T(2,128)S(1)}) custom-call(f32[72,128]{1,0:T(8,128)S(1)} %shard_map.107.refs_0_, f32[72,128]{1,0:T(8,128)S(1)} %convert_element_type.30.refs_1_, f32[72,128]{1,0:T(8,128)S(1)} %convert_element_type.31.refs_2_, bf16[640,1024]{1,0:T(8,128)(2,1)S(1)} %get-tuple-element.23.refs_3_, ...), custom_call_target="tpu_custom_call" | custom-call | tf_op jit(solution)/shard_map/pallas_call | solution.py:352
  15.0 0.3 %collective-permute-start.6 = (f32[2,1024]{1,0:T(2,128)S(1)}, f32[2,1024]{1,0:T(2,128)S(1)}, u32[]{:S(2)}, u32[]{:S(2)}) collective-permute-start(f32[2,1024]{1,0:T(2,128)S(1)} %get-tuple-element.26), channel_id=1, source_target_pairs={{0,1},{1,0},{2,3},{3,2},{4,5},{5,4},{6,7},{7,6},{8,9},{9,8},{10,11... | collective-permute-start | bytes 24584 | tf_op jit(solution)/shard_map/ppermute | solution.py:370
  15.2 1.0 %collective-permute-done.6 = f32[2,1024]{1,0:T(2,128)S(1)} collective-permute-done((f32[2,1024]{1,0:T(2,128)S(1)}, f32[2,1024]{1,0:T(2,128)S(1)}, u32[]{:S(2)}, u32[]{:S(2)}) %collective-permute-start.6) | collective-permute-done | bytes 8224 | tf_op jit(solution)/shard_map/ppermute | solution.py:370
  16.2 1.4 %collective-permute-start.7 = (f32[1,1024]{1,0:T(1,128)S(1)}, f32[1,1024]{1,0:T(1,128)S(1)}, u32[]{:S(2)}, u32[]{:S(2)}) collective-permute-start(f32[1,1024]{1,0:T(1,128)S(1)} %get-tuple-element.31), channel_id=1, source_target_pairs={{0,3},{1,2},{2,1},{3,0},{4,7},{5,6},{6,5},{7,4},{8,11},{9,10},{10,... | collective-permute-start | bytes 12296 | tf_op jit(solution)/shard_map/ppermute | solution.py:370
  17.6 1.4 %shard_map.109.high_ref = f32[2,2,8]{2,1,0:T(2,128)S(1)} custom-call(bf16[4,16,128]{2,1,0:T(8,128)(2,1)S(1)} %get-tuple-element.18.q_ref, s32[4,8]{1,0:T(4,128)S(1)} %get-tuple-element.19.len_ref, s32[4,2,32,128]{3,2,1,0:T(8,128)S(1)} %get-tuple-element.20.code_ref, f32[2,4,32,256]{3,2,1,0:T(8,128)S(1)} %get-tuple-element.21.cent_ref, f32[2,1024]{1,0:T(2,128)S(1)} %add.3.after), custom_call_target="tpu_custom_call" | custom-call | flops 500000000 | bytes 4194304 | tf_op jit(solution)/shard_map/pallas_call | solution.py:352
  19.0 0.4 %collective-permute-done.7.b_ref = f32[1,1024]{1,0:T(1,128)S(1)} collective-permute-done((f32[1,1024]{1,0:T(1,128)S(1)}, f32[1,1024]{1,0:T(1,128)S(1)}, u32[]{:S(2)}, u32[]{:S(2)}) %collective-permute-start.7) | collective-permute-done | bytes 4128 | tf_op jit(solution)/shard_map/ppermute | solution.py:370
  19.3 0.6 %shard_map.110 = (bf16[1,1024]{1,0:T(2,128)(2,1)}, bf16[1,1,1024]{2,1,0:T(2,128)(2,1)}, f32[4,2,8]{2,1,0:T(2,128)}) custom-call(f32[1,1024]{1,0:T(1,128)S(1)} %get-tuple-element.32.a_ref, f32[1,1024]{1,0:T(1,128)S(1)} %collective-permute-done.7.b_ref, f32[8,128]{1,0:T(8,128)S(1)} %get-tuple-element.27.att_ref, ...), custom_call_target="tpu_custom_call" | custom-call | tf_op jit(solution)/shard_map/pallas_call | solution.py:352
  (12 shorter events, 0.1 us)
Async XLA Ops:
  2.4 5.6 %collective-permute-start = (f16[72,128]{1,0:T(8,128)(2,1)S(1)}, f16[72,128]{1,0:T(8,128)(2,1)S(1)}, u32[]{:S(2)}, u32[]{:S(2)}) collective-permute-start(f16[72,128]{1,0:T(8,128)(2,1)S(1)} %convert_element_type.24), channel_id=1, source_target_pairs={{0,17},{1,16},{2,19},{3,18},{4,21},{5,20},{6,23},{7,22},{8,25},{9,... | collective-permute-start | bytes 55304 | tf_op jit(solution)/shard_map/ppermute | solution.py:370
  6.0 2.1 %collective-permute-start.1 = (f16[72,128]{1,0:T(8,128)(2,1)S(1)}, f16[72,128]{1,0:T(8,128)(2,1)S(1)}, u32[]{:S(2)}, u32[]{:S(2)}) collective-permute-start(f16[72,128]{1,0:T(8,128)(2,1)S(1)} %convert_element_type.24), channel_id=1, source_target_pairs={{0,1},{1,0},{2,3},{3,2},{4,5},{5,4},{6,7},{7,6},{8,9},{9,8},{10,11... | collective-permute-start | bytes 55304 | tf_op jit(solution)/shard_map/ppermute | solution.py:370
  8.2 4.8 %collective-permute-start.2 = (f16[72,128]{1,0:T(8,128)(2,1)S(1)}, f16[72,128]{1,0:T(8,128)(2,1)S(1)}, u32[]{:S(2)}, u32[]{:S(2)}) collective-permute-start(f16[72,128]{1,0:T(8,128)(2,1)S(1)} %convert_element_type.27), channel_id=1, source_target_pairs={{0,13},{1,12},{2,15},{3,14},{4,9},{5,8},{6,11},{7,10},{8,5},{9,4},... | collective-permute-start | bytes 55304 | tf_op jit(solution)/shard_map/ppermute | solution.py:370
  10.4 3.2 %collective-permute-start.3 = (f16[72,128]{1,0:T(8,128)(2,1)S(1)}, f16[72,128]{1,0:T(8,128)(2,1)S(1)}, u32[]{:S(2)}, u32[]{:S(2)}) collective-permute-start(f16[72,128]{1,0:T(8,128)(2,1)S(1)} %convert_element_type.27), channel_id=1, source_target_pairs={{0,9},{1,8},{2,11},{3,10},{4,13},{5,12},{6,15},{7,14},{8,1},{9,0},... | collective-permute-start | bytes 55304 | tf_op jit(solution)/shard_map/ppermute | solution.py:370
  10.9 3.2 %collective-permute-start.4 = (f16[72,128]{1,0:T(8,128)(2,1)S(1)}, f16[72,128]{1,0:T(8,128)(2,1)S(1)}, u32[]{:S(2)}, u32[]{:S(2)}) collective-permute-start(f16[72,128]{1,0:T(8,128)(2,1)S(1)} %convert_element_type.27), channel_id=1, source_target_pairs={{0,5},{1,4},{2,7},{3,6},{4,1},{5,0},{6,3},{7,2},{8,13},{9,12},{10,... | collective-permute-start | bytes 55304 | tf_op jit(solution)/shard_map/ppermute | solution.py:370
  11.1 3.0 %collective-permute-start.5 = (f16[72,128]{1,0:T(8,128)(2,1)S(1)}, f16[72,128]{1,0:T(8,128)(2,1)S(1)}, u32[]{:S(2)}, u32[]{:S(2)}) collective-permute-start(f16[72,128]{1,0:T(8,128)(2,1)S(1)} %convert_element_type.27), channel_id=1, source_target_pairs={{0,1},{1,0},{2,3},{3,2},{4,5},{5,4},{6,7},{7,6},{8,9},{9,8},{10,11... | collective-permute-start | bytes 55304 | tf_op jit(solution)/shard_map/ppermute | solution.py:370
  15.0 1.2 %collective-permute-start.6 = (f32[2,1024]{1,0:T(2,128)S(1)}, f32[2,1024]{1,0:T(2,128)S(1)}, u32[]{:S(2)}, u32[]{:S(2)}) collective-permute-start(f32[2,1024]{1,0:T(2,128)S(1)} %get-tuple-element.26), channel_id=1, source_target_pairs={{0,1},{1,0},{2,3},{3,2},{4,5},{5,4},{6,7},{7,6},{8,9},{9,8},{10,11... | collective-permute-start | bytes 24584 | tf_op jit(solution)/shard_map/ppermute | solution.py:370
  16.2 3.1 %collective-permute-start.7 = (f32[1,1024]{1,0:T(1,128)S(1)}, f32[1,1024]{1,0:T(1,128)S(1)}, u32[]{:S(2)}, u32[]{:S(2)}) collective-permute-start(f32[1,1024]{1,0:T(1,128)S(1)} %get-tuple-element.31), channel_id=1, source_target_pairs={{0,3},{1,2},{2,1},{3,0},{4,7},{5,6},{6,5},{7,4},{8,11},{9,10},{10,... | collective-permute-start | bytes 12296 | tf_op jit(solution)/shard_map/ppermute | solution.py:370
